TPU v7x, 32 devices: a whole 2x2x4 slice. The times are simulated.
32 devices in a mesh: groups: 2 (over y), row: 4 (over x, core), col: 4 (over z).
Axes of the slice: x: 2, y: 2, z: 4, core: 2. Of those that a mesh axis runs over, the one named last changes fastest.
Arguments:
- tiles: float32 [512, 128, 128], P(('groups', 'row', 'col')), parts along dimension 0, may hold values from 0 to 9
- tile_index: int32 [512, 2], P(('groups', 'row', 'col')), parts along dimension 0, may hold values from 0 to 3, as said below
- tile_count: int32 [32], P(('groups', 'row', 'col')), parts along dimension 0, may hold values from 4 to 16, as said below
- sources: int32 [16], P('groups'), parts along dimension 0, may hold values from 0 to 2047
Outputs:
- distance: float32 [16, 2048], P('groups', ('row', 'col')), parts along dimension 0
- path_counts: float32 [16, 2048], P('groups', ('row', 'col')), parts along dimension 0
- centrality: float32 [4096], P(('groups', 'row', 'col')), parts along dimension 0
There are 2 independent parts, one for each index of `groups`. A program takes and returns all parts, laid end to end along the dimension named above; each array names one. Nothing has to cross between parts.
Inputs may be any that keep to these rules, and one draw needn't show every extreme that they name: `tile_index`: entry (r, c) of a slot has r below 4 and c below 4; the 16 slots of one device name distinct pairs. `tile_count`: one entry per device; slots of a device from its count on hold only zeros; some device has all 16 slots live.
All inputs are finite; a program needn't handle non-finite values.
Results may differ from a plain program's by a relative error of at most 0.0003.
Values sent between devices are 32-bit elements; how exact they have to be, the bound alone decides.
No kernel may reach another device: no remote copies, remote signals or barrier semaphores. Data moves between devices by JAX's collectives and lax.ppermute only.
A program may use at most 64 MiB of HBM per device.

v0:
```python
import functools

import jax
import jax.numpy as jnp
from jax import lax
from jax.experimental import pallas as pl
from jax.experimental.pallas import tpu as pltpu
from jax.sharding import PartitionSpec as P

LEVELS = 3
BACK = 2
LANES = 128
SUB = 8
PAIR = 2

far_value = 1000000.0
no_edge = 2000000.0
large_limit = 8 * 1024 * 1024
small_limit = 2 * 1024 * 1024


def in_vmem():
    return pl.BlockSpec(memory_space=pltpu.VMEM)


def in_smem():
    return pl.BlockSpec(memory_space=pltpu.SMEM)


def piece(*shape):
    return jax.ShapeDtypeStruct(shape, jnp.float32)


def params(limit):
    return pltpu.CompilerParams(vmem_limit_bytes=limit)


def is_dense(dims):
    return dims[2] == dims[0] * dims[1]


def position():
    return lax.axis_index("chip"), lax.axis_index("core"), lax.axis_index("col")


def source_ids(sources, first, half):
    row = lax.broadcasted_iota(jnp.int32, (half, LANES), 0)
    ids = jnp.zeros((half, LANES), jnp.int32)
    for s in range(half):
        ids = jnp.where(row == s, sources[first + s], ids)
    return ids


def is_source(ids, block):
    return ids == block * LANES + lax.broadcasted_iota(jnp.int32, ids.shape, 1)


def settle(found_dist, found_count, at_source):
    dist = jnp.where(at_source, 0.0, jnp.minimum(found_dist, far_value))
    count = jnp.where(found_dist == dist, found_count, 0.0)
    return dist, jnp.where(at_source, 1.0, 0.0) + count


def merge(pairs):
    best = functools.reduce(jnp.minimum, [p[0] for p in pairs])
    total = functools.reduce(jnp.add, [jnp.where(p[0] == best, p[1], 0.0) for p in pairs])
    return best, total


def first_kernel(dims, places, sources, tiles, out, turned, slot_of, lines):
    n_row, n_col, slots, half = dims
    my_x, my_core, my_col = position()
    my_row = my_x * PAIR + my_core

    def clear(at, _):
        slot_of[at] = -1
        return 0

    if not is_dense(dims):
        lax.fori_loop(0, n_row * n_col, clear, 0)
    for g in range(slots):
        slot_of[places[0, g] * n_row + places[1, g]] = g
    lines[...] = jnp.zeros(lines.shape, jnp.float32)
    for s in range(PAIR * half):
        vertex = sources[s]
        block, place = vertex // LANES, lax.rem(vertex, LANES)
        r = lax.rem(block, n_col)

        @pl.when(block // n_col == my_row)
        def _():
            for c in range(n_row):
                g = slot_of[r * n_row + c]

                @pl.when(g >= 0)
                def _():
                    line = c % PAIR * half + s % half
                    row = tiles[g, pl.ds(place, 1), :]
                    lines[c // PAIR, s // half, pl.ds(line, 1), :] = row

    for chip in range(n_row // PAIR):
        for core in range(PAIR):
            line = lines[chip, core]
            line = jnp.where(line > 0, line, far_value)
            for col in range(n_col):
                out[(chip * PAIR + core) * n_col + col] = line
    for at in range(slots):
        raw = tiles[slot_of[at] if is_dense(dims) else at]
        turned[at] = jnp.where(raw > 0, raw, no_edge).T


def first_level(dims, places, sources, tiles):
    n_row, n_col, slots, half = dims
    return pl.pallas_call(
        functools.partial(first_kernel, dims),
        out_shape=[piece(n_row * n_col, PAIR * half, LANES), piece(*tiles.shape)],
        in_specs=[in_smem(), in_smem(), in_vmem()],
        out_specs=[in_vmem()] * 2,
        scratch_shapes=[
            pltpu.SMEM((n_row * n_col,), jnp.int32),
            pltpu.VMEM((n_row // PAIR, PAIR, PAIR * half, LANES), jnp.float32),
        ],
        compiler_params=params(large_limit),
        name="first_level",
    )(places, sources, tiles)


def list_slots(dims, places, table, filled):
    n_row, n_col, slots, half = dims
    if is_dense(dims):
        return

    def clear(at, _):
        filled[at] = 0
        return 0

    lax.fori_loop(0, PAIR * n_row, clear, 0)
    for k in range(PAIR):

        def enter(g, _):
            at = k * n_row + places[k][1, g]
            table[at * n_col + filled[at]] = g
            filled[at] += 1
            return 0

        lax.fori_loop(0, slots, enter, 0)


def over_slots(dims, places, table, filled, c, step, carry):
    n_row, n_col, slots, half = dims
    for k in range(PAIR):
        if is_dense(dims):
            for r in range(n_col):
                carry = step(k, r * n_row + c, k * n_col + r, carry)
        else:
            at = k * n_row + c

            def entry(e, carry):
                g = table[at * n_col + e]
                return step(k, g, k * n_col + places[k][0, g], carry)

            carry = lax.fori_loop(0, filled[at], entry, carry)
    return carry


def slot_scratch(dims):
    n_row, n_col, slots, half = dims
    return [
        pltpu.SMEM((PAIR * n_row * n_col,), jnp.int32),
        pltpu.SMEM((PAIR * n_row,), jnp.int32),
    ]


def relax_kernel(dims, counted, whole, *refs):
    n_row, n_col, slots, half = dims
    chips = n_row // PAIR
    n_places = 0 if is_dense(dims) else PAIR
    places, refs = refs[:n_places], refs[n_places:]
    sources, tiles, refs = refs[0], refs[1 : 1 + PAIR], refs[1 + PAIR :]
    came, out, near, found, table, filled = refs
    my_x, my_core, my_col = position()
    ids = source_ids(sources, my_core * half, half)
    list_slots(dims, places, table, filled)
    for r in range(n_col):
        for k in range(PAIR):
            h = my_core ^ k
            at_source = is_source(ids, (PAIR * my_x + h) * n_col + r)
            if counted:
                blocks = [came[chip * n_col + r, h] for chip in range(chips)]
                reached, count = merge([(block[:half], block[half:]) for block in blocks])
            else:
                parts = [came[at * n_col + r, pl.ds(h * half, half), :] for at in range(n_row)]
                reached = functools.reduce(jnp.minimum, parts)
                count = jnp.where(reached < far_value, 1.0, 0.0)
            dist, count = settle(reached, count, at_source)
            near[k * n_col + r, :half, :] = dist
            near[k * n_col + r, half:, :] = count
    lane = lax.broadcasted_iota(jnp.int32, (LANES, LANES), 1)

    def column(c, _):
        def lowest(s):
            def step(k, g, b, carry):
                return jnp.minimum(carry, tiles[k][g] + near[b, pl.ds(s, 1), :])

            start = jnp.full((LANES, LANES), far_value, jnp.float32)
            reached = over_slots(dims, places, table, filled, c, step, start)
            return jnp.min(reached, axis=1, keepdims=True)

        def tally(s, best):
            def step(k, g, b, carry):
                hit = tiles[k][g] + near[b, pl.ds(s, 1), :] == best
                return carry + jnp.where(hit, near[b, pl.ds(half + s, 1), :], 0.0)

            start = jnp.zeros((LANES, LANES), jnp.float32)
            counts = over_slots(dims, places, table, filled, c, step, start)
            return jnp.sum(counts, axis=1, keepdims=True)

        turned = jnp.zeros((LANES, LANES), jnp.float32)
        best = lowest(0)
        for s in range(half):
            later = lowest(s + 1) if s + 1 < half else None
            total = tally(s, best)
            turned = jnp.where(lane == s, best, jnp.where(lane == half + s, total, turned))
            best = later
        found[c] = turned.T[: 2 * half]
        return 0

    lax.fori_loop(0, n_row, column, 0)
    for chip in range(chips):
        for col in range(n_col):
            if whole:
                out[chip * n_col + col] = found[...]
            else:
                out[chip * n_col + col] = found[pl.ds(PAIR * chip, PAIR)]


def relax_level(dims, counted, whole, places, sources, tiles, came):
    n_row, n_col, slots, half = dims
    blocks = n_row if whole else PAIR
    return pl.pallas_call(
        functools.partial(relax_kernel, dims, counted, whole),
        out_shape=piece(n_row // PAIR * n_col, blocks, 2 * half, LANES),
        in_specs=[in_smem()] * (len(places) + 1) + [in_vmem()] * (PAIR + 1),
        out_specs=in_vmem(),
        scratch_shapes=[
            pltpu.VMEM((PAIR * n_col, 2 * half, LANES), jnp.float32),
            pltpu.VMEM((n_row, 2 * half, LANES), jnp.float32),
        ]
        + slot_scratch(dims),
        compiler_params=params(large_limit),
        name="relax_level",
    )(*places, sources, *tiles, came)


def depend_kernel(dims, first, last, *refs):
    n_row, n_col, slots, half = dims
    chips = n_row // PAIR
    n_places = 0 if is_dense(dims) else PAIR
    places, refs = refs[:n_places], refs[n_places:]
    sources, tiles, refs = refs[0], refs[1 : 1 + PAIR], refs[1 + PAIR :]
    if first:
        came, out, near, low, lower, acc, table, filled = refs
    else:
        near, low, came, out, shown, paths, lower, acc, table, filled = refs
    my_x, my_core, my_col = position()
    ids = source_ids(sources, my_core * half, half)
    list_slots(dims, places, table, filled)
    if first:
        for r in range(n_col):
            for k in range(PAIR):
                h = my_core ^ k
                at_source = is_source(ids, (PAIR * my_x + h) * n_col + r)
                blocks = [came[chip * n_col + r, PAIR * my_x + h] for chip in range(chips)]
                found = merge([(block[:half], block[half:]) for block in blocks])
                dist, count = settle(*found, at_source)
                near[k * n_col + r, :half, :] = dist
                near[k * n_col + r, half:, :] = count
        for c in range(n_row):
            at_source = is_source(ids, c * n_col + my_col)
            blocks = [came[chip * n_col + my_col, c] for chip in range(chips)]
            found = merge([(block[:half], block[half:]) for block in blocks])
            dist, count = settle(*found, at_source)
            low[c, :half, :] = dist
            low[c, half:, :] = count
            lower[c, :half, :] = dist
            lower[c, half:, :] = jnp.where(count > 0.5, 1.0 / jnp.maximum(count, 1.0), 0.0)
    else:
        other = came[(PAIR * my_x + 1 - my_core) * n_col + my_col]
        for core in range(PAIR):
            block = jnp.where(my_core == core, near[my_col], other)
            dist = block[:half]
            shown[pl.ds(core * half, half), :] = jnp.where(dist < 0.5 * far_value, dist, -1.0)
            paths[pl.ds(core * half, half), :] = block[half:]
        for chip in range(chips):
            line = (PAIR * chip + my_core) * n_col
            parts = [came[line + col] for col in range(n_col)]
            total = functools.reduce(jnp.add, parts)
            for h in range(PAIR):
                c = PAIR * chip + h
                count = low[c, half:, :]
                coef = (1.0 + count * total[h * half : h * half + half]) / jnp.maximum(count, 1.0)
                lower[c, :half, :] = low[c, :half, :]
                lower[c, half:, :] = jnp.where(count > 0.5, coef, 0.0)
    acc[...] = jnp.zeros(acc.shape, jnp.float32)

    def column(c, _):
        turned = lower[c].T
        for s in range(half):
            dist = jnp.broadcast_to(turned[:, s : s + 1], (LANES, LANES))
            coef = jnp.broadcast_to(turned[:, half + s : half + s + 1], (LANES, LANES))

            def step(k, g, b, carry):
                hit = tiles[k][g] + near[b, pl.ds(s, 1), :] == dist
                terms = jnp.where(hit, coef, 0.0).reshape(LANES // SUB, SUB, LANES)
                acc[b, s] += jnp.sum(terms, axis=0)
                return carry

            over_slots(dims, places, table, filled, c, step, 0)
        return 0

    lax.fori_loop(0, n_row, column, 0)
    for r in range(n_col):
        for k in range(PAIR):
            if last:
                b = k * n_col + r
                at_source = is_source(ids, (PAIR * my_x + (my_core ^ k)) * n_col + r)
                term = jnp.where(at_source, 0.0, near[b, half:, :] * jnp.sum(acc[b], axis=1))
                out[(my_core ^ k) * n_col + r] = jnp.sum(term, axis=0, keepdims=True)
            else:
                sums = jnp.sum(acc[(my_core ^ k) * n_col + r], axis=1)
                for chip in range(chips):
                    line = (PAIR * chip + my_core) * n_col
                    out[line + r, pl.ds(k * half, half), :] = sums
    if not last:
        for chip in range(chips):
            for r in range(n_col):
                out[(PAIR * chip + 1 - my_core) * n_col + r] = near[n_col + my_col]


def depend_level(dims, first, last, places, sources, tiles, bands, came):
    n_row, n_col, slots, half = dims
    if last:
        out_shape = [piece(PAIR * n_col, 1, LANES)]
    else:
        out_shape = [piece(n_row * n_col, PAIR * half, LANES)]
    if first:
        out_shape += [piece(PAIR * n_col, 2 * half, LANES), piece(n_row, 2 * half, LANES)]
    else:
        out_shape += [piece(PAIR * half, LANES)] * 2
    return pl.pallas_call(
        functools.partial(depend_kernel, dims, first, last),
        out_shape=out_shape,
        in_specs=[in_smem()] * (len(places) + 1) + [in_vmem()] * (PAIR + len(bands) + 1),
        out_specs=[in_vmem()] * len(out_shape),
        scratch_shapes=[
            pltpu.VMEM((n_row, 2 * half, LANES), jnp.float32),
            pltpu.VMEM((PAIR * n_col, half, SUB, LANES), jnp.float32),
        ]
        + slot_scratch(dims),
        compiler_params=params(large_limit),
        name="depend_level",
    )(*places, sources, *tiles, *bands, came)


def all_to_all(value, axes):
    return lax.all_to_all(value, axes, split_axis=0, concat_axis=0, tiled=True)


def swap_core(value):
    return lax.ppermute(value, "core", [(0, 1), (1, 0)])


def per_device(tiles, tile_index, tile_count, sources):
    slots = tiles.shape[0]
    rows = sources.shape[0]
    dims = (lax.axis_size("chip") * PAIR, lax.axis_size("col"), slots, rows // PAIR)
    own_places = tile_index.T
    line = ("chip", "col")

    everyone = ("chip", "core", "col")

    firsts, turned = first_level(dims, own_places, sources, tiles)
    both = [turned, swap_core(turned)]
    places = [] if is_dense(dims) else [own_places, swap_core(own_places)]
    came = all_to_all(firsts, everyone)
    for level_no in range(1, LEVELS):
        whole = level_no == LEVELS - 1
        outs = relax_level(dims, level_no > 1, whole, places, sources, both, came)
        came = all_to_all(outs, line)
    sums, *bands = depend_level(dims, True, False, places, sources, both, [], came)
    for back_no in range(1, BACK):
        last = back_no == BACK - 1
        came = all_to_all(sums, everyone)
        sums, shown, paths = depend_level(dims, False, last, places, sources, both, bands, came)
    total = jnp.sum(all_to_all(sums, ("core", "col")), axis=(0, 1))
    return shown, paths, total / rows


def solution(mesh):
    groups, rows, cols = mesh.devices.shape
    pairs = mesh.devices.reshape(groups, rows // PAIR, PAIR, cols)
    paired = jax.sharding.Mesh(pairs, ("groups", "chip", "core", "col"))
    vertices = ("chip", "core", "col")
    everywhere = ("groups",) + vertices
    in_specs = (P(everywhere, None, None), P(everywhere, None), P(everywhere), P("groups"))
    out_specs = (P("groups", vertices), P("groups", vertices), P(everywhere))
    return jax.shard_map(
        per_device, mesh=paired, in_specs=in_specs, out_specs=out_specs, check_vma=False
    )
```

profile of v0, /device:TPU:0, one launch (start us, length us, event | category | flops | bytes accessed | tf_op | source)
XLA Modules:
  0.0 65.2 jit_solution(9611336318616046567)
XLA Ops:
  0.6 0.0 copy-start.1
  0.6 0.0 copy-start.2
  0.7 0.6 copy-done.1
  1.3 0.0 copy-done.2
  1.3 0.0 copy-start
  1.3 1.2 %copy-done = f32[16,128,128]{2,1,0:T(8,128)S(1)} copy-done((f32[16,128,128]{2,1,0:T(8,128)S(1)}, f32[16,128,128]{2,1,0:T(8,128)}, u32[]{:S(2)}) %copy-start) | copy-done | bytes 1048600
  2.6 1.1 %first_level.1 = (f32[16,8,128]{2,1,0:T(8,128)S(1)}, f32[16,128,128]{2,1,0:T(8,128)S(1)}) custom-call(s32[2,16]{1,0:T(2,128)S(1)} %bitcast.1, s32[8]{0:T(128)S(1)} %copy-done.1, f32[16,128,128]{2,1,0:T(8,128)S(1)} %copy-done), custom_call_target="tpu_custom_call" | custom-call | tf_op jit(solution)/shard_map/first_level/pallas_call | solution.py:113
  3.7 0.5 collective-permute-start
  4.2 13.5 %all_to_all.25.refs_3_ = f32[16,8,128]{2,1,0:T(8,128)S(1)} all-to-all(f32[16,8,128]{2,1,0:T(8,128)S(1)} %get-tuple-element.12), channel_id=1, replica_groups=mesh['groups'=2,'chip'=2,'core'=2,'col'=4] {'chip','core','col'}, dimensions={0} | all-to-all | bytes 131072 | tf_op jit(solution)/shard_map/all_to_all | solution.py:365
  17.7 0.0 collective-permute-done.refs_2_
  17.7 2.8 %relax_level.2 = f32[8,2,8,128]{3,2,1,0:T(8,128)S(1)} custom-call(s32[8]{0:T(128)S(1)} %copy-done.1, f32[16,128,128]{2,1,0:T(8,128)S(1)} %get-tuple-element.11.refs_1_, f32[16,128,128]{2,1,0:T(8,128)S(1)} %collective-permute-done.refs_2_, f32[16,8,128]{2,1,0:T(8,128)S(1)} %all_to_all.25.refs_3_), custom_call_target="tpu_custom_call" | custom-call | tf_op jit(solution)/shard_map/relax_level/pallas_call | solution.py:239
  20.5 9.4 %all_to_all.26.refs_3_ = f32[8,2,8,128]{3,2,1,0:T(8,128)S(1)} all-to-all(f32[8,2,8,128]{3,2,1,0:T(8,128)S(1)} %relax_level.2), channel_id=1, replica_groups=mesh['groups'=2,'chip'=2,'core'=2,'col'=4] {'chip','col'}, dimensions={0} | all-to-all | bytes 131072 | tf_op jit(solution)/shard_map/all_to_all | solution.py:365
  29.8 2.8 %relax_level.3 = f32[8,4,8,128]{3,2,1,0:T(8,128)S(1)} custom-call(s32[8]{0:T(128)S(1)} %copy-done.1, f32[16,128,128]{2,1,0:T(8,128)S(1)} %get-tuple-element.11.refs_1_, f32[16,128,128]{2,1,0:T(8,128)S(1)} %collective-permute-done.refs_2_, f32[8,2,8,128]{3,2,1,0:T(8,128)S(1)} %all_to_all.26.refs_3_), custom_call_target="tpu_custom_call" | custom-call | tf_op jit(solution)/shard_map/relax_level/pallas_call | solution.py:239
  32.7 9.9 %all_to_all.27.refs_3_ = f32[8,4,8,128]{3,2,1,0:T(8,128)S(1)} all-to-all(f32[8,4,8,128]{3,2,1,0:T(8,128)S(1)} %relax_level.3), channel_id=1, replica_groups=mesh['groups'=2,'chip'=2,'core'=2,'col'=4] {'chip','col'}, dimensions={0} | all-to-all | bytes 262144 | tf_op jit(solution)/shard_map/all_to_all | solution.py:365
  42.6 2.5 %depend_level.2 = (f32[16,8,128]{2,1,0:T(8,128)S(1)}, f32[8,8,128]{2,1,0:T(8,128)S(1)}, f32[4,8,128]{2,1,0:T(8,128)S(1)}) custom-call(s32[8]{0:T(128)S(1)} %copy-done.1, f32[16,128,128]{2,1,0:T(8,128)S(1)} %get-tuple-element.11.refs_1_, f32[16,128,128]{2,1,0:T(8,128)S(1)} %collective-permute-done.refs_2_, f32[8,4,8,128]{3,2,1,0:T(8,128)S(1)} %all_to_all.27.refs_3_), custom_call_target="tpu_custom_call" | custom-call | tf_op jit(solution)/shard_map/depend_level/pallas_call | solution.py:349
  45.0 9.2 %all_to_all.28.refs_5_ = f32[16,8,128]{2,1,0:T(8,128)S(1)} all-to-all(f32[16,8,128]{2,1,0:T(8,128)S(1)} %get-tuple-element.15), channel_id=1, replica_groups=mesh['groups'=2,'chip'=2,'core'=2,'col'=4] {'chip','core','col'}, dimensions={0} | all-to-all | bytes 131072 | tf_op jit(solution)/shard_map/all_to_all | solution.py:365
  54.2 2.6 %depend_level.3 = (f32[8,1,128]{2,1,0:T(1,128)S(1)}, f32[8,128]{1,0:T(8,128)}, f32[8,128]{1,0:T(8,128)}) custom-call(s32[8]{0:T(128)S(1)} %copy-done.1, f32[16,128,128]{2,1,0:T(8,128)S(1)} %get-tuple-element.11.refs_1_, f32[16,128,128]{2,1,0:T(8,128)S(1)} %collective-permute-done.refs_2_, f32[8,8,128]{2,1,0:T(8,128)S(1)} %get-tuple-element.13.refs_3_, ...), custom_call_target="tpu_custom_call" | custom-call | tf_op jit(solution)/shard_map/depend_level/pallas_call | solution.py:349
  56.8 7.9 %all_to_all.29 = f32[8,1,128]{2,1,0:T(1,128)S(1)} all-to-all(f32[8,1,128]{2,1,0:T(1,128)S(1)} %get-tuple-element.18), channel_id=1, replica_groups=mesh['groups'=2,'chip'=2,'core'=2,'col'=4] {'core','col'}, dimensions={0} | all-to-all | bytes 8192 | tf_op jit(solution)/shard_map/all_to_all | solution.py:365
  64.7 0.5 broadcast_multiply_fusion
  (1 shorter events, 0.0 us)
Async XLA Ops:
  0.6 0.7 %copy-start.1 = (s32[8]{0:T(128)S(1)}, s32[8]{0:T(128)}, u32[]{:S(2)}) copy-start(s32[8]{0:T(128)} %refs_0_.7) | copy-start | bytes 100
  0.6 0.7 %copy-start.2 = (s32[16,2]{0,1:T(2,128)S(1)}, s32[16,2]{0,1:T(2,128)}, u32[]{:S(2)}) copy-start(s32[16,2]{0,1:T(2,128)} %param.5) | copy-start | bytes 388
  1.3 1.2 %copy-start = (f32[16,128,128]{2,1,0:T(8,128)S(1)}, f32[16,128,128]{2,1,0:T(8,128)}, u32[]{:S(2)}) copy-start(f32[16,128,128]{2,1,0:T(8,128)} %tiles.1) | copy-start | bytes 3145732
  3.7 14.0 %collective-permute-start = (f32[16,128,128]{2,1,0:T(8,128)S(1)}, f32[16,128,128]{2,1,0:T(8,128)S(1)}, u32[]{:S(2)}, u32[]{:S(2)}) collective-permute-start(f32[16,128,128]{2,1,0:T(8,128)S(1)} %get-tuple-element.11.refs_1_), channel_id=1, source_target_pairs={{0,4},{4,0},{1,5},{5,1},{2,6},{6,2},{3,7},{7,3},{8,12},{12,8},{9,1... | collective-permute-start | bytes 3145736 | tf_op jit(solution)/shard_map/ppermute | solution.py:369
where the time goes:
time: 65.6 us; the launch traced here: 65.2 us
  blocking collectives  49.9 us (76%)
  Pallas kernels  11.8 us (18%)
  local copies, waits for them, and re-layouts  1.9 us (3%)
  between operations  0.68 us (1%)
    all_to_all x5, blocking collectives, all_to_all(): return lax.all_to_all(value, axes, split_axis=0, concat_axis=0, tiled=True)  49.9 us
    pallas_call x2, Pallas kernels, relax_level(): pl.pallas_call(functools.partial(relax_kernel, dims, counted, whole), out...  5.63 us
    pallas_call x2, Pallas kernels, depend_level(): pl.pallas_call(functools.partial(depend_kernel, dims, first, last), out_s...  5.02 us
    unnamed x6, local copies, waits for them, and re-layouts  1.9 us
  transfers between devices with their start and end apart: 1, of which 0 were waited for; matrix products, arithmetic and copies ran while one was open for 0% of the time, Pallas kernels for 0%

commit v1 on v0

--- a/solution.py
+++ b/solution.py
@@ -12,6 +12,7 @@
 LANES = 128
 SUB = 8
 PAIR = 2
+UNROLL = 2
 
 far_value = 1000000.0
 no_edge = 2000000.0
@@ -67,7 +68,7 @@
     return best, total
 
 
-def first_kernel(dims, places, sources, tiles, out, turned, slot_of, lines):
+def first_kernel(dims, places, sources, tiles, out, turned, ids, slot_of, lines):
     n_row, n_col, slots, half = dims
     my_x, my_core, my_col = position()
     my_row = my_x * PAIR + my_core
@@ -80,6 +81,7 @@
         lax.fori_loop(0, n_row * n_col, clear, 0)
     for g in range(slots):
         slot_of[places[0, g] * n_row + places[1, g]] = g
+    ids[...] = source_ids(sources, my_core * half, half)
     lines[...] = jnp.zeros(lines.shape, jnp.float32)
     for s in range(PAIR * half):
         vertex = sources[s]
@@ -112,9 +114,13 @@
     n_row, n_col, slots, half = dims
     return pl.pallas_call(
         functools.partial(first_kernel, dims),
-        out_shape=[piece(n_row * n_col, PAIR * half, LANES), piece(*tiles.shape)],
+        out_shape=[
+            piece(n_row * n_col, PAIR * half, LANES),
+            piece(*tiles.shape),
+            jax.ShapeDtypeStruct((half, LANES), jnp.int32),
+        ],
         in_specs=[in_smem(), in_smem(), in_vmem()],
-        out_specs=[in_vmem()] * 2,
+        out_specs=[in_vmem()] * 3,
         scratch_shapes=[
             pltpu.SMEM((n_row * n_col,), jnp.int32),
             pltpu.VMEM((n_row // PAIR, PAIR, PAIR * half, LANES), jnp.float32),
@@ -175,10 +181,10 @@
     chips = n_row // PAIR
     n_places = 0 if is_dense(dims) else PAIR
     places, refs = refs[:n_places], refs[n_places:]
-    sources, tiles, refs = refs[0], refs[1 : 1 + PAIR], refs[1 + PAIR :]
+    source_rows, tiles, refs = refs[0], refs[1 : 1 + PAIR], refs[1 + PAIR :]
     came, out, near, found, table, filled = refs
     my_x, my_core, my_col = position()
-    ids = source_ids(sources, my_core * half, half)
+    ids = source_rows[...]
     list_slots(dims, places, table, filled)
     for r in range(n_col):
         for k in range(PAIR):
@@ -224,7 +230,7 @@
         found[c] = turned.T[: 2 * half]
         return 0
 
-    lax.fori_loop(0, n_row, column, 0)
+    lax.fori_loop(0, n_row, column, 0, unroll=UNROLL)
     for chip in range(chips):
         for col in range(n_col):
             if whole:
@@ -233,13 +239,13 @@
                 out[chip * n_col + col] = found[pl.ds(PAIR * chip, PAIR)]
 
 
-def relax_level(dims, counted, whole, places, sources, tiles, came):
+def relax_level(dims, counted, whole, places, ids, tiles, came):
     n_row, n_col, slots, half = dims
     blocks = n_row if whole else PAIR
     return pl.pallas_call(
         functools.partial(relax_kernel, dims, counted, whole),
         out_shape=piece(n_row // PAIR * n_col, blocks, 2 * half, LANES),
-        in_specs=[in_smem()] * (len(places) + 1) + [in_vmem()] * (PAIR + 1),
+        in_specs=[in_smem()] * len(places) + [in_vmem()] * (PAIR + 2),
         out_specs=in_vmem(),
         scratch_shapes=[
             pltpu.VMEM((PAIR * n_col, 2 * half, LANES), jnp.float32),
@@ -248,7 +254,7 @@
         + slot_scratch(dims),
         compiler_params=params(large_limit),
         name="relax_level",
-    )(*places, sources, *tiles, came)
+    )(*places, ids, *tiles, came)
 
 
 def depend_kernel(dims, first, last, *refs):
@@ -256,13 +262,13 @@
     chips = n_row // PAIR
     n_places = 0 if is_dense(dims) else PAIR
     places, refs = refs[:n_places], refs[n_places:]
-    sources, tiles, refs = refs[0], refs[1 : 1 + PAIR], refs[1 + PAIR :]
+    source_rows, tiles, refs = refs[0], refs[1 : 1 + PAIR], refs[1 + PAIR :]
     if first:
         came, out, near, low, lower, acc, table, filled = refs
     else:
         near, low, came, out, shown, paths, lower, acc, table, filled = refs
     my_x, my_core, my_col = position()
-    ids = source_ids(sources, my_core * half, half)
+    ids = source_rows[...]
     list_slots(dims, places, table, filled)
     if first:
         for r in range(n_col):
@@ -317,7 +323,7 @@
             over_slots(dims, places, table, filled, c, step, 0)
         return 0
 
-    lax.fori_loop(0, n_row, column, 0)
+    lax.fori_loop(0, n_row, column, 0, unroll=UNROLL)
     for r in range(n_col):
         for k in range(PAIR):
             if last:
@@ -336,7 +342,7 @@
                 out[(PAIR * chip + 1 - my_core) * n_col + r] = near[n_col + my_col]
 
 
-def depend_level(dims, first, last, places, sources, tiles, bands, came):
+def depend_level(dims, first, last, places, ids, tiles, bands, came):
     n_row, n_col, slots, half = dims
     if last:
         out_shape = [piece(PAIR * n_col, 1, LANES)]
@@ -349,7 +355,7 @@
     return pl.pallas_call(
         functools.partial(depend_kernel, dims, first, last),
         out_shape=out_shape,
-        in_specs=[in_smem()] * (len(places) + 1) + [in_vmem()] * (PAIR + len(bands) + 1),
+        in_specs=[in_smem()] * len(places) + [in_vmem()] * (PAIR + len(bands) + 2),
         out_specs=[in_vmem()] * len(out_shape),
         scratch_shapes=[
             pltpu.VMEM((n_row, 2 * half, LANES), jnp.float32),
@@ -358,7 +364,7 @@
         + slot_scratch(dims),
         compiler_params=params(large_limit),
         name="depend_level",
-    )(*places, sources, *tiles, *bands, came)
+    )(*places, ids, *tiles, *bands, came)
 
 
 def all_to_all(value, axes):
@@ -378,19 +384,19 @@
 
     everyone = ("chip", "core", "col")
 
-    firsts, turned = first_level(dims, own_places, sources, tiles)
+    firsts, turned, ids = first_level(dims, own_places, sources, tiles)
     both = [turned, swap_core(turned)]
     places = [] if is_dense(dims) else [own_places, swap_core(own_places)]
     came = all_to_all(firsts, everyone)
     for level_no in range(1, LEVELS):
         whole = level_no == LEVELS - 1
-        outs = relax_level(dims, level_no > 1, whole, places, sources, both, came)
+        outs = relax_level(dims, level_no > 1, whole, places, ids, both, came)
         came = all_to_all(outs, line)
-    sums, *bands = depend_level(dims, True, False, places, sources, both, [], came)
+    sums, *bands = depend_level(dims, True, False, places, ids, both, [], came)
     for back_no in range(1, BACK):
         last = back_no == BACK - 1
         came = all_to_all(sums, everyone)
-        sums, shown, paths = depend_level(dims, False, last, places, sources, both, bands, came)
+        sums, shown, paths = depend_level(dims, False, last, places, ids, both, bands, came)
     total = jnp.sum(all_to_all(sums, ("core", "col")), axis=(0, 1))
     return shown, paths, total / rows
 

time: 65.6 us -> 63 us (0.960)
  Pallas kernels: 11.8 us -> 9.2 us
    pallas_call x2, Pallas kernels: 5.63 us -> 4.08 us  [relax_level(): pl.pallas_call(functools.partial(relax_kernel, dims, counted, whole), out...]
    pallas_call x2, Pallas kernels: 5.02 us -> 3.95 us  [depend_level(): pl.pallas_call(functools.partial(depend_kernel, dims, first, last), out_s...]
where the time goes in v1:
time: 63 us; the launch traced here: 62.6 us
  blocking collectives  49.8 us (79%)
  Pallas kernels  9.2 us (15%)
  local copies, waits for them, and re-layouts  1.9 us (3%)
  between operations  0.68 us (1%)
    all_to_all x5, blocking collectives, all_to_all(): return lax.all_to_all(value, axes, split_axis=0, concat_axis=0, tiled=True)  49.8 us
    pallas_call x2, Pallas kernels, relax_level(): pl.pallas_call(functools.partial(relax_kernel, dims, counted, whole), out...  4.08 us
    pallas_call x2, Pallas kernels, depend_level(): pl.pallas_call(functools.partial(depend_kernel, dims, first, last), out_s...  3.95 us
    unnamed x6, local copies, waits for them, and re-layouts  1.9 us
  transfers between devices with their start and end apart: 1, of which 0 were waited for; matrix products, arithmetic and copies ran while one was open for 0% of the time, Pallas kernels for 0%

profile of v1, /device:TPU:0, one launch (start us, length us, event | category | flops | bytes accessed | tf_op | source)
XLA Modules:
  0.0 62.6 jit_solution(14579715019136065341)
XLA Ops:
  0.6 0.0 copy-start.2
  0.6 0.0 copy-start.1
  0.7 0.6 %copy-done.2 = s32[8]{0:T(128)S(1)} copy-done((s32[8]{0:T(128)S(1)}, s32[8]{0:T(128)}, u32[]{:S(2)}) %copy-start.2) | copy-done | bytes 56
  1.3 0.0 copy-done.1
  1.3 0.0 copy-start
  1.3 1.2 %copy-done = f32[16,128,128]{2,1,0:T(8,128)S(1)} copy-done((f32[16,128,128]{2,1,0:T(8,128)S(1)}, f32[16,128,128]{2,1,0:T(8,128)}, u32[]{:S(2)}) %copy-start) | copy-done | bytes 1048600
  2.6 1.2 %first_level.1 = (f32[16,8,128]{2,1,0:T(8,128)S(1)}, f32[16,128,128]{2,1,0:T(8,128)S(1)}, s32[4,128]{1,0:T(4,128)S(1)}) custom-call(s32[2,16]{1,0:T(2,128)S(1)} %bitcast.1, s32[8]{0:T(128)S(1)} %copy-done.2, f32[16,128,128]{2,1,0:T(8,128)S(1)} %copy-done), custom_call_target="tpu_custom_call" | custom-call | tf_op jit(solution)/shard_map/first_level/pallas_call | solution.py:115
  3.7 0.5 collective-permute-start
  4.2 13.4 %all_to_all.25.refs_3_ = f32[16,8,128]{2,1,0:T(8,128)S(1)} all-to-all(f32[16,8,128]{2,1,0:T(8,128)S(1)} %get-tuple-element.14), channel_id=1, replica_groups=mesh['groups'=2,'chip'=2,'core'=2,'col'=4] {'chip','core','col'}, dimensions={0} | all-to-all | bytes 131072 | tf_op jit(solution)/shard_map/all_to_all | solution.py:371
  17.6 0.0 collective-permute-done.refs_2_
  17.6 2.0 %relax_level.2 = f32[8,2,8,128]{3,2,1,0:T(8,128)S(1)} custom-call(s32[4,128]{1,0:T(4,128)S(1)} %get-tuple-element.12.refs_0_, f32[16,128,128]{2,1,0:T(8,128)S(1)} %get-tuple-element.13.refs_1_, f32[16,128,128]{2,1,0:T(8,128)S(1)} %collective-permute-done.refs_2_, f32[16,8,128]{2,1,0:T(8,128)S(1)} %all_to_all.25.refs_3_), custom_call_target="tpu_custom_call" | custom-call | tf_op jit(solution)/shard_map/relax_level/pallas_call | solution.py:245
  19.7 9.4 %all_to_all.26.refs_3_ = f32[8,2,8,128]{3,2,1,0:T(8,128)S(1)} all-to-all(f32[8,2,8,128]{3,2,1,0:T(8,128)S(1)} %relax_level.2), channel_id=1, replica_groups=mesh['groups'=2,'chip'=2,'core'=2,'col'=4] {'chip','col'}, dimensions={0} | all-to-all | bytes 131072 | tf_op jit(solution)/shard_map/all_to_all | solution.py:371
  29.0 2.0 %relax_level.3 = f32[8,4,8,128]{3,2,1,0:T(8,128)S(1)} custom-call(s32[4,128]{1,0:T(4,128)S(1)} %get-tuple-element.12.refs_0_, f32[16,128,128]{2,1,0:T(8,128)S(1)} %get-tuple-element.13.refs_1_, f32[16,128,128]{2,1,0:T(8,128)S(1)} %collective-permute-done.refs_2_, f32[8,2,8,128]{3,2,1,0:T(8,128)S(1)} %all_to_all.26.refs_3_), custom_call_target="tpu_custom_call" | custom-call | tf_op jit(solution)/shard_map/relax_level/pallas_call | solution.py:245
  31.1 9.9 %all_to_all.27.refs_3_ = f32[8,4,8,128]{3,2,1,0:T(8,128)S(1)} all-to-all(f32[8,4,8,128]{3,2,1,0:T(8,128)S(1)} %relax_level.3), channel_id=1, replica_groups=mesh['groups'=2,'chip'=2,'core'=2,'col'=4] {'chip','col'}, dimensions={0} | all-to-all | bytes 262144 | tf_op jit(solution)/shard_map/all_to_all | solution.py:371
  41.0 1.7 %depend_level.2 = (f32[16,8,128]{2,1,0:T(8,128)S(1)}, f32[8,8,128]{2,1,0:T(8,128)S(1)}, f32[4,8,128]{2,1,0:T(8,128)S(1)}) custom-call(s32[4,128]{1,0:T(4,128)S(1)} %get-tuple-element.12.refs_0_, f32[16,128,128]{2,1,0:T(8,128)S(1)} %get-tuple-element.13.refs_1_, f32[16,128,128]{2,1,0:T(8,128)S(1)} %collective-permute-done.refs_2_, ...), custom_call_target="tpu_custom_call" | custom-call | tf_op jit(solution)/shard_map/depend_level/pallas_call | solution.py:355
  42.7 9.2 %all_to_all.28.refs_5_ = f32[16,8,128]{2,1,0:T(8,128)S(1)} all-to-all(f32[16,8,128]{2,1,0:T(8,128)S(1)} %get-tuple-element.17), channel_id=1, replica_groups=mesh['groups'=2,'chip'=2,'core'=2,'col'=4] {'chip','core','col'}, dimensions={0} | all-to-all | bytes 131072 | tf_op jit(solution)/shard_map/all_to_all | solution.py:371
  51.9 2.2 %depend_level.3 = (f32[8,1,128]{2,1,0:T(1,128)S(1)}, f32[8,128]{1,0:T(8,128)}, f32[8,128]{1,0:T(8,128)}) custom-call(s32[4,128]{1,0:T(4,128)S(1)} %get-tuple-element.12.refs_0_, f32[16,128,128]{2,1,0:T(8,128)S(1)} %get-tuple-element.13.refs_1_, f32[16,128,128]{2,1,0:T(8,128)S(1)} %collective-permute-done.refs_2_, ...), custom_call_target="tpu_custom_call" | custom-call | tf_op jit(solution)/shard_map/depend_level/pallas_call | solution.py:355
  54.2 7.9 %all_to_all.29 = f32[8,1,128]{2,1,0:T(1,128)S(1)} all-to-all(f32[8,1,128]{2,1,0:T(1,128)S(1)} %get-tuple-element.20), channel_id=1, replica_groups=mesh['groups'=2,'chip'=2,'core'=2,'col'=4] {'core','col'}, dimensions={0} | all-to-all | bytes 8192 | tf_op jit(solution)/shard_map/all_to_all | solution.py:371
  62.1 0.5 broadcast_multiply_fusion
  (1 shorter events, 0.0 us)
Async XLA Ops:
  0.6 0.7 %copy-start.2 = (s32[8]{0:T(128)S(1)}, s32[8]{0:T(128)}, u32[]{:S(2)}) copy-start(s32[8]{0:T(128)} %sources.1) | copy-start | bytes 100
  0.6 0.7 %copy-start.1 = (s32[16,2]{0,1:T(2,128)S(1)}, s32[16,2]{0,1:T(2,128)}, u32[]{:S(2)}) copy-start(s32[16,2]{0,1:T(2,128)} %param.5) | copy-start | bytes 388
  1.3 1.2 %copy-start = (f32[16,128,128]{2,1,0:T(8,128)S(1)}, f32[16,128,128]{2,1,0:T(8,128)}, u32[]{:S(2)}) copy-start(f32[16,128,128]{2,1,0:T(8,128)} %tiles.1) | copy-start | bytes 3145732
  3.7 13.9 %collective-permute-start = (f32[16,128,128]{2,1,0:T(8,128)S(1)}, f32[16,128,128]{2,1,0:T(8,128)S(1)}, u32[]{:S(2)}, u32[]{:S(2)}) collective-permute-start(f32[16,128,128]{2,1,0:T(8,128)S(1)} %get-tuple-element.13.refs_1_), channel_id=1, source_target_pairs={{0,4},{4,0},{1,5},{5,1},{2,6},{6,2},{3,7},{7,3},{8,12},{12,8},{9,1... | collective-permute-start | bytes 3145736 | tf_op jit(solution)/shard_map/ppermute | solution.py:375

commit v2 on v1

--- a/solution.py
+++ b/solution.py
@@ -191,7 +191,7 @@
             h = my_core ^ k
             at_source = is_source(ids, (PAIR * my_x + h) * n_col + r)
             if counted:
-                blocks = [came[chip * n_col + r, h] for chip in range(chips)]
+                blocks = [came[r * chips + chip, h] for chip in range(chips)]
                 reached, count = merge([(block[:half], block[half:]) for block in blocks])
             else:
                 parts = [came[at * n_col + r, pl.ds(h * half, half), :] for at in range(n_row)]
@@ -234,9 +234,9 @@
     for chip in range(chips):
         for col in range(n_col):
             if whole:
-                out[chip * n_col + col] = found[...]
+                out[col * chips + chip] = found[...]
             else:
-                out[chip * n_col + col] = found[pl.ds(PAIR * chip, PAIR)]
+                out[col * chips + chip] = found[pl.ds(PAIR * chip, PAIR)]
 
 
 def relax_level(dims, counted, whole, places, ids, tiles, came):
@@ -266,7 +266,7 @@
     if first:
         came, out, near, low, lower, acc, table, filled = refs
     else:
-        near, low, came, out, shown, paths, lower, acc, table, filled = refs
+        near, low, came, out, state, lower, acc, table, filled = refs
     my_x, my_core, my_col = position()
     ids = source_rows[...]
     list_slots(dims, places, table, filled)
@@ -275,14 +275,14 @@
             for k in range(PAIR):
                 h = my_core ^ k
                 at_source = is_source(ids, (PAIR * my_x + h) * n_col + r)
-                blocks = [came[chip * n_col + r, PAIR * my_x + h] for chip in range(chips)]
+                blocks = [came[r * chips + chip, PAIR * my_x + h] for chip in range(chips)]
                 found = merge([(block[:half], block[half:]) for block in blocks])
                 dist, count = settle(*found, at_source)
                 near[k * n_col + r, :half, :] = dist
                 near[k * n_col + r, half:, :] = count
         for c in range(n_row):
             at_source = is_source(ids, c * n_col + my_col)
-            blocks = [came[chip * n_col + my_col, c] for chip in range(chips)]
+            blocks = [came[my_col * chips + chip, c] for chip in range(chips)]
             found = merge([(block[:half], block[half:]) for block in blocks])
             dist, count = settle(*found, at_source)
             low[c, :half, :] = dist
@@ -294,8 +294,9 @@
         for core in range(PAIR):
             block = jnp.where(my_core == core, near[my_col], other)
             dist = block[:half]
-            shown[pl.ds(core * half, half), :] = jnp.where(dist < 0.5 * far_value, dist, -1.0)
-            paths[pl.ds(core * half, half), :] = block[half:]
+            rows = pl.ds(core * half, half)
+            state[0, rows, :] = jnp.where(dist < 0.5 * far_value, dist, -1.0)
+            state[1, rows, :] = block[half:]
         for chip in range(chips):
             line = (PAIR * chip + my_core) * n_col
             parts = [came[line + col] for col in range(n_col)]
@@ -351,7 +352,7 @@
     if first:
         out_shape += [piece(PAIR * n_col, 2 * half, LANES), piece(n_row, 2 * half, LANES)]
     else:
-        out_shape += [piece(PAIR * half, LANES)] * 2
+        out_shape += [piece(2, PAIR * half, LANES)]
     return pl.pallas_call(
         functools.partial(depend_kernel, dims, first, last),
         out_shape=out_shape,
@@ -367,6 +368,25 @@
     )(*places, ids, *tiles, *bands, came)
 
 
+def result_kernel(rows, came, state, shown, paths, centrality):
+    shown[...] = state[0]
+    paths[...] = state[1]
+    shares = [came[at] for at in range(came.shape[0])]
+    centrality[...] = functools.reduce(jnp.add, shares) / rows
+
+
+def results(dims, came, state):
+    rows = PAIR * dims[3]
+    return pl.pallas_call(
+        functools.partial(result_kernel, rows),
+        out_shape=[piece(rows, LANES)] * 2 + [piece(1, LANES)],
+        in_specs=[in_vmem()] * 2,
+        out_specs=[in_vmem()] * 3,
+        compiler_params=params(small_limit),
+        name="results",
+    )(came, state)
+
+
 def all_to_all(value, axes):
     return lax.all_to_all(value, axes, split_axis=0, concat_axis=0, tiled=True)
 
@@ -380,7 +400,7 @@
     rows = sources.shape[0]
     dims = (lax.axis_size("chip") * PAIR, lax.axis_size("col"), slots, rows // PAIR)
     own_places = tile_index.T
-    line = ("chip", "col")
+    line = ("col", "chip")
 
     everyone = ("chip", "core", "col")
 
@@ -396,9 +416,9 @@
     for back_no in range(1, BACK):
         last = back_no == BACK - 1
         came = all_to_all(sums, everyone)
-        sums, shown, paths = depend_level(dims, False, last, places, ids, both, bands, came)
-    total = jnp.sum(all_to_all(sums, ("core", "col")), axis=(0, 1))
-    return shown, paths, total / rows
+        sums, state = depend_level(dims, False, last, places, ids, both, bands, came)
+    shown, paths, centrality = results(dims, all_to_all(sums, ("core", "col")), state)
+    return shown, paths, centrality.reshape(LANES)
 
 
 def solution(mesh):

time: 63 us -> 62.3 us (0.989)
  no operation moved by 1% of the time
where the time goes in v2:
time: 62.3 us; the launch traced here: 61.9 us
  blocking collectives  49.6 us (80%)
  Pallas kernels  9.3 us (15%)
  local copies, waits for them, and re-layouts  1.9 us (3%)
  between operations  0.68 us (1%)
    all_to_all x5, blocking collectives, all_to_all(): return lax.all_to_all(value, axes, split_axis=0, concat_axis=0, tiled=True)  49.6 us
    pallas_call x2, Pallas kernels, relax_level(): pl.pallas_call(functools.partial(relax_kernel, dims, counted, whole), out...  4.08 us
    pallas_call x2, Pallas kernels, depend_level(): pl.pallas_call(functools.partial(depend_kernel, dims, first, last), out_s...  3.43 us
    unnamed x6, local copies, waits for them, and re-layouts  1.9 us
  transfers between devices with their start and end apart: 1, of which 0 were waited for; matrix products, arithmetic and copies ran while one was open for 0% of the time, Pallas kernels for 0%

profile of v2, /device:TPU:0, one launch (start us, length us, event | category | flops | bytes accessed | tf_op | source)
XLA Modules:
  0.0 61.9 jit_solution(3004825293596327994)
XLA Ops:
  0.6 0.0 copy-start.2
  0.6 0.0 copy-start.1
  0.7 0.6 %copy-done.2 = s32[8]{0:T(128)S(1)} copy-done((s32[8]{0:T(128)S(1)}, s32[8]{0:T(128)}, u32[]{:S(2)}) %copy-start.2) | copy-done | bytes 56
  1.3 0.0 copy-done.1
  1.3 0.0 copy-start
  1.3 1.2 %copy-done = f32[16,128,128]{2,1,0:T(8,128)S(1)} copy-done((f32[16,128,128]{2,1,0:T(8,128)S(1)}, f32[16,128,128]{2,1,0:T(8,128)}, u32[]{:S(2)}) %copy-start) | copy-done | bytes 1048600
  2.6 1.2 %first_level.1 = (f32[16,8,128]{2,1,0:T(8,128)S(1)}, f32[16,128,128]{2,1,0:T(8,128)S(1)}, s32[4,128]{1,0:T(4,128)S(1)}) custom-call(s32[2,16]{1,0:T(2,128)S(1)} %bitcast.2, s32[8]{0:T(128)S(1)} %copy-done.2, f32[16,128,128]{2,1,0:T(8,128)S(1)} %copy-done), custom_call_target="tpu_custom_call" | custom-call | tf_op jit(solution)/shard_map/first_level/pallas_call | solution.py:115
  3.8 0.4 collective-permute-start
  4.2 13.4 %all_to_all.25.refs_3_ = f32[16,8,128]{2,1,0:T(8,128)S(1)} all-to-all(f32[16,8,128]{2,1,0:T(8,128)S(1)} %get-tuple-element.16), channel_id=1, replica_groups=mesh['groups'=2,'chip'=2,'core'=2,'col'=4] {'chip','core','col'}, dimensions={0} | all-to-all | bytes 131072 | tf_op jit(solution)/shard_map/all_to_all | solution.py:391
  17.6 0.0 collective-permute-done.refs_2_
  17.6 2.0 %relax_level.2 = f32[8,2,8,128]{3,2,1,0:T(8,128)S(1)} custom-call(s32[4,128]{1,0:T(4,128)S(1)} %get-tuple-element.14.refs_0_, f32[16,128,128]{2,1,0:T(8,128)S(1)} %get-tuple-element.15.refs_1_, f32[16,128,128]{2,1,0:T(8,128)S(1)} %collective-permute-done.refs_2_, f32[16,8,128]{2,1,0:T(8,128)S(1)} %all_to_all.25.refs_3_), custom_call_target="tpu_custom_call" | custom-call | tf_op jit(solution)/shard_map/relax_level/pallas_call | solution.py:245
  19.7 9.3 %all_to_all.26.refs_3_ = f32[8,2,8,128]{3,2,1,0:T(8,128)S(1)} all-to-all(f32[8,2,8,128]{3,2,1,0:T(8,128)S(1)} %relax_level.2), channel_id=1, replica_groups=mesh['groups'=2,'chip'=2,'core'=2,'col'=4] {'col','chip'}, dimensions={0} | all-to-all | bytes 131072 | tf_op jit(solution)/shard_map/all_to_all | solution.py:391
  29.0 2.0 %relax_level.3 = f32[8,4,8,128]{3,2,1,0:T(8,128)S(1)} custom-call(s32[4,128]{1,0:T(4,128)S(1)} %get-tuple-element.14.refs_0_, f32[16,128,128]{2,1,0:T(8,128)S(1)} %get-tuple-element.15.refs_1_, f32[16,128,128]{2,1,0:T(8,128)S(1)} %collective-permute-done.refs_2_, f32[8,2,8,128]{3,2,1,0:T(8,128)S(1)} %all_to_all.26.refs_3_), custom_call_target="tpu_custom_call" | custom-call | tf_op jit(solution)/shard_map/relax_level/pallas_call | solution.py:245
  31.0 9.7 %all_to_all.27.refs_3_ = f32[8,4,8,128]{3,2,1,0:T(8,128)S(1)} all-to-all(f32[8,4,8,128]{3,2,1,0:T(8,128)S(1)} %relax_level.3), channel_id=1, replica_groups=mesh['groups'=2,'chip'=2,'core'=2,'col'=4] {'col','chip'}, dimensions={0} | all-to-all | bytes 262144 | tf_op jit(solution)/shard_map/all_to_all | solution.py:391
  40.7 1.7 %depend_level.2 = (f32[16,8,128]{2,1,0:T(8,128)S(1)}, f32[8,8,128]{2,1,0:T(8,128)S(1)}, f32[4,8,128]{2,1,0:T(8,128)S(1)}) custom-call(s32[4,128]{1,0:T(4,128)S(1)} %get-tuple-element.14.refs_0_, f32[16,128,128]{2,1,0:T(8,128)S(1)} %get-tuple-element.15.refs_1_, f32[16,128,128]{2,1,0:T(8,128)S(1)} %collective-permute-done.refs_2_, ...), custom_call_target="tpu_custom_call" | custom-call | tf_op jit(solution)/shard_map/depend_level/pallas_call | solution.py:356
  42.5 9.2 %all_to_all.28.refs_5_ = f32[16,8,128]{2,1,0:T(8,128)S(1)} all-to-all(f32[16,8,128]{2,1,0:T(8,128)S(1)} %get-tuple-element.19), channel_id=1, replica_groups=mesh['groups'=2,'chip'=2,'core'=2,'col'=4] {'chip','core','col'}, dimensions={0} | all-to-all | bytes 131072 | tf_op jit(solution)/shard_map/all_to_all | solution.py:391
  51.7 1.7 %depend_level.3 = (f32[8,1,128]{2,1,0:T(1,128)S(1)}, f32[2,8,128]{2,1,0:T(8,128)S(1)}) custom-call(s32[4,128]{1,0:T(4,128)S(1)} %get-tuple-element.14.refs_0_, f32[16,128,128]{2,1,0:T(8,128)S(1)} %get-tuple-element.15.refs_1_, f32[16,128,128]{2,1,0:T(8,128)S(1)} %collective-permute-done.refs_2_, f32[8,8,128]{2,1,0:T(8,128)S(1)} %get-tuple-element.17.refs_3_, ...), custom_call_target="tpu_custom_call" | custom-call | tf_op jit(solution)/shard_map/depend_level/pallas_call | solution.py:356
  53.4 7.9 %all_to_all.29.came = f32[8,1,128]{2,1,0:T(1,128)S(1)} all-to-all(f32[8,1,128]{2,1,0:T(1,128)S(1)} %get-tuple-element.20), channel_id=1, replica_groups=mesh['groups'=2,'chip'=2,'core'=2,'col'=4] {'core','col'}, dimensions={0} | all-to-all | bytes 8192 | tf_op jit(solution)/shard_map/all_to_all | solution.py:391
  61.3 0.6 results.1
Async XLA Ops:
  0.6 0.7 %copy-start.2 = (s32[8]{0:T(128)S(1)}, s32[8]{0:T(128)}, u32[]{:S(2)}) copy-start(s32[8]{0:T(128)} %sources.1) | copy-start | bytes 100
  0.6 0.7 %copy-start.1 = (s32[16,2]{0,1:T(2,128)S(1)}, s32[16,2]{0,1:T(2,128)}, u32[]{:S(2)}) copy-start(s32[16,2]{0,1:T(2,128)} %param.5) | copy-start | bytes 388
  1.3 1.2 %copy-start = (f32[16,128,128]{2,1,0:T(8,128)S(1)}, f32[16,128,128]{2,1,0:T(8,128)}, u32[]{:S(2)}) copy-start(f32[16,128,128]{2,1,0:T(8,128)} %tiles.1) | copy-start | bytes 3145732
  3.8 13.9 %collective-permute-start = (f32[16,128,128]{2,1,0:T(8,128)S(1)}, f32[16,128,128]{2,1,0:T(8,128)S(1)}, u32[]{:S(2)}, u32[]{:S(2)}) collective-permute-start(f32[16,128,128]{2,1,0:T(8,128)S(1)} %get-tuple-element.15.refs_1_), channel_id=1, source_target_pairs={{0,4},{4,0},{1,5},{5,1},{2,6},{6,2},{3,7},{7,3},{8,12},{12,8},{9,1... | collective-permute-start | bytes 3145736 | tf_op jit(solution)/shard_map/ppermute | solution.py:395

commit v3 on v2

--- a/solution.py
+++ b/solution.py
@@ -40,8 +40,15 @@
     return dims[2] == dims[0] * dims[1]
 
 
-def position():
-    return lax.axis_index("chip"), lax.axis_index("core"), lax.axis_index("col")
+def position(dims):
+    n_row, n_col, slots, half = dims
+    at = lax.axis_index("device")
+    chip, core = at // (PAIR * n_col), lax.rem(at // n_col, PAIR)
+    return chip, core, lax.rem(at, n_col), half_of(chip, core)
+
+
+def half_of(chip, core):
+    return core ^ (chip & 1)
 
 
 def source_ids(sources, first, half):
@@ -70,7 +77,7 @@
 
 def first_kernel(dims, places, sources, tiles, out, turned, ids, slot_of, lines):
     n_row, n_col, slots, half = dims
-    my_x, my_core, my_col = position()
+    my_x, my_core, my_col, my_half = position(dims)
     my_row = my_x * PAIR + my_core
 
     def clear(at, _):
@@ -81,7 +88,7 @@
         lax.fori_loop(0, n_row * n_col, clear, 0)
     for g in range(slots):
         slot_of[places[0, g] * n_row + places[1, g]] = g
-    ids[...] = source_ids(sources, my_core * half, half)
+    ids[...] = source_ids(sources, my_half * half, half)
     lines[...] = jnp.zeros(lines.shape, jnp.float32)
     for s in range(PAIR * half):
         vertex = sources[s]
@@ -101,7 +108,7 @@
 
     for chip in range(n_row // PAIR):
         for core in range(PAIR):
-            line = lines[chip, core]
+            line = lines[chip, half_of(chip, core)]
             line = jnp.where(line > 0, line, far_value)
             for col in range(n_col):
                 out[(chip * PAIR + core) * n_col + col] = line
@@ -183,7 +190,7 @@
     places, refs = refs[:n_places], refs[n_places:]
     source_rows, tiles, refs = refs[0], refs[1 : 1 + PAIR], refs[1 + PAIR :]
     came, out, near, found, table, filled = refs
-    my_x, my_core, my_col = position()
+    my_x, my_core, my_col, my_half = position(dims)
     ids = source_rows[...]
     list_slots(dims, places, table, filled)
     for r in range(n_col):
@@ -267,7 +274,7 @@
         came, out, near, low, lower, acc, table, filled = refs
     else:
         near, low, came, out, state, lower, acc, table, filled = refs
-    my_x, my_core, my_col = position()
+    my_x, my_core, my_col, my_half = position(dims)
     ids = source_rows[...]
     list_slots(dims, places, table, filled)
     if first:
@@ -292,13 +299,13 @@
     else:
         other = came[(PAIR * my_x + 1 - my_core) * n_col + my_col]
         for core in range(PAIR):
-            block = jnp.where(my_core == core, near[my_col], other)
+            block = jnp.where(my_half == core, near[my_col], other)
             dist = block[:half]
             rows = pl.ds(core * half, half)
             state[0, rows, :] = jnp.where(dist < 0.5 * far_value, dist, -1.0)
             state[1, rows, :] = block[half:]
         for chip in range(chips):
-            line = (PAIR * chip + my_core) * n_col
+            line = (PAIR * chip + half_of(chip, my_half)) * n_col
             parts = [came[line + col] for col in range(n_col)]
             total = functools.reduce(jnp.add, parts)
             for h in range(PAIR):
@@ -335,12 +342,12 @@
             else:
                 sums = jnp.sum(acc[(my_core ^ k) * n_col + r], axis=1)
                 for chip in range(chips):
-                    line = (PAIR * chip + my_core) * n_col
+                    line = (PAIR * chip + half_of(chip, my_half)) * n_col
                     out[line + r, pl.ds(k * half, half), :] = sums
     if not last:
         for chip in range(chips):
             for r in range(n_col):
-                out[(PAIR * chip + 1 - my_core) * n_col + r] = near[n_col + my_col]
+                out[(PAIR * chip + 1 - half_of(chip, my_half)) * n_col + r] = near[n_col + my_col]
 
 
 def depend_level(dims, first, last, places, ids, tiles, bands, came):
@@ -387,48 +394,61 @@
     )(came, state)
 
 
-def all_to_all(value, axes):
-    return lax.all_to_all(value, axes, split_axis=0, concat_axis=0, tiled=True)
-
-
-def swap_core(value):
-    return lax.ppermute(value, "core", [(0, 1), (1, 0)])
-
-
-def per_device(tiles, tile_index, tile_count, sources):
+def all_to_all(value, groups=None):
+    return lax.all_to_all(
+        value, "device", split_axis=0, concat_axis=0, axis_index_groups=groups, tiled=True
+    )
+
+
+def per_device(n_row, n_col, tiles, tile_index, tile_count, sources):
     slots = tiles.shape[0]
     rows = sources.shape[0]
-    dims = (lax.axis_size("chip") * PAIR, lax.axis_size("col"), slots, rows // PAIR)
+    dims = (n_row, n_col, slots, rows // PAIR)
     own_places = tile_index.T
-    line = ("col", "chip")
-
-    everyone = ("chip", "core", "col")
+    chips, cols = range(n_row // PAIR), range(n_col)
+    device = lambda chip, core, col: (PAIR * chip + core) * n_col + col
+    lines = [
+        [device(chip, half_of(chip, part), col) for col in cols for chip in chips]
+        for part in range(PAIR)
+    ]
+    columns = [[device(chip, core, col) for core in range(PAIR) for col in cols] for chip in chips]
+    swaps = [
+        (device(chip, core, col), device(chip, 1 - core, col))
+        for chip in chips
+        for core in range(PAIR)
+        for col in cols
+    ]
+
+    def swap_core(value):
+        return lax.ppermute(value, "device", swaps)
 
     firsts, turned, ids = first_level(dims, own_places, sources, tiles)
     both = [turned, swap_core(turned)]
     places = [] if is_dense(dims) else [own_places, swap_core(own_places)]
-    came = all_to_all(firsts, everyone)
+    came = all_to_all(firsts)
     for level_no in range(1, LEVELS):
         whole = level_no == LEVELS - 1
         outs = relax_level(dims, level_no > 1, whole, places, ids, both, came)
-        came = all_to_all(outs, line)
+        came = all_to_all(outs, lines)
     sums, *bands = depend_level(dims, True, False, places, ids, both, [], came)
     for back_no in range(1, BACK):
         last = back_no == BACK - 1
-        came = all_to_all(sums, everyone)
+        came = all_to_all(sums)
         sums, state = depend_level(dims, False, last, places, ids, both, bands, came)
-    shown, paths, centrality = results(dims, all_to_all(sums, ("core", "col")), state)
+    shown, paths, centrality = results(dims, all_to_all(sums, columns), state)
     return shown, paths, centrality.reshape(LANES)
 
 
 def solution(mesh):
-    groups, rows, cols = mesh.devices.shape
-    pairs = mesh.devices.reshape(groups, rows // PAIR, PAIR, cols)
-    paired = jax.sharding.Mesh(pairs, ("groups", "chip", "core", "col"))
-    vertices = ("chip", "core", "col")
-    everywhere = ("groups",) + vertices
+    groups, n_row, n_col = mesh.devices.shape
+    flat = jax.sharding.Mesh(mesh.devices.reshape(groups, n_row * n_col), ("groups", "device"))
+    everywhere = ("groups", "device")
     in_specs = (P(everywhere, None, None), P(everywhere, None), P(everywhere), P("groups"))
-    out_specs = (P("groups", vertices), P("groups", vertices), P(everywhere))
+    out_specs = (P("groups", "device"), P("groups", "device"), P(everywhere))
     return jax.shard_map(
-        per_device, mesh=paired, in_specs=in_specs, out_specs=out_specs, check_vma=False
+        functools.partial(per_device, n_row, n_col),
+        mesh=flat,
+        in_specs=in_specs,
+        out_specs=out_specs,
+        check_vma=False,
     )

time: 62.3 us -> 62.4 us (level)
  no operation moved by 1% of the time
where the time goes in v3:
time: 62.4 us; the launch traced here: 62 us
  blocking collectives  49.7 us (80%)
  Pallas kernels  9.32 us (15%)
  local copies, waits for them, and re-layouts  1.9 us (3%)
  between operations  0.68 us (1%)
    all_to_all x5, blocking collectives, all_to_all(): lax.all_to_all(value, 'device', split_axis=0, concat_axis=0, axis_index_g...  49.7 us
    pallas_call x2, Pallas kernels, relax_level(): pl.pallas_call(functools.partial(relax_kernel, dims, counted, whole), out...  4.08 us
    pallas_call x2, Pallas kernels, depend_level(): pl.pallas_call(functools.partial(depend_kernel, dims, first, last), out_s...  3.44 us
    unnamed x6, local copies, waits for them, and re-layouts  1.9 us
  transfers between devices with their start and end apart: 1, of which 0 were waited for; matrix products, arithmetic and copies ran while one was open for 0% of the time, Pallas kernels for 0%

profile of v3, /device:TPU:0, one launch (start us, length us, event | category | flops | bytes accessed | tf_op | source)
XLA Modules:
  0.0 62.0 jit_solution(16419190959407281355)
XLA Ops:
  0.6 0.0 copy-start.2
  0.6 0.0 copy-start.1
  0.7 0.6 %copy-done.2 = s32[8]{0:T(128)S(1)} copy-done((s32[8]{0:T(128)S(1)}, s32[8]{0:T(128)}, u32[]{:S(2)}) %copy-start.2) | copy-done | bytes 56
  1.3 0.0 copy-done.1
  1.3 0.0 copy-start
  1.3 1.2 %copy-done = f32[16,128,128]{2,1,0:T(8,128)S(1)} copy-done((f32[16,128,128]{2,1,0:T(8,128)S(1)}, f32[16,128,128]{2,1,0:T(8,128)}, u32[]{:S(2)}) %copy-start) | copy-done | bytes 1048600
  2.6 1.2 %first_level.1 = (f32[16,8,128]{2,1,0:T(8,128)S(1)}, f32[16,128,128]{2,1,0:T(8,128)S(1)}, s32[4,128]{1,0:T(4,128)S(1)}) custom-call(s32[2,16]{1,0:T(2,128)S(1)} %bitcast.2, s32[8]{0:T(128)S(1)} %copy-done.2, f32[16,128,128]{2,1,0:T(8,128)S(1)} %copy-done), custom_call_target="tpu_custom_call" | custom-call | tf_op jit(solution)/shard_map/first_level/pallas_call | solution.py:122
  3.8 0.4 collective-permute-start
  4.2 13.4 %all_to_all.25.refs_3_ = f32[16,8,128]{2,1,0:T(8,128)S(1)} all-to-all(f32[16,8,128]{2,1,0:T(8,128)S(1)} %get-tuple-element.16), channel_id=1, replica_groups=mesh['groups'=2,'row'=4,'col'=4] {'row','col'}, dimensions={0} | all-to-all | bytes 131072 | tf_op jit(solution)/shard_map/all_to_all | solution.py:398
  17.6 0.0 collective-permute-done.refs_2_
  17.6 2.0 %relax_level.2 = f32[8,2,8,128]{3,2,1,0:T(8,128)S(1)} custom-call(s32[4,128]{1,0:T(4,128)S(1)} %get-tuple-element.14.refs_0_, f32[16,128,128]{2,1,0:T(8,128)S(1)} %get-tuple-element.15.refs_1_, f32[16,128,128]{2,1,0:T(8,128)S(1)} %collective-permute-done.refs_2_, f32[16,8,128]{2,1,0:T(8,128)S(1)} %all_to_all.25.refs_3_), custom_call_target="tpu_custom_call" | custom-call | tf_op jit(solution)/shard_map/relax_level/pallas_call | solution.py:252
  19.7 8.8 %all_to_all.26.refs_3_ = f32[8,2,8,128]{3,2,1,0:T(8,128)S(1)} all-to-all(f32[8,2,8,128]{3,2,1,0:T(8,128)S(1)} %relax_level.2), channel_id=1, replica_groups={{0,12,1,13,2,14,3,15},{4,8,5,9,6,10,7,11},{16,28,17,29,18,30,19,31},{20..., dimensions={0} | all-to-all | bytes 131072 | tf_op jit(solution)/shard_map/all_to_all | solution.py:398
  28.5 2.0 %relax_level.3 = f32[8,4,8,128]{3,2,1,0:T(8,128)S(1)} custom-call(s32[4,128]{1,0:T(4,128)S(1)} %get-tuple-element.14.refs_0_, f32[16,128,128]{2,1,0:T(8,128)S(1)} %get-tuple-element.15.refs_1_, f32[16,128,128]{2,1,0:T(8,128)S(1)} %collective-permute-done.refs_2_, f32[8,2,8,128]{3,2,1,0:T(8,128)S(1)} %all_to_all.26.refs_3_), custom_call_target="tpu_custom_call" | custom-call | tf_op jit(solution)/shard_map/relax_level/pallas_call | solution.py:252
  30.6 9.7 %all_to_all.27.refs_3_ = f32[8,4,8,128]{3,2,1,0:T(8,128)S(1)} all-to-all(f32[8,4,8,128]{3,2,1,0:T(8,128)S(1)} %relax_level.3), channel_id=1, replica_groups={{0,12,1,13,2,14,3,15},{4,8,5,9,6,10,7,11},{16,28,17,29,18,30,19,31},{20..., dimensions={0} | all-to-all | bytes 262144 | tf_op jit(solution)/shard_map/all_to_all | solution.py:398
  40.3 1.7 %depend_level.2 = (f32[16,8,128]{2,1,0:T(8,128)S(1)}, f32[8,8,128]{2,1,0:T(8,128)S(1)}, f32[4,8,128]{2,1,0:T(8,128)S(1)}) custom-call(s32[4,128]{1,0:T(4,128)S(1)} %get-tuple-element.14.refs_0_, f32[16,128,128]{2,1,0:T(8,128)S(1)} %get-tuple-element.15.refs_1_, f32[16,128,128]{2,1,0:T(8,128)S(1)} %collective-permute-done.refs_2_, ...), custom_call_target="tpu_custom_call" | custom-call | tf_op jit(solution)/shard_map/depend_level/pallas_call | solution.py:363
  42.0 9.7 %all_to_all.28.refs_5_ = f32[16,8,128]{2,1,0:T(8,128)S(1)} all-to-all(f32[16,8,128]{2,1,0:T(8,128)S(1)} %get-tuple-element.19), channel_id=1, replica_groups=mesh['groups'=2,'row'=4,'col'=4] {'row','col'}, dimensions={0} | all-to-all | bytes 131072 | tf_op jit(solution)/shard_map/all_to_all | solution.py:398
  51.8 1.7 %depend_level.3 = (f32[8,1,128]{2,1,0:T(1,128)S(1)}, f32[2,8,128]{2,1,0:T(8,128)S(1)}) custom-call(s32[4,128]{1,0:T(4,128)S(1)} %get-tuple-element.14.refs_0_, f32[16,128,128]{2,1,0:T(8,128)S(1)} %get-tuple-element.15.refs_1_, f32[16,128,128]{2,1,0:T(8,128)S(1)} %collective-permute-done.refs_2_, f32[8,8,128]{2,1,0:T(8,128)S(1)} %get-tuple-element.17.refs_3_, ...), custom_call_target="tpu_custom_call" | custom-call | tf_op jit(solution)/shard_map/depend_level/pallas_call | solution.py:363
  53.5 7.9 %all_to_all.29.came = f32[8,1,128]{2,1,0:T(1,128)S(1)} all-to-all(f32[8,1,128]{2,1,0:T(1,128)S(1)} %get-tuple-element.20), channel_id=1, replica_groups={{0,1,2,3,4,5,6,7},{8,9,10,11,12,13,14,15},{16,17,18,19,20,21,22,23},{24..., dimensions={0} | all-to-all | bytes 8192 | tf_op jit(solution)/shard_map/all_to_all | solution.py:398
  61.4 0.6 results.1
Async XLA Ops:
  0.6 0.7 %copy-start.2 = (s32[8]{0:T(128)S(1)}, s32[8]{0:T(128)}, u32[]{:S(2)}) copy-start(s32[8]{0:T(128)} %sources.1) | copy-start | bytes 100
  0.6 0.7 %copy-start.1 = (s32[16,2]{0,1:T(2,128)S(1)}, s32[16,2]{0,1:T(2,128)}, u32[]{:S(2)}) copy-start(s32[16,2]{0,1:T(2,128)} %param.5) | copy-start | bytes 388
  1.3 1.2 %copy-start = (f32[16,128,128]{2,1,0:T(8,128)S(1)}, f32[16,128,128]{2,1,0:T(8,128)}, u32[]{:S(2)}) copy-start(f32[16,128,128]{2,1,0:T(8,128)} %tiles.1) | copy-start | bytes 3145732
  3.8 13.9 %collective-permute-start = (f32[16,128,128]{2,1,0:T(8,128)S(1)}, f32[16,128,128]{2,1,0:T(8,128)S(1)}, u32[]{:S(2)}, u32[]{:S(2)}) collective-permute-start(f32[16,128,128]{2,1,0:T(8,128)S(1)} %get-tuple-element.15.refs_1_), channel_id=1, source_target_pairs={{0,4},{1,5},{2,6},{3,7},{4,0},{5,1},{6,2},{7,3},{8,12},{9,13},{10,... | collective-permute-start | bytes 3145736 | tf_op jit(solution)/shard_map/ppermute | solution.py:423

commit v4 on v2

--- a/solution.py
+++ b/solution.py
@@ -28,6 +28,10 @@
     return pl.BlockSpec(memory_space=pltpu.SMEM)
 
 
+def in_hbm():
+    return pl.BlockSpec(memory_space=pltpu.HBM)
+
+
 def piece(*shape):
     return jax.ShapeDtypeStruct(shape, jnp.float32)
 
@@ -68,10 +72,25 @@
     return best, total
 
 
-def first_kernel(dims, places, sources, tiles, out, turned, ids, slot_of, lines):
-    n_row, n_col, slots, half = dims
+def first_kernel(dims, *refs):
+    n_row, n_col, slots, half = dims
+    places_in, sources_in, tiles_in, out, turned, ids = refs[:6]
+    places, sources, slot_of, tiles, lines, sems = refs[6:]
     my_x, my_core, my_col = position()
     my_row = my_x * PAIR + my_core
+    parts = sems.shape[0] - 2
+    size = slots // parts
+    given = [
+        pltpu.make_async_copy(places_in, places, sems.at[parts]),
+        pltpu.make_async_copy(sources_in, sources, sems.at[parts + 1]),
+    ]
+    fetch = []
+    for part in range(parts):
+        span = pl.ds(part * size, size)
+        fetch.append(pltpu.make_async_copy(tiles_in.at[span], tiles.at[span], sems.at[part]))
+    for copy in given + fetch:
+        copy.start()
+    lines[...] = jnp.zeros(lines.shape, jnp.float32)
 
     def clear(at, _):
         slot_of[at] = -1
@@ -79,10 +98,17 @@
 
     if not is_dense(dims):
         lax.fori_loop(0, n_row * n_col, clear, 0)
+    for copy in given:
+        copy.wait()
     for g in range(slots):
         slot_of[places[0, g] * n_row + places[1, g]] = g
     ids[...] = source_ids(sources, my_core * half, half)
-    lines[...] = jnp.zeros(lines.shape, jnp.float32)
+    for part in range(parts):
+        fetch[part].wait()
+        for g in range(part * size, part * size + size):
+            at = places[0, g] * n_row + places[1, g] if is_dense(dims) else g
+            raw = tiles[g]
+            turned[at] = jnp.where(raw > 0, raw, no_edge).T
     for s in range(PAIR * half):
         vertex = sources[s]
         block, place = vertex // LANES, lax.rem(vertex, LANES)
@@ -105,13 +131,12 @@
             line = jnp.where(line > 0, line, far_value)
             for col in range(n_col):
                 out[(chip * PAIR + core) * n_col + col] = line
-    for at in range(slots):
-        raw = tiles[slot_of[at] if is_dense(dims) else at]
-        turned[at] = jnp.where(raw > 0, raw, no_edge).T
 
 
 def first_level(dims, places, sources, tiles):
     n_row, n_col, slots, half = dims
+    parts = 4 if slots % 4 == 0 else 1
+    inputs = [pltpu.with_memory_space_constraint(x, pltpu.HBM) for x in (places, sources, tiles)]
     return pl.pallas_call(
         functools.partial(first_kernel, dims),
         out_shape=[
@@ -119,15 +144,19 @@
             piece(*tiles.shape),
             jax.ShapeDtypeStruct((half, LANES), jnp.int32),
         ],
-        in_specs=[in_smem(), in_smem(), in_vmem()],
+        in_specs=[in_hbm()] * 3,
         out_specs=[in_vmem()] * 3,
         scratch_shapes=[
+            pltpu.SMEM(places.shape, jnp.int32),
+            pltpu.SMEM(sources.shape, jnp.int32),
             pltpu.SMEM((n_row * n_col,), jnp.int32),
+            pltpu.VMEM(tiles.shape, jnp.float32),
             pltpu.VMEM((n_row // PAIR, PAIR, PAIR * half, LANES), jnp.float32),
+            pltpu.SemaphoreType.DMA((parts + 2,)),
         ],
         compiler_params=params(large_limit),
         name="first_level",
-    )(places, sources, tiles)
+    )(*inputs)
 
 
 def list_slots(dims, places, table, filled):

time: 62.3 us -> 60.9 us (0.978)
  local copies, waits for them, and re-layouts: 1.9 us -> 0 us
    unnamed x6 -> x0, local copies, waits for them, and re-layouts: 1.9 us -> none
where the time goes in v4:
time: 60.9 us; the launch traced here: 60.6 us
  blocking collectives  49.5 us (81%)
  Pallas kernels  9.87 us (16%)
  between operations  0.66 us (1%)
    all_to_all x5, blocking collectives, all_to_all(): return lax.all_to_all(value, axes, split_axis=0, concat_axis=0, tiled=True)  49.5 us
    pallas_call x2, Pallas kernels, relax_level(): pl.pallas_call(functools.partial(relax_kernel, dims, counted, whole), out...  4.08 us
    pallas_call x2, Pallas kernels, depend_level(): pl.pallas_call(functools.partial(depend_kernel, dims, first, last), out_s...  3.43 us
    pallas_call x1, Pallas kernels, first_level(): pl.pallas_call(functools.partial(first_kernel, dims), out_shape=[piece(n_...  1.76 us
  transfers between devices with their start and end apart: 1, of which 0 were waited for; matrix products, arithmetic and copies ran while one was open for 0% of the time, Pallas kernels for 0%

profile of v4, /device:TPU:0, one launch (start us, length us, event | category | flops | bytes accessed | tf_op | source)
XLA Modules:
  0.0 60.6 jit_solution(9484321388647481010)
XLA Ops:
  0.6 1.8 %first_level.1 = (f32[16,8,128]{2,1,0:T(8,128)S(1)}, f32[16,128,128]{2,1,0:T(8,128)S(1)}, s32[4,128]{1,0:T(4,128)S(1)}) custom-call(s32[2,16]{1,0:T(2,128)} %bitcast.2, s32[8]{0:T(128)} %refs_1_.1, f32[16,128,128]{2,1,0:T(8,128)} %refs_2_.1), custom_call_target="tpu_custom_call" | custom-call | tf_op jit(solution)/shard_map/first_level/pallas_call | solution.py:140
  2.4 0.5 collective-permute-start
  2.9 13.4 %all_to_all.25.refs_3_ = f32[16,8,128]{2,1,0:T(8,128)S(1)} all-to-all(f32[16,8,128]{2,1,0:T(8,128)S(1)} %get-tuple-element.16), channel_id=1, replica_groups=mesh['groups'=2,'chip'=2,'core'=2,'col'=4] {'chip','core','col'}, dimensions={0} | all-to-all | bytes 131072 | tf_op jit(solution)/shard_map/all_to_all | solution.py:420
  16.3 0.0 collective-permute-done.refs_2_
  16.3 2.0 %relax_level.2 = f32[8,2,8,128]{3,2,1,0:T(8,128)S(1)} custom-call(s32[4,128]{1,0:T(4,128)S(1)} %get-tuple-element.14.refs_0_, f32[16,128,128]{2,1,0:T(8,128)S(1)} %get-tuple-element.15.refs_1_, f32[16,128,128]{2,1,0:T(8,128)S(1)} %collective-permute-done.refs_2_, f32[16,8,128]{2,1,0:T(8,128)S(1)} %all_to_all.25.refs_3_), custom_call_target="tpu_custom_call" | custom-call | tf_op jit(solution)/shard_map/relax_level/pallas_call | solution.py:274
  18.4 9.3 %all_to_all.26.refs_3_ = f32[8,2,8,128]{3,2,1,0:T(8,128)S(1)} all-to-all(f32[8,2,8,128]{3,2,1,0:T(8,128)S(1)} %relax_level.2), channel_id=1, replica_groups=mesh['groups'=2,'chip'=2,'core'=2,'col'=4] {'col','chip'}, dimensions={0} | all-to-all | bytes 131072 | tf_op jit(solution)/shard_map/all_to_all | solution.py:420
  27.7 2.0 %relax_level.3 = f32[8,4,8,128]{3,2,1,0:T(8,128)S(1)} custom-call(s32[4,128]{1,0:T(4,128)S(1)} %get-tuple-element.14.refs_0_, f32[16,128,128]{2,1,0:T(8,128)S(1)} %get-tuple-element.15.refs_1_, f32[16,128,128]{2,1,0:T(8,128)S(1)} %collective-permute-done.refs_2_, f32[8,2,8,128]{3,2,1,0:T(8,128)S(1)} %all_to_all.26.refs_3_), custom_call_target="tpu_custom_call" | custom-call | tf_op jit(solution)/shard_map/relax_level/pallas_call | solution.py:274
  29.7 9.7 %all_to_all.27.refs_3_ = f32[8,4,8,128]{3,2,1,0:T(8,128)S(1)} all-to-all(f32[8,4,8,128]{3,2,1,0:T(8,128)S(1)} %relax_level.3), channel_id=1, replica_groups=mesh['groups'=2,'chip'=2,'core'=2,'col'=4] {'col','chip'}, dimensions={0} | all-to-all | bytes 262144 | tf_op jit(solution)/shard_map/all_to_all | solution.py:420
  39.4 1.7 %depend_level.2 = (f32[16,8,128]{2,1,0:T(8,128)S(1)}, f32[8,8,128]{2,1,0:T(8,128)S(1)}, f32[4,8,128]{2,1,0:T(8,128)S(1)}) custom-call(s32[4,128]{1,0:T(4,128)S(1)} %get-tuple-element.14.refs_0_, f32[16,128,128]{2,1,0:T(8,128)S(1)} %get-tuple-element.15.refs_1_, f32[16,128,128]{2,1,0:T(8,128)S(1)} %collective-permute-done.refs_2_, ...), custom_call_target="tpu_custom_call" | custom-call | tf_op jit(solution)/shard_map/depend_level/pallas_call | solution.py:385
  41.2 9.2 %all_to_all.28.refs_5_ = f32[16,8,128]{2,1,0:T(8,128)S(1)} all-to-all(f32[16,8,128]{2,1,0:T(8,128)S(1)} %get-tuple-element.19), channel_id=1, replica_groups=mesh['groups'=2,'chip'=2,'core'=2,'col'=4] {'chip','core','col'}, dimensions={0} | all-to-all | bytes 131072 | tf_op jit(solution)/shard_map/all_to_all | solution.py:420
  50.4 1.7 %depend_level.3 = (f32[8,1,128]{2,1,0:T(1,128)S(1)}, f32[2,8,128]{2,1,0:T(8,128)S(1)}) custom-call(s32[4,128]{1,0:T(4,128)S(1)} %get-tuple-element.14.refs_0_, f32[16,128,128]{2,1,0:T(8,128)S(1)} %get-tuple-element.15.refs_1_, f32[16,128,128]{2,1,0:T(8,128)S(1)} %collective-permute-done.refs_2_, f32[8,8,128]{2,1,0:T(8,128)S(1)} %get-tuple-element.17.refs_3_, ...), custom_call_target="tpu_custom_call" | custom-call | tf_op jit(solution)/shard_map/depend_level/pallas_call | solution.py:385
  52.1 7.9 %all_to_all.29.came = f32[8,1,128]{2,1,0:T(1,128)S(1)} all-to-all(f32[8,1,128]{2,1,0:T(1,128)S(1)} %get-tuple-element.20), channel_id=1, replica_groups=mesh['groups'=2,'chip'=2,'core'=2,'col'=4] {'core','col'}, dimensions={0} | all-to-all | bytes 8192 | tf_op jit(solution)/shard_map/all_to_all | solution.py:420
  60.0 0.6 results.1
Async XLA Ops:
  2.4 13.9 %collective-permute-start = (f32[16,128,128]{2,1,0:T(8,128)S(1)}, f32[16,128,128]{2,1,0:T(8,128)S(1)}, u32[]{:S(2)}, u32[]{:S(2)}) collective-permute-start(f32[16,128,128]{2,1,0:T(8,128)S(1)} %get-tuple-element.15.refs_1_), channel_id=1, source_target_pairs={{0,4},{4,0},{1,5},{5,1},{2,6},{6,2},{3,7},{7,3},{8,12},{12,8},{9,1... | collective-permute-start | bytes 3145736 | tf_op jit(solution)/shard_map/ppermute | solution.py:424

commit v5 on v4

--- a/solution.py
+++ b/solution.py
@@ -18,6 +18,7 @@
 no_edge = 2000000.0
 large_limit = 8 * 1024 * 1024
 small_limit = 2 * 1024 * 1024
+terms_limit = 20 * 1024 * 1024
 
 
 def in_vmem():
@@ -291,11 +292,12 @@
     chips = n_row // PAIR
     n_places = 0 if is_dense(dims) else PAIR
     places, refs = refs[:n_places], refs[n_places:]
-    source_rows, tiles, refs = refs[0], refs[1 : 1 + PAIR], refs[1 + PAIR :]
+    source_rows, refs = refs[0], refs[1:]
     if first:
-        came, out, near, low, lower, acc, table, filled = refs
+        tiles, refs = refs[:PAIR], refs[PAIR:]
+        came, out, near, low, terms, acc, table, filled = refs
     else:
-        near, low, came, out, state, lower, acc, table, filled = refs
+        near, low, terms, came, out, state, acc, table, filled = refs
     my_x, my_core, my_col = position()
     ids = source_rows[...]
     list_slots(dims, places, table, filled)
@@ -316,8 +318,6 @@
             dist, count = settle(*found, at_source)
             low[c, :half, :] = dist
             low[c, half:, :] = count
-            lower[c, :half, :] = dist
-            lower[c, half:, :] = jnp.where(count > 0.5, 1.0 / jnp.maximum(count, 1.0), 0.0)
     else:
         other = came[(PAIR * my_x + 1 - my_core) * n_col + my_col]
         for core in range(PAIR):
@@ -326,34 +326,48 @@
             rows = pl.ds(core * half, half)
             state[0, rows, :] = jnp.where(dist < 0.5 * far_value, dist, -1.0)
             state[1, rows, :] = block[half:]
-        for chip in range(chips):
-            line = (PAIR * chip + my_core) * n_col
-            parts = [came[line + col] for col in range(n_col)]
-            total = functools.reduce(jnp.add, parts)
-            for h in range(PAIR):
-                c = PAIR * chip + h
-                count = low[c, half:, :]
-                coef = (1.0 + count * total[h * half : h * half + half]) / jnp.maximum(count, 1.0)
-                lower[c, :half, :] = low[c, :half, :]
-                lower[c, half:, :] = jnp.where(count > 0.5, coef, 0.0)
     acc[...] = jnp.zeros(acc.shape, jnp.float32)
 
-    def column(c, _):
-        turned = lower[c].T
+    def add_terms(b, s, part):
+        acc[b, s] += jnp.sum(part.reshape(LANES // SUB, SUB, LANES), axis=0)
+
+    def select(c, _):
+        count = low[c, half:, :]
+        share = jnp.where(count > 0.5, 1.0 / jnp.maximum(count, 1.0), 0.0)
+        turned = jnp.concatenate([low[c, :half, :], share], axis=0).T
         for s in range(half):
             dist = jnp.broadcast_to(turned[:, s : s + 1], (LANES, LANES))
             coef = jnp.broadcast_to(turned[:, half + s : half + s + 1], (LANES, LANES))
 
             def step(k, g, b, carry):
                 hit = tiles[k][g] + near[b, pl.ds(s, 1), :] == dist
-                terms = jnp.where(hit, coef, 0.0).reshape(LANES // SUB, SUB, LANES)
-                acc[b, s] += jnp.sum(terms, axis=0)
+                part = jnp.where(hit, coef, 0.0)
+                terms[(k * slots + g) * half + s] = part
+                add_terms(b, s, part)
                 return carry
 
             over_slots(dims, places, table, filled, c, step, 0)
         return 0
 
-    lax.fori_loop(0, n_row, column, 0, unroll=UNROLL)
+    def scale(c, _):
+        line = (c // PAIR * PAIR + my_core) * n_col
+        rows = pl.ds(c % PAIR * half, half)
+        total = functools.reduce(jnp.add, [came[line + col, rows, :] for col in range(n_col)])
+        turned = (1.0 + low[c, half:, :] * total).T
+        for s in range(half):
+            factor = jnp.broadcast_to(turned[:, s : s + 1], (LANES, LANES))
+
+            def step(k, g, b, carry):
+                add_terms(b, s, terms[(k * slots + g) * half + s] * factor)
+                return carry
+
+            over_slots(dims, places, table, filled, c, step, 0)
+
+    if first:
+        lax.fori_loop(0, n_row, select, 0, unroll=UNROLL)
+    else:
+        for c in range(n_row):
+            scale(c, 0)
     for r in range(n_col):
         for k in range(PAIR):
             if last:
@@ -379,22 +393,24 @@
     else:
         out_shape = [piece(n_row * n_col, PAIR * half, LANES)]
     if first:
-        out_shape += [piece(PAIR * n_col, 2 * half, LANES), piece(n_row, 2 * half, LANES)]
+        out_shape += [
+            piece(PAIR * n_col, 2 * half, LANES),
+            piece(n_row, 2 * half, LANES),
+            piece(PAIR * slots * half, LANES, LANES),
+        ]
     else:
         out_shape += [piece(2, PAIR * half, LANES)]
+    vectors = [ids, *(tiles if first else []), *bands, came]
     return pl.pallas_call(
         functools.partial(depend_kernel, dims, first, last),
         out_shape=out_shape,
-        in_specs=[in_smem()] * len(places) + [in_vmem()] * (PAIR + len(bands) + 2),
+        in_specs=[in_smem()] * len(places) + [in_vmem()] * len(vectors),
         out_specs=[in_vmem()] * len(out_shape),
-        scratch_shapes=[
-            pltpu.VMEM((n_row, 2 * half, LANES), jnp.float32),
-            pltpu.VMEM((PAIR * n_col, half, SUB, LANES), jnp.float32),
-        ]
+        scratch_shapes=[pltpu.VMEM((PAIR * n_col, half, SUB, LANES), jnp.float32)]
         + slot_scratch(dims),
-        compiler_params=params(large_limit),
+        compiler_params=params(terms_limit),
         name="depend_level",
-    )(*places, ids, *tiles, *bands, came)
+    )(*places, *vectors)
 
 
 def result_kernel(rows, came, state, shown, paths, centrality):

time: 60.9 us -> 60.3 us (level)
    pallas_call x2, Pallas kernels: 3.43 us -> 2.82 us  [depend_level(): pl.pallas_call(functools.partial(depend_kernel, dims, first, last), out_s...]
where the time goes in v5:
time: 60.3 us; the launch traced here: 60 us
  blocking collectives  49.5 us (82%)
  Pallas kernels  9.29 us (15%)
  between operations  0.66 us (1%)
    all_to_all x5, blocking collectives, all_to_all(): return lax.all_to_all(value, axes, split_axis=0, concat_axis=0, tiled=True)  49.5 us
    pallas_call x2, Pallas kernels, relax_level(): pl.pallas_call(functools.partial(relax_kernel, dims, counted, whole), out...  4.08 us
    pallas_call x2, Pallas kernels, depend_level(): pl.pallas_call(functools.partial(depend_kernel, dims, first, last), out_s...  2.82 us
    pallas_call x1, Pallas kernels, first_level(): pl.pallas_call(functools.partial(first_kernel, dims), out_shape=[piece(n_...  1.79 us
  transfers between devices with their start and end apart: 1, of which 0 were waited for; matrix products, arithmetic and copies ran while one was open for 0% of the time, Pallas kernels for 0%

profile of v5, /device:TPU:0, one launch (start us, length us, event | category | flops | bytes accessed | tf_op | source)
XLA Modules:
  0.0 60.0 jit_solution(13316634729870585435)
XLA Ops:
  0.6 1.8 %first_level.1 = (f32[16,8,128]{2,1,0:T(8,128)S(1)}, f32[16,128,128]{2,1,0:T(8,128)S(1)}, s32[4,128]{1,0:T(4,128)S(1)}) custom-call(s32[2,16]{1,0:T(2,128)} %bitcast.2, s32[8]{0:T(128)} %refs_1_.1, f32[16,128,128]{2,1,0:T(8,128)} %refs_2_.1), custom_call_target="tpu_custom_call" | custom-call | tf_op jit(solution)/shard_map/first_level/pallas_call | solution.py:141
  2.4 0.5 collective-permute-start
  2.9 13.4 %all_to_all.25.refs_3_ = f32[16,8,128]{2,1,0:T(8,128)S(1)} all-to-all(f32[16,8,128]{2,1,0:T(8,128)S(1)} %get-tuple-element.17), channel_id=1, replica_groups=mesh['groups'=2,'chip'=2,'core'=2,'col'=4] {'chip','core','col'}, dimensions={0} | all-to-all | bytes 131072 | tf_op jit(solution)/shard_map/all_to_all | solution.py:436
  16.3 0.0 collective-permute-done.refs_2_
  16.3 2.0 %relax_level.2 = f32[8,2,8,128]{3,2,1,0:T(8,128)S(1)} custom-call(s32[4,128]{1,0:T(4,128)S(1)} %get-tuple-element.15.refs_0_, f32[16,128,128]{2,1,0:T(8,128)S(1)} %get-tuple-element.16.refs_1_, f32[16,128,128]{2,1,0:T(8,128)S(1)} %collective-permute-done.refs_2_, f32[16,8,128]{2,1,0:T(8,128)S(1)} %all_to_all.25.refs_3_), custom_call_target="tpu_custom_call" | custom-call | tf_op jit(solution)/shard_map/relax_level/pallas_call | solution.py:275
  18.4 9.3 %all_to_all.26.refs_3_ = f32[8,2,8,128]{3,2,1,0:T(8,128)S(1)} all-to-all(f32[8,2,8,128]{3,2,1,0:T(8,128)S(1)} %relax_level.2), channel_id=1, replica_groups=mesh['groups'=2,'chip'=2,'core'=2,'col'=4] {'col','chip'}, dimensions={0} | all-to-all | bytes 131072 | tf_op jit(solution)/shard_map/all_to_all | solution.py:436
  27.7 2.0 %relax_level.3 = f32[8,4,8,128]{3,2,1,0:T(8,128)S(1)} custom-call(s32[4,128]{1,0:T(4,128)S(1)} %get-tuple-element.15.refs_0_, f32[16,128,128]{2,1,0:T(8,128)S(1)} %get-tuple-element.16.refs_1_, f32[16,128,128]{2,1,0:T(8,128)S(1)} %collective-permute-done.refs_2_, f32[8,2,8,128]{3,2,1,0:T(8,128)S(1)} %all_to_all.26.refs_3_), custom_call_target="tpu_custom_call" | custom-call | tf_op jit(solution)/shard_map/relax_level/pallas_call | solution.py:275
  29.7 9.7 %all_to_all.27.refs_3_ = f32[8,4,8,128]{3,2,1,0:T(8,128)S(1)} all-to-all(f32[8,4,8,128]{3,2,1,0:T(8,128)S(1)} %relax_level.3), channel_id=1, replica_groups=mesh['groups'=2,'chip'=2,'core'=2,'col'=4] {'col','chip'}, dimensions={0} | all-to-all | bytes 262144 | tf_op jit(solution)/shard_map/all_to_all | solution.py:436
  39.4 1.8 %depend_level.2 = (f32[16,8,128]{2,1,0:T(8,128)S(1)}, f32[8,8,128]{2,1,0:T(8,128)S(1)}, f32[4,8,128]{2,1,0:T(8,128)S(1)}, f32[128,128,128]{2,1,0:T(8,128)S(1)}) custom-call(s32[4,128]{1,0:T(4,128)S(1)} %get-tuple-element.15.refs_0_, f32[16,128,128]{2,1,0:T(8,128)S(1)} %get-tuple-element.16.refs_1_, f32[16,128,128]{2,1,0:T(8,128)S(1)} %collective-permute-done.refs_2_, ...), custom_call_target="tpu_custom_call" | custom-call | tf_op jit(solution)/shard_map/depend_level/pallas_call | solution.py:404
  41.3 9.2 %all_to_all.28.refs_4_ = f32[16,8,128]{2,1,0:T(8,128)S(1)} all-to-all(f32[16,8,128]{2,1,0:T(8,128)S(1)} %get-tuple-element.21), channel_id=1, replica_groups=mesh['groups'=2,'chip'=2,'core'=2,'col'=4] {'chip','core','col'}, dimensions={0} | all-to-all | bytes 131072 | tf_op jit(solution)/shard_map/all_to_all | solution.py:436
  50.5 1.0 %depend_level.3 = (f32[8,1,128]{2,1,0:T(1,128)S(1)}, f32[2,8,128]{2,1,0:T(8,128)S(1)}) custom-call(s32[4,128]{1,0:T(4,128)S(1)} %get-tuple-element.15.refs_0_, f32[8,8,128]{2,1,0:T(8,128)S(1)} %get-tuple-element.18.refs_1_, f32[4,8,128]{2,1,0:T(8,128)S(1)} %get-tuple-element.19.refs_2_, f32[128,128,128]{2,1,0:T(8,128)S(1)} %get-tuple-element.20.refs_3_, ...), custom_call_target="tpu_custom_call" | custom-call | tf_op jit(solution)/shard_map/depend_level/pallas_call | solution.py:404
  51.5 7.9 %all_to_all.29.came = f32[8,1,128]{2,1,0:T(1,128)S(1)} all-to-all(f32[8,1,128]{2,1,0:T(1,128)S(1)} %get-tuple-element.22), channel_id=1, replica_groups=mesh['groups'=2,'chip'=2,'core'=2,'col'=4] {'core','col'}, dimensions={0} | all-to-all | bytes 8192 | tf_op jit(solution)/shard_map/all_to_all | solution.py:436
  59.4 0.6 %results.1 = (f32[8,128]{1,0:T(8,128)}, f32[8,128]{1,0:T(8,128)}, f32[1,128]{1,0:T(1,128)}) custom-call(f32[8,1,128]{2,1,0:T(1,128)S(1)} %all_to_all.29.came, f32[2,8,128]{2,1,0:T(8,128)S(1)} %get-tuple-element.23.state), custom_call_target="tpu_custom_call" | custom-call | tf_op jit(solution)/shard_map/results/pallas_call | solution.py:425
Async XLA Ops:
  2.4 13.9 %collective-permute-start = (f32[16,128,128]{2,1,0:T(8,128)S(1)}, f32[16,128,128]{2,1,0:T(8,128)S(1)}, u32[]{:S(2)}, u32[]{:S(2)}) collective-permute-start(f32[16,128,128]{2,1,0:T(8,128)S(1)} %get-tuple-element.16.refs_1_), channel_id=1, source_target_pairs={{0,4},{4,0},{1,5},{5,1},{2,6},{6,2},{3,7},{7,3},{8,12},{12,8},{9,1... | collective-permute-start | bytes 3145736 | tf_op jit(solution)/shard_map/ppermute | solution.py:440

commit v6 on v5

--- a/solution.py
+++ b/solution.py
@@ -232,35 +232,38 @@
             near[k * n_col + r, half:, :] = count
     lane = lax.broadcasted_iota(jnp.int32, (LANES, LANES), 1)
 
-    def column(c, _):
-        def lowest(s):
-            def step(k, g, b, carry):
-                return jnp.minimum(carry, tiles[k][g] + near[b, pl.ds(s, 1), :])
-
-            start = jnp.full((LANES, LANES), far_value, jnp.float32)
-            reached = over_slots(dims, places, table, filled, c, step, start)
-            return jnp.min(reached, axis=1, keepdims=True)
-
-        def tally(s, best):
-            def step(k, g, b, carry):
-                hit = tiles[k][g] + near[b, pl.ds(s, 1), :] == best
-                return carry + jnp.where(hit, near[b, pl.ds(half + s, 1), :], 0.0)
-
-            start = jnp.zeros((LANES, LANES), jnp.float32)
-            counts = over_slots(dims, places, table, filled, c, step, start)
-            return jnp.sum(counts, axis=1, keepdims=True)
-
+    def lowest(c, s):
+        def step(k, g, b, carry):
+            return jnp.minimum(carry, tiles[k][g] + near[b, pl.ds(s, 1), :])
+
+        start = jnp.full((LANES, LANES), far_value, jnp.float32)
+        reached = over_slots(dims, places, table, filled, c, step, start)
+        best = jnp.min(reached, axis=1, keepdims=True)
+        return jnp.broadcast_to(best, (LANES, LANES))
+
+    def tally(c, s, best):
+        def step(k, g, b, carry):
+            hit = tiles[k][g] + near[b, pl.ds(s, 1), :] == best
+            return carry + jnp.where(hit, near[b, pl.ds(half + s, 1), :], 0.0)
+
+        start = jnp.zeros((LANES, LANES), jnp.float32)
+        counts = over_slots(dims, places, table, filled, c, step, start)
+        return jnp.sum(counts, axis=1, keepdims=True)
+
+    def column(c, best):
         turned = jnp.zeros((LANES, LANES), jnp.float32)
-        best = lowest(0)
         for s in range(half):
-            later = lowest(s + 1) if s + 1 < half else None
-            total = tally(s, best)
+            if s + 1 < half:
+                later = lowest(c, s + 1)
+            else:
+                later = lowest(jnp.minimum(c + 1, n_row - 1), 0)
+            total = tally(c, s, best)
             turned = jnp.where(lane == s, best, jnp.where(lane == half + s, total, turned))
             best = later
         found[c] = turned.T[: 2 * half]
-        return 0
-
-    lax.fori_loop(0, n_row, column, 0, unroll=UNROLL)
+        return best
+
+    lax.fori_loop(0, n_row, column, lowest(0, 0), unroll=UNROLL)
     for chip in range(chips):
         for col in range(n_col):
             if whole:

time: 60.3 us -> 60.8 us (level)
  no operation moved by 1% of the time
where the time goes in v6:
time: 60.8 us; the launch traced here: 60.5 us
  blocking collectives  49.5 us (81%)
  Pallas kernels  9.71 us (16%)
  between operations  0.67 us (1%)
    all_to_all x5, blocking collectives, all_to_all(): return lax.all_to_all(value, axes, split_axis=0, concat_axis=0, tiled=True)  49.5 us
    pallas_call x2, Pallas kernels, relax_level(): pl.pallas_call(functools.partial(relax_kernel, dims, counted, whole), out...  4.53 us
    pallas_call x2, Pallas kernels, depend_level(): pl.pallas_call(functools.partial(depend_kernel, dims, first, last), out_s...  2.82 us
    pallas_call x1, Pallas kernels, first_level(): pl.pallas_call(functools.partial(first_kernel, dims), out_shape=[piece(n_...  1.76 us
  transfers between devices with their start and end apart: 1, of which 0 were waited for; matrix products, arithmetic and copies ran while one was open for 0% of the time, Pallas kernels for 0%

profile of v6, /device:TPU:0, one launch (start us, length us, event | category | flops | bytes accessed | tf_op | source)
XLA Modules:
  0.0 60.5 jit_solution(8091290158934759169)
XLA Ops:
  0.6 1.8 %first_level.1 = (f32[16,8,128]{2,1,0:T(8,128)S(1)}, f32[16,128,128]{2,1,0:T(8,128)S(1)}, s32[4,128]{1,0:T(4,128)S(1)}) custom-call(s32[2,16]{1,0:T(2,128)} %bitcast.2, s32[8]{0:T(128)} %refs_1_.1, f32[16,128,128]{2,1,0:T(8,128)} %refs_2_.1), custom_call_target="tpu_custom_call" | custom-call | tf_op jit(solution)/shard_map/first_level/pallas_call | solution.py:141
  2.4 0.5 collective-permute-start
  3.0 13.4 %all_to_all.25.refs_3_ = f32[16,8,128]{2,1,0:T(8,128)S(1)} all-to-all(f32[16,8,128]{2,1,0:T(8,128)S(1)} %get-tuple-element.17), channel_id=1, replica_groups=mesh['groups'=2,'chip'=2,'core'=2,'col'=4] {'chip','core','col'}, dimensions={0} | all-to-all | bytes 131072 | tf_op jit(solution)/shard_map/all_to_all | solution.py:439
  16.3 0.0 collective-permute-done.refs_2_
  16.3 2.3 %relax_level.2 = f32[8,2,8,128]{3,2,1,0:T(8,128)S(1)} custom-call(s32[4,128]{1,0:T(4,128)S(1)} %get-tuple-element.15.refs_0_, f32[16,128,128]{2,1,0:T(8,128)S(1)} %get-tuple-element.16.refs_1_, f32[16,128,128]{2,1,0:T(8,128)S(1)} %collective-permute-done.refs_2_, f32[16,8,128]{2,1,0:T(8,128)S(1)} %all_to_all.25.refs_3_), custom_call_target="tpu_custom_call" | custom-call | tf_op jit(solution)/shard_map/relax_level/pallas_call | solution.py:278
  18.6 9.3 %all_to_all.26.refs_3_ = f32[8,2,8,128]{3,2,1,0:T(8,128)S(1)} all-to-all(f32[8,2,8,128]{3,2,1,0:T(8,128)S(1)} %relax_level.2), channel_id=1, replica_groups=mesh['groups'=2,'chip'=2,'core'=2,'col'=4] {'col','chip'}, dimensions={0} | all-to-all | bytes 131072 | tf_op jit(solution)/shard_map/all_to_all | solution.py:439
  27.9 2.3 %relax_level.3 = f32[8,4,8,128]{3,2,1,0:T(8,128)S(1)} custom-call(s32[4,128]{1,0:T(4,128)S(1)} %get-tuple-element.15.refs_0_, f32[16,128,128]{2,1,0:T(8,128)S(1)} %get-tuple-element.16.refs_1_, f32[16,128,128]{2,1,0:T(8,128)S(1)} %collective-permute-done.refs_2_, f32[8,2,8,128]{3,2,1,0:T(8,128)S(1)} %all_to_all.26.refs_3_), custom_call_target="tpu_custom_call" | custom-call | tf_op jit(solution)/shard_map/relax_level/pallas_call | solution.py:278
  30.2 9.7 %all_to_all.27.refs_3_ = f32[8,4,8,128]{3,2,1,0:T(8,128)S(1)} all-to-all(f32[8,4,8,128]{3,2,1,0:T(8,128)S(1)} %relax_level.3), channel_id=1, replica_groups=mesh['groups'=2,'chip'=2,'core'=2,'col'=4] {'col','chip'}, dimensions={0} | all-to-all | bytes 262144 | tf_op jit(solution)/shard_map/all_to_all | solution.py:439
  39.9 1.8 %depend_level.2 = (f32[16,8,128]{2,1,0:T(8,128)S(1)}, f32[8,8,128]{2,1,0:T(8,128)S(1)}, f32[4,8,128]{2,1,0:T(8,128)S(1)}, f32[128,128,128]{2,1,0:T(8,128)S(1)}) custom-call(s32[4,128]{1,0:T(4,128)S(1)} %get-tuple-element.15.refs_0_, f32[16,128,128]{2,1,0:T(8,128)S(1)} %get-tuple-element.16.refs_1_, f32[16,128,128]{2,1,0:T(8,128)S(1)} %collective-permute-done.refs_2_, ...), custom_call_target="tpu_custom_call" | custom-call | tf_op jit(solution)/shard_map/depend_level/pallas_call | solution.py:407
  41.7 9.2 %all_to_all.28.refs_4_ = f32[16,8,128]{2,1,0:T(8,128)S(1)} all-to-all(f32[16,8,128]{2,1,0:T(8,128)S(1)} %get-tuple-element.21), channel_id=1, replica_groups=mesh['groups'=2,'chip'=2,'core'=2,'col'=4] {'chip','core','col'}, dimensions={0} | all-to-all | bytes 131072 | tf_op jit(solution)/shard_map/all_to_all | solution.py:439
  50.9 1.0 %depend_level.3 = (f32[8,1,128]{2,1,0:T(1,128)S(1)}, f32[2,8,128]{2,1,0:T(8,128)S(1)}) custom-call(s32[4,128]{1,0:T(4,128)S(1)} %get-tuple-element.15.refs_0_, f32[8,8,128]{2,1,0:T(8,128)S(1)} %get-tuple-element.18.refs_1_, f32[4,8,128]{2,1,0:T(8,128)S(1)} %get-tuple-element.19.refs_2_, f32[128,128,128]{2,1,0:T(8,128)S(1)} %get-tuple-element.20.refs_3_, ...), custom_call_target="tpu_custom_call" | custom-call | tf_op jit(solution)/shard_map/depend_level/pallas_call | solution.py:407
  51.9 7.9 %all_to_all.29.came = f32[8,1,128]{2,1,0:T(1,128)S(1)} all-to-all(f32[8,1,128]{2,1,0:T(1,128)S(1)} %get-tuple-element.22), channel_id=1, replica_groups=mesh['groups'=2,'chip'=2,'core'=2,'col'=4] {'core','col'}, dimensions={0} | all-to-all | bytes 8192 | tf_op jit(solution)/shard_map/all_to_all | solution.py:439
  59.9 0.6 results.1
Async XLA Ops:
  2.4 13.9 %collective-permute-start = (f32[16,128,128]{2,1,0:T(8,128)S(1)}, f32[16,128,128]{2,1,0:T(8,128)S(1)}, u32[]{:S(2)}, u32[]{:S(2)}) collective-permute-start(f32[16,128,128]{2,1,0:T(8,128)S(1)} %get-tuple-element.16.refs_1_), channel_id=1, source_target_pairs={{0,4},{4,0},{1,5},{5,1},{2,6},{6,2},{3,7},{7,3},{8,12},{12,8},{9,1... | collective-permute-start | bytes 3145736 | tf_op jit(solution)/shard_map/ppermute | solution.py:443

commit v7 on v6

--- a/solution.py
+++ b/solution.py
@@ -12,7 +12,6 @@
 LANES = 128
 SUB = 8
 PAIR = 2
-UNROLL = 2
 
 far_value = 1000000.0
 no_edge = 2000000.0
@@ -50,15 +49,23 @@
 
 
 def source_ids(sources, first, half):
-    row = lax.broadcasted_iota(jnp.int32, (half, LANES), 0)
-    ids = jnp.zeros((half, LANES), jnp.int32)
+    row = lax.broadcasted_iota(jnp.int32, (PAIR * half, LANES), 0)
+    ids = jnp.zeros((PAIR * half, LANES), jnp.int32)
     for s in range(half):
-        ids = jnp.where(row == s, sources[first + s], ids)
+        ids = jnp.where(lax.rem(row, half) == s, sources[first + s], ids)
     return ids
 
 
-def is_source(ids, block):
-    return ids == block * LANES + lax.broadcasted_iota(jnp.int32, ids.shape, 1)
+def is_source(dims, ids, chip, col):
+    n_row, n_col, slots, half = dims
+    block = lax.broadcasted_iota(jnp.int32, ids.shape, 0) // half
+    lane = lax.broadcasted_iota(jnp.int32, ids.shape, 1)
+    return ids == ((PAIR * chip + block) * n_col + col) * LANES + lane
+
+
+def own_first(rows, my_core):
+    half = rows.shape[0] // PAIR
+    return jnp.where(my_core == 0, rows, jnp.concatenate([rows[half:], rows[:half]], axis=0))
 
 
 def settle(found_dist, found_count, at_source):
@@ -143,7 +150,7 @@
         out_shape=[
             piece(n_row * n_col, PAIR * half, LANES),
             piece(*tiles.shape),
-            jax.ShapeDtypeStruct((half, LANES), jnp.int32),
+            jax.ShapeDtypeStruct((PAIR * half, LANES), jnp.int32),
         ],
         in_specs=[in_hbm()] * 3,
         out_specs=[in_vmem()] * 3,
@@ -186,13 +193,13 @@
     for k in range(PAIR):
         if is_dense(dims):
             for r in range(n_col):
-                carry = step(k, r * n_row + c, k * n_col + r, carry)
+                carry = step(k, r * n_row + c, r, carry)
         else:
             at = k * n_row + c
 
             def entry(e, carry):
                 g = table[at * n_col + e]
-                return step(k, g, k * n_col + places[k][0, g], carry)
+                return step(k, g, places[k][0, g], carry)
 
             carry = lax.fori_loop(0, filled[at], entry, carry)
     return carry
@@ -217,72 +224,72 @@
     ids = source_rows[...]
     list_slots(dims, places, table, filled)
     for r in range(n_col):
-        for k in range(PAIR):
-            h = my_core ^ k
-            at_source = is_source(ids, (PAIR * my_x + h) * n_col + r)
-            if counted:
-                blocks = [came[r * chips + chip, h] for chip in range(chips)]
-                reached, count = merge([(block[:half], block[half:]) for block in blocks])
-            else:
-                parts = [came[at * n_col + r, pl.ds(h * half, half), :] for at in range(n_row)]
-                reached = functools.reduce(jnp.minimum, parts)
-                count = jnp.where(reached < far_value, 1.0, 0.0)
-            dist, count = settle(reached, count, at_source)
-            near[k * n_col + r, :half, :] = dist
-            near[k * n_col + r, half:, :] = count
+        if counted:
+            blocks = [came[r * chips + chip, 0] for chip in range(chips)]
+            reached, count = merge([(block[0], block[1]) for block in blocks])
+        else:
+            parts = [came[at * n_col + r] for at in range(n_row)]
+            reached = functools.reduce(jnp.minimum, parts)
+            count = jnp.where(reached < far_value, 1.0, 0.0)
+        dist, count = settle(reached, count, is_source(dims, ids, my_x, r))
+        near[r, 0] = own_first(dist, my_core)
+        near[r, 1] = own_first(count, my_core)
     lane = lax.broadcasted_iota(jnp.int32, (LANES, LANES), 1)
 
     def lowest(c, s):
-        def step(k, g, b, carry):
-            return jnp.minimum(carry, tiles[k][g] + near[b, pl.ds(s, 1), :])
+        def step(k, g, r, carry):
+            return jnp.minimum(carry, tiles[k][g] + near[r, 0, pl.ds(k * half + s, 1), :])
 
         start = jnp.full((LANES, LANES), far_value, jnp.float32)
         reached = over_slots(dims, places, table, filled, c, step, start)
-        best = jnp.min(reached, axis=1, keepdims=True)
-        return jnp.broadcast_to(best, (LANES, LANES))
+        return jnp.min(reached, axis=1, keepdims=True)
 
     def tally(c, s, best):
-        def step(k, g, b, carry):
-            hit = tiles[k][g] + near[b, pl.ds(s, 1), :] == best
-            return carry + jnp.where(hit, near[b, pl.ds(half + s, 1), :], 0.0)
+        def step(k, g, r, carry):
+            row = pl.ds(k * half + s, 1)
+            hit = tiles[k][g] + near[r, 0, row, :] == best
+            return carry + jnp.where(hit, near[r, 1, row, :], 0.0)
 
         start = jnp.zeros((LANES, LANES), jnp.float32)
         counts = over_slots(dims, places, table, filled, c, step, start)
         return jnp.sum(counts, axis=1, keepdims=True)
 
-    def column(c, best):
+    def columns(chip, _):
         turned = jnp.zeros((LANES, LANES), jnp.float32)
-        for s in range(half):
-            if s + 1 < half:
-                later = lowest(c, s + 1)
-            else:
-                later = lowest(jnp.minimum(c + 1, n_row - 1), 0)
-            total = tally(c, s, best)
-            turned = jnp.where(lane == s, best, jnp.where(lane == half + s, total, turned))
+        rows = PAIR * half
+        best = lowest(PAIR * chip, 0)
+        for at in range(rows):
+            later = None
+            if at + 1 < rows:
+                later = lowest(PAIR * chip + (at + 1) // half, (at + 1) % half)
+            total = tally(PAIR * chip + at // half, at % half, best)
+            turned = jnp.where(lane == at, best, jnp.where(lane == rows + at, total, turned))
             best = later
-        found[c] = turned.T[: 2 * half]
-        return best
-
-    lax.fori_loop(0, n_row, column, lowest(0, 0), unroll=UNROLL)
+        both = turned.T
+        found[chip, 0] = both[:rows]
+        found[chip, 1] = both[rows : 2 * rows]
+        return 0
+
+    lax.fori_loop(0, chips, columns, 0)
     for chip in range(chips):
         for col in range(n_col):
             if whole:
                 out[col * chips + chip] = found[...]
             else:
-                out[col * chips + chip] = found[pl.ds(PAIR * chip, PAIR)]
+                out[col * chips + chip, 0] = found[chip]
 
 
 def relax_level(dims, counted, whole, places, ids, tiles, came):
     n_row, n_col, slots, half = dims
-    blocks = n_row if whole else PAIR
+    chips = n_row // PAIR
     return pl.pallas_call(
         functools.partial(relax_kernel, dims, counted, whole),
-        out_shape=piece(n_row // PAIR * n_col, blocks, 2 * half, LANES),
+        out_shape=piece(chips * n_col, chips if whole else 1, 2, PAIR * half, LANES),
         in_specs=[in_smem()] * len(places) + [in_vmem()] * (PAIR + 2),
         out_specs=in_vmem(),
         scratch_shapes=[
-            pltpu.VMEM((PAIR * n_col, 2 * half, LANES), jnp.float32),
-            pltpu.VMEM((n_row, 2 * half, LANES), jnp.float32),
+            pltpu.VMEM((n_col, 2, PAIR * half, LANES), jnp.float32),
+            pltpu.VMEM((chips, 2, PAIR * half, LANES), jnp.float32),
         ]
         + slot_scratch(dims),
         compiler_params=params(large_limit),
@@ -306,77 +313,78 @@
     list_slots(dims, places, table, filled)
     if first:
         for r in range(n_col):
-            for k in range(PAIR):
-                h = my_core ^ k
-                at_source = is_source(ids, (PAIR * my_x + h) * n_col + r)
-                blocks = [came[r * chips + chip, PAIR * my_x + h] for chip in range(chips)]
-                found = merge([(block[:half], block[half:]) for block in blocks])
-                dist, count = settle(*found, at_source)
-                near[k * n_col + r, :half, :] = dist
-                near[k * n_col + r, half:, :] = count
-        for c in range(n_row):
-            at_source = is_source(ids, c * n_col + my_col)
-            blocks = [came[my_col * chips + chip, c] for chip in range(chips)]
-            found = merge([(block[:half], block[half:]) for block in blocks])
-            dist, count = settle(*found, at_source)
-            low[c, :half, :] = dist
-            low[c, half:, :] = count
+            blocks = [came[r * chips + chip, my_x] for chip in range(chips)]
+            found = merge([(block[0], block[1]) for block in blocks])
+            dist, count = settle(*found, is_source(dims, ids, my_x, r))
+            near[r, 0] = own_first(dist, my_core)
+            near[r, 1] = own_first(count, my_core)
+        for at in range(chips):
+            blocks = [came[my_col * chips + chip, at] for chip in range(chips)]
+            found = merge([(block[0], block[1]) for block in blocks])
+            dist, count = settle(*found, is_source(dims, ids, at, my_col))
+            low[at, 0] = dist
+            low[at, 1] = count
     else:
         other = came[(PAIR * my_x + 1 - my_core) * n_col + my_col]
+        mine = jnp.concatenate([near[my_col, 0, :half, :], near[my_col, 1, :half, :]], axis=0)
         for core in range(PAIR):
-            block = jnp.where(my_core == core, near[my_col], other)
+            block = jnp.where(my_core == core, mine, other)
             dist = block[:half]
             rows = pl.ds(core * half, half)
             state[0, rows, :] = jnp.where(dist < 0.5 * far_value, dist, -1.0)
             state[1, rows, :] = block[half:]
     acc[...] = jnp.zeros(acc.shape, jnp.float32)
 
-    def add_terms(b, s, part):
-        acc[b, s] += jnp.sum(part.reshape(LANES // SUB, SUB, LANES), axis=0)
-
-    def select(c, _):
-        count = low[c, half:, :]
+    def add_terms(k, r, s, part):
+        acc[k * n_col + r, s] += jnp.sum(part.reshape(LANES // SUB, SUB, LANES), axis=0)
+
+    def select(chip, _):
+        rows = PAIR * half
+        count = low[chip, 1]
         share = jnp.where(count > 0.5, 1.0 / jnp.maximum(count, 1.0), 0.0)
-        turned = jnp.concatenate([low[c, :half, :], share], axis=0).T
-        for s in range(half):
-            dist = jnp.broadcast_to(turned[:, s : s + 1], (LANES, LANES))
-            coef = jnp.broadcast_to(turned[:, half + s : half + s + 1], (LANES, LANES))
-
-            def step(k, g, b, carry):
-                hit = tiles[k][g] + near[b, pl.ds(s, 1), :] == dist
+        turned = jnp.concatenate([low[chip, 0], share], axis=0).T
+        for at in range(rows):
+            c, s = PAIR * chip + at // half, at % half
+            dist = jnp.broadcast_to(turned[:, at : at + 1], (LANES, LANES))
+            coef = jnp.broadcast_to(turned[:, rows + at : rows + at + 1], (LANES, LANES))
+
+            def step(k, g, r, carry):
+                hit = tiles[k][g] + near[r, 0, pl.ds(k * half + s, 1), :] == dist
                 part = jnp.where(hit, coef, 0.0)
                 terms[(k * slots + g) * half + s] = part
-                add_terms(b, s, part)
+                add_terms(k, r, s, part)
                 return carry
 
             over_slots(dims, places, table, filled, c, step, 0)
         return 0
 
-    def scale(c, _):
-        line = (c // PAIR * PAIR + my_core) * n_col
-        rows = pl.ds(c % PAIR * half, half)
-        total = functools.reduce(jnp.add, [came[line + col, rows, :] for col in range(n_col)])
-        turned = (1.0 + low[c, half:, :] * total).T
-        for s in range(half):
-            factor = jnp.broadcast_to(turned[:, s : s + 1], (LANES, LANES))
-
-            def step(k, g, b, carry):
-                add_terms(b, s, terms[(k * slots + g) * half + s] * factor)
+    def scale(chip):
+        line = (PAIR * chip + my_core) * n_col
+        total = functools.reduce(jnp.add, [came[line + col] for col in range(n_col)])
+        turned = (1.0 + low[chip, 1] * total).T
+        for at in range(PAIR * half):
+            c, s = PAIR * chip + at // half, at % half
+            factor = jnp.broadcast_to(turned[:, at : at + 1], (LANES, LANES))
+
+            def step(k, g, r, carry):
+                add_terms(k, r, s, terms[(k * slots + g) * half + s] * factor)
                 return carry
 
             over_slots(dims, places, table, filled, c, step, 0)
 
     if first:
-        lax.fori_loop(0, n_row, select, 0, unroll=UNROLL)
+        lax.fori_loop(0, chips, select, 0)
     else:
-        for c in range(n_row):
-            scale(c, 0)
+        for chip in range(chips):
+            scale(chip)
     for r in range(n_col):
+        if last:
+            counted = jnp.where(is_source(dims, ids, my_x, r), 0.0, 1.0)
+            weight = own_first(counted, my_core) * near[r, 1]
         for k in range(PAIR):
             if last:
-                b = k * n_col + r
-                at_source = is_source(ids, (PAIR * my_x + (my_core ^ k)) * n_col + r)
-                term = jnp.where(at_source, 0.0, near[b, half:, :] * jnp.sum(acc[b], axis=1))
+                sums = jnp.sum(acc[k * n_col + r], axis=1)
+                term = weight[k * half : k * half + half] * sums
                 out[(my_core ^ k) * n_col + r] = jnp.sum(term, axis=0, keepdims=True)
             else:
                 sums = jnp.sum(acc[(my_core ^ k) * n_col + r], axis=1)
@@ -384,9 +392,10 @@
                     line = (PAIR * chip + my_core) * n_col
                     out[line + r, pl.ds(k * half, half), :] = sums
     if not last:
+        give = jnp.concatenate([near[my_col, 0, half:, :], near[my_col, 1, half:, :]], axis=0)
         for chip in range(chips):
             for r in range(n_col):
-                out[(PAIR * chip + 1 - my_core) * n_col + r] = near[n_col + my_col]
+                out[(PAIR * chip + 1 - my_core) * n_col + r] = give
 
 
 def depend_level(dims, first, last, places, ids, tiles, bands, came):
@@ -397,8 +406,8 @@
         out_shape = [piece(n_row * n_col, PAIR * half, LANES)]
     if first:
         out_shape += [
-            piece(PAIR * n_col, 2 * half, LANES),
-            piece(n_row, 2 * half, LANES),
+            piece(n_col, 2, PAIR * half, LANES),
+            piece(n_row // PAIR, 2, PAIR * half, LANES),
             piece(PAIR * slots * half, LANES, LANES),
         ]
     else:

time: 60.8 us -> 60.4 us (level)
  no operation moved by 1% of the time
where the time goes in v7:
time: 60.4 us; the launch traced here: 60.1 us
  blocking collectives  49.5 us (82%)
  Pallas kernels  9.37 us (16%)
  between operations  0.66 us (1%)
  starting transfers between devices  0.63 us (1%)
    all_to_all x5, blocking collectives, all_to_all(): return lax.all_to_all(value, axes, split_axis=0, concat_axis=0, tiled=True)  49.5 us
    pallas_call x2, Pallas kernels, relax_level(): pl.pallas_call(functools.partial(relax_kernel, dims, counted, whole), out...  4.11 us
    pallas_call x2, Pallas kernels, depend_level(): pl.pallas_call(functools.partial(depend_kernel, dims, first, last), out_s...  2.92 us
    pallas_call x1, Pallas kernels, first_level(): pl.pallas_call(functools.partial(first_kernel, dims), out_shape=[piece(n_...  1.74 us
  transfers between devices with their start and end apart: 1, of which 0 were waited for; matrix products, arithmetic and copies ran while one was open for 0% of the time, Pallas kernels for 0%

profile of v7, /device:TPU:0, one launch (start us, length us, event | category | flops | bytes accessed | tf_op | source)
XLA Modules:
  0.0 60.1 jit_solution(8033269922078071724)
XLA Ops:
  0.6 1.7 %first_level.1 = (f32[16,8,128]{2,1,0:T(8,128)S(1)}, f32[16,128,128]{2,1,0:T(8,128)S(1)}, s32[8,128]{1,0:T(8,128)S(1)}) custom-call(s32[2,16]{1,0:T(2,128)} %bitcast.2, s32[8]{0:T(128)} %refs_1_.1, f32[16,128,128]{2,1,0:T(8,128)} %refs_2_.1), custom_call_target="tpu_custom_call" | custom-call | tf_op jit(solution)/shard_map/first_level/pallas_call | solution.py:148
  2.4 0.6 %collective-permute-start = (f32[16,128,128]{2,1,0:T(8,128)S(1)}, f32[16,128,128]{2,1,0:T(8,128)S(1)}, u32[]{:S(2)}, u32[]{:S(2)}) collective-permute-start(f32[16,128,128]{2,1,0:T(8,128)S(1)} %get-tuple-element.16.refs_1_), channel_id=1, source_target_pairs={{0,4},{4,0},{1,5},{5,1},{2,6},{6,2},{3,7},{7,3},{8,12},{12,8},{9,1... | collective-permute-start | bytes 3145736 | tf_op jit(solution)/shard_map/ppermute | solution.py:452
  3.0 13.3 %all_to_all.25.refs_3_ = f32[16,8,128]{2,1,0:T(8,128)S(1)} all-to-all(f32[16,8,128]{2,1,0:T(8,128)S(1)} %get-tuple-element.17), channel_id=1, replica_groups=mesh['groups'=2,'chip'=2,'core'=2,'col'=4] {'chip','core','col'}, dimensions={0} | all-to-all | bytes 131072 | tf_op jit(solution)/shard_map/all_to_all | solution.py:448
  16.3 0.0 collective-permute-done.refs_2_
  16.3 2.1 %relax_level.2 = f32[8,1,2,8,128]{4,3,2,1,0:T(8,128)S(1)} custom-call(s32[8,128]{1,0:T(8,128)S(1)} %get-tuple-element.15.refs_0_, f32[16,128,128]{2,1,0:T(8,128)S(1)} %get-tuple-element.16.refs_1_, f32[16,128,128]{2,1,0:T(8,128)S(1)} %collective-permute-done.refs_2_, f32[16,8,128]{2,1,0:T(8,128)S(1)} %all_to_all.25.refs_3_), custom_call_target="tpu_custom_call" | custom-call | tf_op jit(solution)/shard_map/relax_level/pallas_call | solution.py:285
  18.4 9.3 %all_to_all.26.refs_3_ = f32[8,1,2,8,128]{4,3,2,1,0:T(8,128)S(1)} all-to-all(f32[8,1,2,8,128]{4,3,2,1,0:T(8,128)S(1)} %relax_level.2), channel_id=1, replica_groups=mesh['groups'=2,'chip'=2,'core'=2,'col'=4] {'col','chip'}, dimensions={0} | all-to-all | bytes 131072 | tf_op jit(solution)/shard_map/all_to_all | solution.py:448
  27.7 2.1 %relax_level.3 = f32[8,2,2,8,128]{4,3,2,1,0:T(8,128)S(1)} custom-call(s32[8,128]{1,0:T(8,128)S(1)} %get-tuple-element.15.refs_0_, f32[16,128,128]{2,1,0:T(8,128)S(1)} %get-tuple-element.16.refs_1_, f32[16,128,128]{2,1,0:T(8,128)S(1)} %collective-permute-done.refs_2_, f32[8,1,2,8,128]{4,3,2,1,0:T(8,128)S(1)} %all_to_all.26.refs_3_), custom_call_target="tpu_custom_call" | custom-call | tf_op jit(solution)/shard_map/relax_level/pallas_call | solution.py:285
  29.7 9.7 %all_to_all.27.refs_3_ = f32[8,2,2,8,128]{4,3,2,1,0:T(8,128)S(1)} all-to-all(f32[8,2,2,8,128]{4,3,2,1,0:T(8,128)S(1)} %relax_level.3), channel_id=1, replica_groups=mesh['groups'=2,'chip'=2,'core'=2,'col'=4] {'col','chip'}, dimensions={0} | all-to-all | bytes 262144 | tf_op jit(solution)/shard_map/all_to_all | solution.py:448
  39.5 1.9 %depend_level.2 = (f32[16,8,128]{2,1,0:T(8,128)S(1)}, f32[4,2,8,128]{3,2,1,0:T(8,128)S(1)}, f32[2,2,8,128]{3,2,1,0:T(8,128)S(1)}, f32[128,128,128]{2,1,0:T(8,128)S(1)}) custom-call(s32[8,128]{1,0:T(8,128)S(1)} %get-tuple-element.15.refs_0_, f32[16,128,128]{2,1,0:T(8,128)S(1)} %get-tuple-element.16.refs_1_, f32[16,128,128]{2,1,0:T(8,128)S(1)} %collective-permute-done.refs_2_, ...), custom_call_target="tpu_custom_call" | custom-call | tf_op jit(solution)/shard_map/depend_level/pallas_call | solution.py:416
  41.4 9.2 %all_to_all.28.refs_4_ = f32[16,8,128]{2,1,0:T(8,128)S(1)} all-to-all(f32[16,8,128]{2,1,0:T(8,128)S(1)} %get-tuple-element.21), channel_id=1, replica_groups=mesh['groups'=2,'chip'=2,'core'=2,'col'=4] {'chip','core','col'}, dimensions={0} | all-to-all | bytes 131072 | tf_op jit(solution)/shard_map/all_to_all | solution.py:448
  50.6 1.0 %depend_level.3 = (f32[8,1,128]{2,1,0:T(1,128)S(1)}, f32[2,8,128]{2,1,0:T(8,128)S(1)}) custom-call(s32[8,128]{1,0:T(8,128)S(1)} %get-tuple-element.15.refs_0_, f32[4,2,8,128]{3,2,1,0:T(8,128)S(1)} %get-tuple-element.18.refs_1_, f32[2,2,8,128]{3,2,1,0:T(8,128)S(1)} %get-tuple-element.19.refs_2_, f32[128,128,128]{2,1,0:T(8,128)S(1)} %get-tuple-element.20.refs_3_, ...), custom_call_target="tpu_custom_call" | custom-call | tf_op jit(solution)/shard_map/depend_level/pallas_call | solution.py:416
  51.6 7.9 %all_to_all.29.came = f32[8,1,128]{2,1,0:T(1,128)S(1)} all-to-all(f32[8,1,128]{2,1,0:T(1,128)S(1)} %get-tuple-element.22), channel_id=1, replica_groups=mesh['groups'=2,'chip'=2,'core'=2,'col'=4] {'core','col'}, dimensions={0} | all-to-all | bytes 8192 | tf_op jit(solution)/shard_map/all_to_all | solution.py:448
  59.5 0.6 results.1
Async XLA Ops:
  2.4 14.0 %collective-permute-start = (f32[16,128,128]{2,1,0:T(8,128)S(1)}, f32[16,128,128]{2,1,0:T(8,128)S(1)}, u32[]{:S(2)}, u32[]{:S(2)}) collective-permute-start(f32[16,128,128]{2,1,0:T(8,128)S(1)} %get-tuple-element.16.refs_1_), channel_id=1, source_target_pairs={{0,4},{4,0},{1,5},{5,1},{2,6},{6,2},{3,7},{7,3},{8,12},{12,8},{9,1... | collective-permute-start | bytes 3145736 | tf_op jit(solution)/shard_map/ppermute | solution.py:452

commit v8 on v7

--- a/solution.py
+++ b/solution.py
@@ -12,6 +12,7 @@
 LANES = 128
 SUB = 8
 PAIR = 2
+SPAN = 64
 
 far_value = 1000000.0
 no_edge = 2000000.0
@@ -234,38 +235,47 @@
         dist, count = settle(reached, count, is_source(dims, ids, my_x, r))
         near[r, 0] = own_first(dist, my_core)
         near[r, 1] = own_first(count, my_core)
-    lane = lax.broadcasted_iota(jnp.int32, (LANES, LANES), 1)
-
-    def lowest(c, s):
+    lane = lax.broadcasted_iota(jnp.int32, (SPAN, LANES), 1)
+
+    def lowest(chip, item):
+        h, s, q = item
+
         def step(k, g, r, carry):
-            return jnp.minimum(carry, tiles[k][g] + near[r, 0, pl.ds(k * half + s, 1), :])
-
-        start = jnp.full((LANES, LANES), far_value, jnp.float32)
-        reached = over_slots(dims, places, table, filled, c, step, start)
+            weight = tiles[k][g, pl.ds(q, SPAN), :]
+            return jnp.minimum(carry, weight + near[r, 0, pl.ds(k * half + s, 1), :])
+
+        start = jnp.full((SPAN, LANES), far_value, jnp.float32)
+        reached = over_slots(dims, places, table, filled, PAIR * chip + h, step, start)
         return jnp.min(reached, axis=1, keepdims=True)
 
-    def tally(c, s, best):
+    def tally(chip, item, best):
+        h, s, q = item
+
         def step(k, g, r, carry):
             row = pl.ds(k * half + s, 1)
-            hit = tiles[k][g] + near[r, 0, row, :] == best
+            hit = tiles[k][g, pl.ds(q, SPAN), :] + near[r, 0, row, :] == best
             return carry + jnp.where(hit, near[r, 1, row, :], 0.0)
 
-        start = jnp.zeros((LANES, LANES), jnp.float32)
-        counts = over_slots(dims, places, table, filled, c, step, start)
+        start = jnp.zeros((SPAN, LANES), jnp.float32)
+        counts = over_slots(dims, places, table, filled, PAIR * chip + h, step, start)
         return jnp.sum(counts, axis=1, keepdims=True)
 
+    spans = range(0, LANES, SPAN)
+    items = [(h, s, q) for h in range(PAIR) for q in spans for s in range(half)]
+
     def columns(chip, _):
-        turned = jnp.zeros((LANES, LANES), jnp.float32)
         rows = PAIR * half
-        best = lowest(PAIR * chip, 0)
-        for at in range(rows):
-            later = None
-            if at + 1 < rows:
-                later = lowest(PAIR * chip + (at + 1) // half, (at + 1) % half)
-            total = tally(PAIR * chip + at // half, at % half, best)
-            turned = jnp.where(lane == at, best, jnp.where(lane == rows + at, total, turned))
+        turned = {q: jnp.zeros((SPAN, LANES), jnp.float32) for q in spans}
+        best = lowest(chip, items[0])
+        for at, item in enumerate(items):
+            later = lowest(chip, items[at + 1]) if at + 1 < len(items) else None
+            total = tally(chip, item, best)
+            h, s, q = item
+            to = h * half + s
+            with_total = jnp.where(lane == rows + to, total, turned[q])
+            turned[q] = jnp.where(lane == to, best, with_total)
             best = later
-        both = turned.T
+        both = jnp.concatenate([turned[q] for q in spans], axis=0).T
         found[chip, 0] = both[:rows]
         found[chip, 1] = both[rows : 2 * rows]
         return 0
@@ -336,22 +346,24 @@
     acc[...] = jnp.zeros(acc.shape, jnp.float32)
 
     def add_terms(k, r, s, part):
-        acc[k * n_col + r, s] += jnp.sum(part.reshape(LANES // SUB, SUB, LANES), axis=0)
+        acc[k * n_col + r, s] += jnp.sum(part.reshape(-1, SUB, LANES), axis=0)
 
     def select(chip, _):
         rows = PAIR * half
         count = low[chip, 1]
         share = jnp.where(count > 0.5, 1.0 / jnp.maximum(count, 1.0), 0.0)
         turned = jnp.concatenate([low[chip, 0], share], axis=0).T
-        for at in range(rows):
+        for at, q in [(at, q) for at in range(rows) for q in range(0, LANES, SPAN)]:
             c, s = PAIR * chip + at // half, at % half
-            dist = jnp.broadcast_to(turned[:, at : at + 1], (LANES, LANES))
-            coef = jnp.broadcast_to(turned[:, rows + at : rows + at + 1], (LANES, LANES))
+            span = slice(q, q + SPAN)
+            dist = jnp.broadcast_to(turned[span, at : at + 1], (SPAN, LANES))
+            coef = jnp.broadcast_to(turned[span, rows + at : rows + at + 1], (SPAN, LANES))
 
             def step(k, g, r, carry):
-                hit = tiles[k][g] + near[r, 0, pl.ds(k * half + s, 1), :] == dist
+                row = near[r, 0, pl.ds(k * half + s, 1), :]
+                hit = tiles[k][g, pl.ds(q, SPAN), :] + row == dist
                 part = jnp.where(hit, coef, 0.0)
-                terms[(k * slots + g) * half + s] = part
+                terms[(k * slots + g) * half + s, pl.ds(q, SPAN), :] = part
                 add_terms(k, r, s, part)
                 return carry
 

time: 60.4 us -> 60.1 us (level)
  no operation moved by 1% of the time
where the time goes in v8:
time: 60.1 us; the launch traced here: 59.8 us
  blocking collectives  49.5 us (82%)
  Pallas kernels  9.13 us (15%)
  between operations  0.66 us (1%)
    all_to_all x5, blocking collectives, all_to_all(): return lax.all_to_all(value, axes, split_axis=0, concat_axis=0, tiled=True)  49.5 us
    pallas_call x2, Pallas kernels, relax_level(): pl.pallas_call(functools.partial(relax_kernel, dims, counted, whole), out...  3.84 us
    pallas_call x2, Pallas kernels, depend_level(): pl.pallas_call(functools.partial(depend_kernel, dims, first, last), out_s...  2.9 us
    pallas_call x1, Pallas kernels, first_level(): pl.pallas_call(functools.partial(first_kernel, dims), out_shape=[piece(n_...  1.79 us
  transfers between devices with their start and end apart: 1, of which 0 were waited for; matrix products, arithmetic and copies ran while one was open for 0% of the time, Pallas kernels for 0%

profile of v8, /device:TPU:0, one launch (start us, length us, event | category | flops | bytes accessed | tf_op | source)
XLA Modules:
  0.0 59.8 jit_solution(10985068563557797554)
XLA Ops:
  0.6 1.8 %first_level.1 = (f32[16,8,128]{2,1,0:T(8,128)S(1)}, f32[16,128,128]{2,1,0:T(8,128)S(1)}, s32[8,128]{1,0:T(8,128)S(1)}) custom-call(s32[2,16]{1,0:T(2,128)} %bitcast.2, s32[8]{0:T(128)} %refs_1_.1, f32[16,128,128]{2,1,0:T(8,128)} %refs_2_.1), custom_call_target="tpu_custom_call" | custom-call | tf_op jit(solution)/shard_map/first_level/pallas_call | solution.py:149
  2.4 0.5 collective-permute-start
  2.9 13.4 %all_to_all.25.refs_3_ = f32[16,8,128]{2,1,0:T(8,128)S(1)} all-to-all(f32[16,8,128]{2,1,0:T(8,128)S(1)} %get-tuple-element.17), channel_id=1, replica_groups=mesh['groups'=2,'chip'=2,'core'=2,'col'=4] {'chip','core','col'}, dimensions={0} | all-to-all | bytes 131072 | tf_op jit(solution)/shard_map/all_to_all | solution.py:460
  16.3 0.0 collective-permute-done.refs_2_
  16.3 1.9 %relax_level.2 = f32[8,1,2,8,128]{4,3,2,1,0:T(8,128)S(1)} custom-call(s32[8,128]{1,0:T(8,128)S(1)} %get-tuple-element.15.refs_0_, f32[16,128,128]{2,1,0:T(8,128)S(1)} %get-tuple-element.16.refs_1_, f32[16,128,128]{2,1,0:T(8,128)S(1)} %collective-permute-done.refs_2_, f32[16,8,128]{2,1,0:T(8,128)S(1)} %all_to_all.25.refs_3_), custom_call_target="tpu_custom_call" | custom-call | tf_op jit(solution)/shard_map/relax_level/pallas_call | solution.py:295
  18.2 9.3 %all_to_all.26.refs_3_ = f32[8,1,2,8,128]{4,3,2,1,0:T(8,128)S(1)} all-to-all(f32[8,1,2,8,128]{4,3,2,1,0:T(8,128)S(1)} %relax_level.2), channel_id=1, replica_groups=mesh['groups'=2,'chip'=2,'core'=2,'col'=4] {'col','chip'}, dimensions={0} | all-to-all | bytes 131072 | tf_op jit(solution)/shard_map/all_to_all | solution.py:460
  27.5 1.9 %relax_level.3 = f32[8,2,2,8,128]{4,3,2,1,0:T(8,128)S(1)} custom-call(s32[8,128]{1,0:T(8,128)S(1)} %get-tuple-element.15.refs_0_, f32[16,128,128]{2,1,0:T(8,128)S(1)} %get-tuple-element.16.refs_1_, f32[16,128,128]{2,1,0:T(8,128)S(1)} %collective-permute-done.refs_2_, f32[8,1,2,8,128]{4,3,2,1,0:T(8,128)S(1)} %all_to_all.26.refs_3_), custom_call_target="tpu_custom_call" | custom-call | tf_op jit(solution)/shard_map/relax_level/pallas_call | solution.py:295
  29.4 9.7 %all_to_all.27.refs_3_ = f32[8,2,2,8,128]{4,3,2,1,0:T(8,128)S(1)} all-to-all(f32[8,2,2,8,128]{4,3,2,1,0:T(8,128)S(1)} %relax_level.3), channel_id=1, replica_groups=mesh['groups'=2,'chip'=2,'core'=2,'col'=4] {'col','chip'}, dimensions={0} | all-to-all | bytes 262144 | tf_op jit(solution)/shard_map/all_to_all | solution.py:460
  39.2 1.9 %depend_level.2 = (f32[16,8,128]{2,1,0:T(8,128)S(1)}, f32[4,2,8,128]{3,2,1,0:T(8,128)S(1)}, f32[2,2,8,128]{3,2,1,0:T(8,128)S(1)}, f32[128,128,128]{2,1,0:T(8,128)S(1)}) custom-call(s32[8,128]{1,0:T(8,128)S(1)} %get-tuple-element.15.refs_0_, f32[16,128,128]{2,1,0:T(8,128)S(1)} %get-tuple-element.16.refs_1_, f32[16,128,128]{2,1,0:T(8,128)S(1)} %collective-permute-done.refs_2_, ...), custom_call_target="tpu_custom_call" | custom-call | tf_op jit(solution)/shard_map/depend_level/pallas_call | solution.py:428
  41.0 9.2 %all_to_all.28.refs_4_ = f32[16,8,128]{2,1,0:T(8,128)S(1)} all-to-all(f32[16,8,128]{2,1,0:T(8,128)S(1)} %get-tuple-element.21), channel_id=1, replica_groups=mesh['groups'=2,'chip'=2,'core'=2,'col'=4] {'chip','core','col'}, dimensions={0} | all-to-all | bytes 131072 | tf_op jit(solution)/shard_map/all_to_all | solution.py:460
  50.2 1.0 %depend_level.3 = (f32[8,1,128]{2,1,0:T(1,128)S(1)}, f32[2,8,128]{2,1,0:T(8,128)S(1)}) custom-call(s32[8,128]{1,0:T(8,128)S(1)} %get-tuple-element.15.refs_0_, f32[4,2,8,128]{3,2,1,0:T(8,128)S(1)} %get-tuple-element.18.refs_1_, f32[2,2,8,128]{3,2,1,0:T(8,128)S(1)} %get-tuple-element.19.refs_2_, f32[128,128,128]{2,1,0:T(8,128)S(1)} %get-tuple-element.20.refs_3_, ...), custom_call_target="tpu_custom_call" | custom-call | tf_op jit(solution)/shard_map/depend_level/pallas_call | solution.py:428
  51.3 7.9 %all_to_all.29.came = f32[8,1,128]{2,1,0:T(1,128)S(1)} all-to-all(f32[8,1,128]{2,1,0:T(1,128)S(1)} %get-tuple-element.22), channel_id=1, replica_groups=mesh['groups'=2,'chip'=2,'core'=2,'col'=4] {'core','col'}, dimensions={0} | all-to-all | bytes 8192 | tf_op jit(solution)/shard_map/all_to_all | solution.py:460
  59.2 0.6 %results.1 = (f32[8,128]{1,0:T(8,128)}, f32[8,128]{1,0:T(8,128)}, f32[1,128]{1,0:T(1,128)}) custom-call(f32[8,1,128]{2,1,0:T(1,128)S(1)} %all_to_all.29.came, f32[2,8,128]{2,1,0:T(8,128)S(1)} %get-tuple-element.23.state), custom_call_target="tpu_custom_call" | custom-call | tf_op jit(solution)/shard_map/results/pallas_call | solution.py:449
Async XLA Ops:
  2.4 13.9 %collective-permute-start = (f32[16,128,128]{2,1,0:T(8,128)S(1)}, f32[16,128,128]{2,1,0:T(8,128)S(1)}, u32[]{:S(2)}, u32[]{:S(2)}) collective-permute-start(f32[16,128,128]{2,1,0:T(8,128)S(1)} %get-tuple-element.16.refs_1_), channel_id=1, source_target_pairs={{0,4},{4,0},{1,5},{5,1},{2,6},{6,2},{3,7},{7,3},{8,12},{12,8},{9,1... | collective-permute-start | bytes 3145736 | tf_op jit(solution)/shard_map/ppermute | solution.py:464

commit v9 on v8

--- a/solution.py
+++ b/solution.py
@@ -84,7 +84,7 @@
 def first_kernel(dims, *refs):
     n_row, n_col, slots, half = dims
     places_in, sources_in, tiles_in, out, turned, ids = refs[:6]
-    places, sources, slot_of, tiles, lines, sems = refs[6:]
+    places, sources, slot_of, tiles, sems = refs[6:]
     my_x, my_core, my_col = position()
     my_row = my_x * PAIR + my_core
     parts = sems.shape[0] - 2
@@ -99,7 +99,6 @@
         fetch.append(pltpu.make_async_copy(tiles_in.at[span], tiles.at[span], sems.at[part]))
     for copy in given + fetch:
         copy.start()
-    lines[...] = jnp.zeros(lines.shape, jnp.float32)
 
     def clear(at, _):
         slot_of[at] = -1
@@ -112,34 +111,34 @@
     for g in range(slots):
         slot_of[places[0, g] * n_row + places[1, g]] = g
     ids[...] = source_ids(sources, my_core * half, half)
-    for part in range(parts):
-        fetch[part].wait()
+
+    def turn(part):
         for g in range(part * size, part * size + size):
             at = places[0, g] * n_row + places[1, g] if is_dense(dims) else g
             raw = tiles[g]
             turned[at] = jnp.where(raw > 0, raw, no_edge).T
-    for s in range(PAIR * half):
-        vertex = sources[s]
-        block, place = vertex // LANES, lax.rem(vertex, LANES)
-        r = lax.rem(block, n_col)
-
-        @pl.when(block // n_col == my_row)
-        def _():
-            for c in range(n_row):
-                g = slot_of[r * n_row + c]
-
-                @pl.when(g >= 0)
-                def _():
-                    line = c % PAIR * half + s % half
-                    row = tiles[g, pl.ds(place, 1), :]
-                    lines[c // PAIR, s // half, pl.ds(line, 1), :] = row
-
-    for chip in range(n_row // PAIR):
-        for core in range(PAIR):
-            line = lines[chip, core]
-            line = jnp.where(line > 0, line, far_value)
-            for col in range(n_col):
-                out[(chip * PAIR + core) * n_col + col] = line
+
+    for part in range(parts):
+        fetch[part].wait()
+        if part + 1 < parts:
+            turn(part)
+    row_at = lax.broadcasted_iota(jnp.int32, (PAIR * half, LANES), 0)
+    lines = {}
+    for c in range(n_row):
+        for s in range(PAIR * half):
+            vertex = sources[s]
+            block, place = vertex // LANES, lax.rem(vertex, LANES)
+            g = slot_of[lax.rem(block, n_col) * n_row + c]
+            here = jnp.logical_and(block // n_col == my_row, g >= 0)
+            row = tiles[jnp.maximum(g, 0), pl.ds(place, 1), :]
+            to = jnp.where(here, c % PAIR * half + s % half, -1)
+            line = lines.get((c // PAIR, s // half), jnp.zeros(row_at.shape, jnp.float32))
+            lines[c // PAIR, s // half] = jnp.where(row_at == to, row, line)
+    for (chip, core), line in lines.items():
+        line = jnp.where(line > 0, line, far_value)
+        for col in range(n_col):
+            out[(chip * PAIR + core) * n_col + col] = line
+    turn(parts - 1)
 
 
 def first_level(dims, places, sources, tiles):
@@ -160,7 +159,6 @@
             pltpu.SMEM(sources.shape, jnp.int32),
             pltpu.SMEM((n_row * n_col,), jnp.int32),
             pltpu.VMEM(tiles.shape, jnp.float32),
-            pltpu.VMEM((n_row // PAIR, PAIR, PAIR * half, LANES), jnp.float32),
             pltpu.SemaphoreType.DMA((parts + 2,)),
         ],
         compiler_params=params(large_limit),
@@ -220,7 +218,7 @@
     n_places = 0 if is_dense(dims) else PAIR
     places, refs = refs[:n_places], refs[n_places:]
     source_rows, tiles, refs = refs[0], refs[1 : 1 + PAIR], refs[1 + PAIR :]
-    came, out, near, found, table, filled = refs
+    came, out, near, found, held, table, filled = refs
     my_x, my_core, my_col = position()
     ids = source_rows[...]
     list_slots(dims, places, table, filled)
@@ -237,24 +235,25 @@
         near[r, 1] = own_first(count, my_core)
     lane = lax.broadcasted_iota(jnp.int32, (SPAN, LANES), 1)
 
-    def lowest(chip, item):
-        h, s, q = item
+    def lowest(chip, at):
+        h, s, q = items[at]
 
         def step(k, g, r, carry):
             weight = tiles[k][g, pl.ds(q, SPAN), :]
-            return jnp.minimum(carry, weight + near[r, 0, pl.ds(k * half + s, 1), :])
+            reached = weight + near[r, 0, pl.ds(k * half + s, 1), :]
+            held[at % 2, k * n_col + r] = reached
+            return jnp.minimum(carry, reached)
 
         start = jnp.full((SPAN, LANES), far_value, jnp.float32)
         reached = over_slots(dims, places, table, filled, PAIR * chip + h, step, start)
         return jnp.min(reached, axis=1, keepdims=True)
 
-    def tally(chip, item, best):
-        h, s, q = item
+    def tally(chip, at, best):
+        h, s, q = items[at]
 
         def step(k, g, r, carry):
-            row = pl.ds(k * half + s, 1)
-            hit = tiles[k][g, pl.ds(q, SPAN), :] + near[r, 0, row, :] == best
-            return carry + jnp.where(hit, near[r, 1, row, :], 0.0)
+            hit = held[at % 2, k * n_col + r] == best
+            return carry + jnp.where(hit, near[r, 1, pl.ds(k * half + s, 1), :], 0.0)
 
         start = jnp.zeros((SPAN, LANES), jnp.float32)
         counts = over_slots(dims, places, table, filled, PAIR * chip + h, step, start)
@@ -266,10 +265,10 @@
     def columns(chip, _):
         rows = PAIR * half
         turned = {q: jnp.zeros((SPAN, LANES), jnp.float32) for q in spans}
-        best = lowest(chip, items[0])
+        best = lowest(chip, 0)
         for at, item in enumerate(items):
-            later = lowest(chip, items[at + 1]) if at + 1 < len(items) else None
-            total = tally(chip, item, best)
+            later = lowest(chip, at + 1) if at + 1 < len(items) else None
+            total = tally(chip, at, best)
             h, s, q = item
             to = h * half + s
             with_total = jnp.where(lane == rows + to, total, turned[q])
@@ -300,6 +299,7 @@
         scratch_shapes=[
             pltpu.VMEM((n_col, 2, PAIR * half, LANES), jnp.float32),
             pltpu.VMEM((chips, 2, PAIR * half, LANES), jnp.float32),
+            pltpu.VMEM((2, PAIR * n_col, SPAN, LANES), jnp.float32),
         ]
         + slot_scratch(dims),
         compiler_params=params(large_limit),

time: 60.1 us -> 60.1 us (level)
  no operation moved by 1% of the time
where the time goes in v9:
time: 60.1 us; the launch traced here: 59.8 us
  blocking collectives  49.6 us (83%)
  Pallas kernels  9.01 us (15%)
  between operations  0.66 us (1%)
    all_to_all x5, blocking collectives, all_to_all(): return lax.all_to_all(value, axes, split_axis=0, concat_axis=0, tiled=True)  49.6 us
    pallas_call x2, Pallas kernels, relax_level(): pl.pallas_call(functools.partial(relax_kernel, dims, counted, whole), out...  3.87 us
    pallas_call x2, Pallas kernels, depend_level(): pl.pallas_call(functools.partial(depend_kernel, dims, first, last), out_s...  2.9 us
    pallas_call x1, Pallas kernels, first_level(): pl.pallas_call(functools.partial(first_kernel, dims), out_shape=[piece(n_...  1.64 us
  transfers between devices with their start and end apart: 1, of which 0 were waited for; matrix products, arithmetic and copies ran while one was open for 0% of the time, Pallas kernels for 0%

profile of v9, /device:TPU:0, one launch (start us, length us, event | category | flops | bytes accessed | tf_op | source)
XLA Modules:
  0.0 59.8 jit_solution(17017747315509336898)
XLA Ops:
  0.6 1.6 %first_level.1 = (f32[16,8,128]{2,1,0:T(8,128)S(1)}, f32[16,128,128]{2,1,0:T(8,128)S(1)}, s32[8,128]{1,0:T(8,128)S(1)}) custom-call(s32[2,16]{1,0:T(2,128)} %bitcast.2, s32[8]{0:T(128)} %refs_1_.1, f32[16,128,128]{2,1,0:T(8,128)} %refs_2_.1), custom_call_target="tpu_custom_call" | custom-call | tf_op jit(solution)/shard_map/first_level/pallas_call | solution.py:148
  2.3 0.5 collective-permute-start
  2.8 13.4 %all_to_all.25.refs_3_ = f32[16,8,128]{2,1,0:T(8,128)S(1)} all-to-all(f32[16,8,128]{2,1,0:T(8,128)S(1)} %get-tuple-element.17), channel_id=1, replica_groups=mesh['groups'=2,'chip'=2,'core'=2,'col'=4] {'chip','core','col'}, dimensions={0} | all-to-all | bytes 131072 | tf_op jit(solution)/shard_map/all_to_all | solution.py:460
  16.2 0.0 collective-permute-done.refs_2_
  16.2 1.9 %relax_level.2 = f32[8,1,2,8,128]{4,3,2,1,0:T(8,128)S(1)} custom-call(s32[8,128]{1,0:T(8,128)S(1)} %get-tuple-element.15.refs_0_, f32[16,128,128]{2,1,0:T(8,128)S(1)} %get-tuple-element.16.refs_1_, f32[16,128,128]{2,1,0:T(8,128)S(1)} %collective-permute-done.refs_2_, f32[16,8,128]{2,1,0:T(8,128)S(1)} %all_to_all.25.refs_3_), custom_call_target="tpu_custom_call" | custom-call | tf_op jit(solution)/shard_map/relax_level/pallas_call | solution.py:294
  18.2 9.3 %all_to_all.26.refs_3_ = f32[8,1,2,8,128]{4,3,2,1,0:T(8,128)S(1)} all-to-all(f32[8,1,2,8,128]{4,3,2,1,0:T(8,128)S(1)} %relax_level.2), channel_id=1, replica_groups=mesh['groups'=2,'chip'=2,'core'=2,'col'=4] {'col','chip'}, dimensions={0} | all-to-all | bytes 131072 | tf_op jit(solution)/shard_map/all_to_all | solution.py:460
  27.5 1.9 %relax_level.3 = f32[8,2,2,8,128]{4,3,2,1,0:T(8,128)S(1)} custom-call(s32[8,128]{1,0:T(8,128)S(1)} %get-tuple-element.15.refs_0_, f32[16,128,128]{2,1,0:T(8,128)S(1)} %get-tuple-element.16.refs_1_, f32[16,128,128]{2,1,0:T(8,128)S(1)} %collective-permute-done.refs_2_, f32[8,1,2,8,128]{4,3,2,1,0:T(8,128)S(1)} %all_to_all.26.refs_3_), custom_call_target="tpu_custom_call" | custom-call | tf_op jit(solution)/shard_map/relax_level/pallas_call | solution.py:294
  29.4 9.7 %all_to_all.27.refs_3_ = f32[8,2,2,8,128]{4,3,2,1,0:T(8,128)S(1)} all-to-all(f32[8,2,2,8,128]{4,3,2,1,0:T(8,128)S(1)} %relax_level.3), channel_id=1, replica_groups=mesh['groups'=2,'chip'=2,'core'=2,'col'=4] {'col','chip'}, dimensions={0} | all-to-all | bytes 262144 | tf_op jit(solution)/shard_map/all_to_all | solution.py:460
  39.1 1.9 %depend_level.2 = (f32[16,8,128]{2,1,0:T(8,128)S(1)}, f32[4,2,8,128]{3,2,1,0:T(8,128)S(1)}, f32[2,2,8,128]{3,2,1,0:T(8,128)S(1)}, f32[128,128,128]{2,1,0:T(8,128)S(1)}) custom-call(s32[8,128]{1,0:T(8,128)S(1)} %get-tuple-element.15.refs_0_, f32[16,128,128]{2,1,0:T(8,128)S(1)} %get-tuple-element.16.refs_1_, f32[16,128,128]{2,1,0:T(8,128)S(1)} %collective-permute-done.refs_2_, ...), custom_call_target="tpu_custom_call" | custom-call | tf_op jit(solution)/shard_map/depend_level/pallas_call | solution.py:428
  41.0 9.2 %all_to_all.28.refs_4_ = f32[16,8,128]{2,1,0:T(8,128)S(1)} all-to-all(f32[16,8,128]{2,1,0:T(8,128)S(1)} %get-tuple-element.21), channel_id=1, replica_groups=mesh['groups'=2,'chip'=2,'core'=2,'col'=4] {'chip','core','col'}, dimensions={0} | all-to-all | bytes 131072 | tf_op jit(solution)/shard_map/all_to_all | solution.py:460
  50.2 1.0 %depend_level.3 = (f32[8,1,128]{2,1,0:T(1,128)S(1)}, f32[2,8,128]{2,1,0:T(8,128)S(1)}) custom-call(s32[8,128]{1,0:T(8,128)S(1)} %get-tuple-element.15.refs_0_, f32[4,2,8,128]{3,2,1,0:T(8,128)S(1)} %get-tuple-element.18.refs_1_, f32[2,2,8,128]{3,2,1,0:T(8,128)S(1)} %get-tuple-element.19.refs_2_, f32[128,128,128]{2,1,0:T(8,128)S(1)} %get-tuple-element.20.refs_3_, ...), custom_call_target="tpu_custom_call" | custom-call | tf_op jit(solution)/shard_map/depend_level/pallas_call | solution.py:428
  51.2 7.9 %all_to_all.29.came = f32[8,1,128]{2,1,0:T(1,128)S(1)} all-to-all(f32[8,1,128]{2,1,0:T(1,128)S(1)} %get-tuple-element.22), channel_id=1, replica_groups=mesh['groups'=2,'chip'=2,'core'=2,'col'=4] {'core','col'}, dimensions={0} | all-to-all | bytes 8192 | tf_op jit(solution)/shard_map/all_to_all | solution.py:460
  59.2 0.6 %results.1 = (f32[8,128]{1,0:T(8,128)}, f32[8,128]{1,0:T(8,128)}, f32[1,128]{1,0:T(1,128)}) custom-call(f32[8,1,128]{2,1,0:T(1,128)S(1)} %all_to_all.29.came, f32[2,8,128]{2,1,0:T(8,128)S(1)} %get-tuple-element.23.state), custom_call_target="tpu_custom_call" | custom-call | tf_op jit(solution)/shard_map/results/pallas_call | solution.py:449
Async XLA Ops:
  2.3 14.0 %collective-permute-start = (f32[16,128,128]{2,1,0:T(8,128)S(1)}, f32[16,128,128]{2,1,0:T(8,128)S(1)}, u32[]{:S(2)}, u32[]{:S(2)}) collective-permute-start(f32[16,128,128]{2,1,0:T(8,128)S(1)} %get-tuple-element.16.refs_1_), channel_id=1, source_target_pairs={{0,4},{4,0},{1,5},{5,1},{2,6},{6,2},{3,7},{7,3},{8,12},{12,8},{9,1... | collective-permute-start | bytes 3145736 | tf_op jit(solution)/shard_map/ppermute | solution.py:464

commit v10 on v9

--- a/solution.py
+++ b/solution.py
@@ -12,7 +12,7 @@
 LANES = 128
 SUB = 8
 PAIR = 2
-SPAN = 64
+SPAN = 32
 
 far_value = 1000000.0
 no_edge = 2000000.0
@@ -218,7 +218,7 @@
     n_places = 0 if is_dense(dims) else PAIR
     places, refs = refs[:n_places], refs[n_places:]
     source_rows, tiles, refs = refs[0], refs[1 : 1 + PAIR], refs[1 + PAIR :]
-    came, out, near, found, held, table, filled = refs
+    came, out, near, found, table, filled = refs
     my_x, my_core, my_col = position()
     ids = source_rows[...]
     list_slots(dims, places, table, filled)
@@ -235,44 +235,48 @@
         near[r, 1] = own_first(count, my_core)
     lane = lax.broadcasted_iota(jnp.int32, (SPAN, LANES), 1)
 
+    spans = range(0, LANES, SPAN)
+    items = [(h, q) for h in range(PAIR) for q in spans]
+
     def lowest(chip, at):
-        h, s, q = items[at]
+        h, q = items[at]
 
         def step(k, g, r, carry):
             weight = tiles[k][g, pl.ds(q, SPAN), :]
-            reached = weight + near[r, 0, pl.ds(k * half + s, 1), :]
-            held[at % 2, k * n_col + r] = reached
-            return jnp.minimum(carry, reached)
-
-        start = jnp.full((SPAN, LANES), far_value, jnp.float32)
+            rows = [near[r, 0, pl.ds(k * half + s, 1), :] for s in range(half)]
+            return tuple(jnp.minimum(low, weight + row) for low, row in zip(carry, rows))
+
+        start = (jnp.full((SPAN, LANES), far_value, jnp.float32),) * half
         reached = over_slots(dims, places, table, filled, PAIR * chip + h, step, start)
-        return jnp.min(reached, axis=1, keepdims=True)
+        return [jnp.min(low, axis=1, keepdims=True) for low in reached]
 
     def tally(chip, at, best):
-        h, s, q = items[at]
+        h, q = items[at]
 
         def step(k, g, r, carry):
-            hit = held[at % 2, k * n_col + r] == best
-            return carry + jnp.where(hit, near[r, 1, pl.ds(k * half + s, 1), :], 0.0)
-
-        start = jnp.zeros((SPAN, LANES), jnp.float32)
+            weight = tiles[k][g, pl.ds(q, SPAN), :]
+            counts = []
+            for s in range(half):
+                row = pl.ds(k * half + s, 1)
+                hit = weight + near[r, 0, row, :] == best[s]
+                counts.append(carry[s] + jnp.where(hit, near[r, 1, row, :], 0.0))
+            return tuple(counts)
+
+        start = (jnp.zeros((SPAN, LANES), jnp.float32),) * half
         counts = over_slots(dims, places, table, filled, PAIR * chip + h, step, start)
-        return jnp.sum(counts, axis=1, keepdims=True)
-
-    spans = range(0, LANES, SPAN)
-    items = [(h, s, q) for h in range(PAIR) for q in spans for s in range(half)]
+        return [jnp.sum(count, axis=1, keepdims=True) for count in counts]
 
     def columns(chip, _):
         rows = PAIR * half
         turned = {q: jnp.zeros((SPAN, LANES), jnp.float32) for q in spans}
         best = lowest(chip, 0)
-        for at, item in enumerate(items):
+        for at, (h, q) in enumerate(items):
             later = lowest(chip, at + 1) if at + 1 < len(items) else None
-            total = tally(chip, at, best)
-            h, s, q = item
-            to = h * half + s
-            with_total = jnp.where(lane == rows + to, total, turned[q])
-            turned[q] = jnp.where(lane == to, best, with_total)
+            totals = tally(chip, at, best)
+            for s in range(half):
+                to = h * half + s
+                with_total = jnp.where(lane == rows + to, totals[s], turned[q])
+                turned[q] = jnp.where(lane == to, best[s], with_total)
             best = later
         both = jnp.concatenate([turned[q] for q in spans], axis=0).T
         found[chip, 0] = both[:rows]
@@ -299,7 +303,6 @@
         scratch_shapes=[
             pltpu.VMEM((n_col, 2, PAIR * half, LANES), jnp.float32),
             pltpu.VMEM((chips, 2, PAIR * half, LANES), jnp.float32),
-            pltpu.VMEM((2, PAIR * n_col, SPAN, LANES), jnp.float32),
         ]
         + slot_scratch(dims),
         compiler_params=params(large_limit),
@@ -353,21 +356,24 @@
         count = low[chip, 1]
         share = jnp.where(count > 0.5, 1.0 / jnp.maximum(count, 1.0), 0.0)
         turned = jnp.concatenate([low[chip, 0], share], axis=0).T
-        for at, q in [(at, q) for at in range(rows) for q in range(0, LANES, SPAN)]:
-            c, s = PAIR * chip + at // half, at % half
+        for h, q in [(h, q) for h in range(PAIR) for q in range(0, LANES, SPAN)]:
             span = slice(q, q + SPAN)
-            dist = jnp.broadcast_to(turned[span, at : at + 1], (SPAN, LANES))
-            coef = jnp.broadcast_to(turned[span, rows + at : rows + at + 1], (SPAN, LANES))
+            wide = [
+                jnp.broadcast_to(turned[span, at : at + 1], (SPAN, LANES))
+                for first_row in (h * half, rows + h * half)
+                for at in range(first_row, first_row + half)
+            ]
 
             def step(k, g, r, carry):
-                row = near[r, 0, pl.ds(k * half + s, 1), :]
-                hit = tiles[k][g, pl.ds(q, SPAN), :] + row == dist
-                part = jnp.where(hit, coef, 0.0)
-                terms[(k * slots + g) * half + s, pl.ds(q, SPAN), :] = part
-                add_terms(k, r, s, part)
+                weight = tiles[k][g, pl.ds(q, SPAN), :]
+                for s in range(half):
+                    hit = weight + near[r, 0, pl.ds(k * half + s, 1), :] == wide[s]
+                    part = jnp.where(hit, wide[half + s], 0.0)
+                    terms[(k * slots + g) * half + s, pl.ds(q, SPAN), :] = part
+                    add_terms(k, r, s, part)
                 return carry
 
-            over_slots(dims, places, table, filled, c, step, 0)
+            over_slots(dims, places, table, filled, PAIR * chip + h, step, 0)
         return 0
 
     def scale(chip):

time: 60.1 us -> 60.1 us (level)
  no operation moved by 1% of the time
where the time goes in v10:
time: 60.1 us; the launch traced here: 59.8 us
  blocking collectives  49.6 us (83%)
  Pallas kernels  9 us (15%)
  between operations  0.66 us (1%)
    all_to_all x5, blocking collectives, all_to_all(): return lax.all_to_all(value, axes, split_axis=0, concat_axis=0, tiled=True)  49.6 us
    pallas_call x2, Pallas kernels, relax_level(): pl.pallas_call(functools.partial(relax_kernel, dims, counted, whole), out...  3.6 us
    pallas_call x2, Pallas kernels, depend_level(): pl.pallas_call(functools.partial(depend_kernel, dims, first, last), out_s...  3.16 us
    pallas_call x1, Pallas kernels, first_level(): pl.pallas_call(functools.partial(first_kernel, dims), out_shape=[piece(n_...  1.64 us
  transfers between devices with their start and end apart: 1, of which 0 were waited for; matrix products, arithmetic and copies ran while one was open for 0% of the time, Pallas kernels for 0%

profile of v10, /device:TPU:0, one launch (start us, length us, event | category | flops | bytes accessed | tf_op | source)
XLA Modules:
  0.0 59.8 jit_solution(2023593337101449704)
XLA Ops:
  0.6 1.6 %first_level.1 = (f32[16,8,128]{2,1,0:T(8,128)S(1)}, f32[16,128,128]{2,1,0:T(8,128)S(1)}, s32[8,128]{1,0:T(8,128)S(1)}) custom-call(s32[2,16]{1,0:T(2,128)} %bitcast.2, s32[8]{0:T(128)} %refs_1_.1, f32[16,128,128]{2,1,0:T(8,128)} %refs_2_.1), custom_call_target="tpu_custom_call" | custom-call | tf_op jit(solution)/shard_map/first_level/pallas_call | solution.py:148
  2.3 0.5 collective-permute-start
  2.8 13.4 %all_to_all.25.refs_3_ = f32[16,8,128]{2,1,0:T(8,128)S(1)} all-to-all(f32[16,8,128]{2,1,0:T(8,128)S(1)} %get-tuple-element.17), channel_id=1, replica_groups=mesh['groups'=2,'chip'=2,'core'=2,'col'=4] {'chip','core','col'}, dimensions={0} | all-to-all | bytes 131072 | tf_op jit(solution)/shard_map/all_to_all | solution.py:466
  16.2 0.0 collective-permute-done.refs_2_
  16.2 1.8 %relax_level.2 = f32[8,1,2,8,128]{4,3,2,1,0:T(8,128)S(1)} custom-call(s32[8,128]{1,0:T(8,128)S(1)} %get-tuple-element.15.refs_0_, f32[16,128,128]{2,1,0:T(8,128)S(1)} %get-tuple-element.16.refs_1_, f32[16,128,128]{2,1,0:T(8,128)S(1)} %collective-permute-done.refs_2_, f32[16,8,128]{2,1,0:T(8,128)S(1)} %all_to_all.25.refs_3_), custom_call_target="tpu_custom_call" | custom-call | tf_op jit(solution)/shard_map/relax_level/pallas_call | solution.py:298
  18.0 9.3 %all_to_all.26.refs_3_ = f32[8,1,2,8,128]{4,3,2,1,0:T(8,128)S(1)} all-to-all(f32[8,1,2,8,128]{4,3,2,1,0:T(8,128)S(1)} %relax_level.2), channel_id=1, replica_groups=mesh['groups'=2,'chip'=2,'core'=2,'col'=4] {'col','chip'}, dimensions={0} | all-to-all | bytes 131072 | tf_op jit(solution)/shard_map/all_to_all | solution.py:466
  27.3 1.8 %relax_level.3 = f32[8,2,2,8,128]{4,3,2,1,0:T(8,128)S(1)} custom-call(s32[8,128]{1,0:T(8,128)S(1)} %get-tuple-element.15.refs_0_, f32[16,128,128]{2,1,0:T(8,128)S(1)} %get-tuple-element.16.refs_1_, f32[16,128,128]{2,1,0:T(8,128)S(1)} %collective-permute-done.refs_2_, f32[8,1,2,8,128]{4,3,2,1,0:T(8,128)S(1)} %all_to_all.26.refs_3_), custom_call_target="tpu_custom_call" | custom-call | tf_op jit(solution)/shard_map/relax_level/pallas_call | solution.py:298
  29.1 9.7 %all_to_all.27.refs_3_ = f32[8,2,2,8,128]{4,3,2,1,0:T(8,128)S(1)} all-to-all(f32[8,2,2,8,128]{4,3,2,1,0:T(8,128)S(1)} %relax_level.3), channel_id=1, replica_groups=mesh['groups'=2,'chip'=2,'core'=2,'col'=4] {'col','chip'}, dimensions={0} | all-to-all | bytes 262144 | tf_op jit(solution)/shard_map/all_to_all | solution.py:466
  38.9 2.1 %depend_level.2 = (f32[16,8,128]{2,1,0:T(8,128)S(1)}, f32[4,2,8,128]{3,2,1,0:T(8,128)S(1)}, f32[2,2,8,128]{3,2,1,0:T(8,128)S(1)}, f32[128,128,128]{2,1,0:T(8,128)S(1)}) custom-call(s32[8,128]{1,0:T(8,128)S(1)} %get-tuple-element.15.refs_0_, f32[16,128,128]{2,1,0:T(8,128)S(1)} %get-tuple-element.16.refs_1_, f32[16,128,128]{2,1,0:T(8,128)S(1)} %collective-permute-done.refs_2_, ...), custom_call_target="tpu_custom_call" | custom-call | tf_op jit(solution)/shard_map/depend_level/pallas_call | solution.py:434
  41.0 9.2 %all_to_all.28.refs_4_ = f32[16,8,128]{2,1,0:T(8,128)S(1)} all-to-all(f32[16,8,128]{2,1,0:T(8,128)S(1)} %get-tuple-element.21), channel_id=1, replica_groups=mesh['groups'=2,'chip'=2,'core'=2,'col'=4] {'chip','core','col'}, dimensions={0} | all-to-all | bytes 131072 | tf_op jit(solution)/shard_map/all_to_all | solution.py:466
  50.2 1.0 %depend_level.3 = (f32[8,1,128]{2,1,0:T(1,128)S(1)}, f32[2,8,128]{2,1,0:T(8,128)S(1)}) custom-call(s32[8,128]{1,0:T(8,128)S(1)} %get-tuple-element.15.refs_0_, f32[4,2,8,128]{3,2,1,0:T(8,128)S(1)} %get-tuple-element.18.refs_1_, f32[2,2,8,128]{3,2,1,0:T(8,128)S(1)} %get-tuple-element.19.refs_2_, f32[128,128,128]{2,1,0:T(8,128)S(1)} %get-tuple-element.20.refs_3_, ...), custom_call_target="tpu_custom_call" | custom-call | tf_op jit(solution)/shard_map/depend_level/pallas_call | solution.py:434
  51.2 7.9 %all_to_all.29.came = f32[8,1,128]{2,1,0:T(1,128)S(1)} all-to-all(f32[8,1,128]{2,1,0:T(1,128)S(1)} %get-tuple-element.22), channel_id=1, replica_groups=mesh['groups'=2,'chip'=2,'core'=2,'col'=4] {'core','col'}, dimensions={0} | all-to-all | bytes 8192 | tf_op jit(solution)/shard_map/all_to_all | solution.py:466
  59.1 0.6 %results.1 = (f32[8,128]{1,0:T(8,128)}, f32[8,128]{1,0:T(8,128)}, f32[1,128]{1,0:T(1,128)}) custom-call(f32[8,1,128]{2,1,0:T(1,128)S(1)} %all_to_all.29.came, f32[2,8,128]{2,1,0:T(8,128)S(1)} %get-tuple-element.23.state), custom_call_target="tpu_custom_call" | custom-call | tf_op jit(solution)/shard_map/results/pallas_call | solution.py:455
Async XLA Ops:
  2.3 14.0 %collective-permute-start = (f32[16,128,128]{2,1,0:T(8,128)S(1)}, f32[16,128,128]{2,1,0:T(8,128)S(1)}, u32[]{:S(2)}, u32[]{:S(2)}) collective-permute-start(f32[16,128,128]{2,1,0:T(8,128)S(1)} %get-tuple-element.16.refs_1_), channel_id=1, source_target_pairs={{0,4},{4,0},{1,5},{5,1},{2,6},{6,2},{3,7},{7,3},{8,12},{12,8},{9,1... | collective-permute-start | bytes 3145736 | tf_op jit(solution)/shard_map/ppermute | solution.py:470

commit v11 on v10

--- a/solution.py
+++ b/solution.py
@@ -12,7 +12,7 @@
 LANES = 128
 SUB = 8
 PAIR = 2
-SPAN = 32
+SPAN = 16
 
 far_value = 1000000.0
 no_edge = 2000000.0
@@ -356,21 +356,16 @@
         count = low[chip, 1]
         share = jnp.where(count > 0.5, 1.0 / jnp.maximum(count, 1.0), 0.0)
         turned = jnp.concatenate([low[chip, 0], share], axis=0).T
-        for h, q in [(h, q) for h in range(PAIR) for q in range(0, LANES, SPAN)]:
-            span = slice(q, q + SPAN)
-            wide = [
-                jnp.broadcast_to(turned[span, at : at + 1], (SPAN, LANES))
-                for first_row in (h * half, rows + h * half)
-                for at in range(first_row, first_row + half)
-            ]
+        for at in range(rows):
+            h, s = at // half, at % half
+            dist = jnp.broadcast_to(turned[:, at : at + 1], (LANES, LANES))
+            coef = jnp.broadcast_to(turned[:, rows + at : rows + at + 1], (LANES, LANES))
 
             def step(k, g, r, carry):
-                weight = tiles[k][g, pl.ds(q, SPAN), :]
-                for s in range(half):
-                    hit = weight + near[r, 0, pl.ds(k * half + s, 1), :] == wide[s]
-                    part = jnp.where(hit, wide[half + s], 0.0)
-                    terms[(k * slots + g) * half + s, pl.ds(q, SPAN), :] = part
-                    add_terms(k, r, s, part)
+                hit = tiles[k][g] + near[r, 0, pl.ds(k * half + s, 1), :] == dist
+                part = jnp.where(hit, coef, 0.0)
+                terms[(k * slots + g) * half + s] = part
+                add_terms(k, r, s, part)
                 return carry
 
             over_slots(dims, places, table, filled, PAIR * chip + h, step, 0)

time: 60.1 us -> 59.9 us (level)
  no operation moved by 1% of the time
where the time goes in v11:
time: 59.9 us; the launch traced here: 59.5 us
  blocking collectives  49.6 us (83%)
  Pallas kernels  8.79 us (15%)
  between operations  0.66 us (1%)
    all_to_all x5, blocking collectives, all_to_all(): return lax.all_to_all(value, axes, split_axis=0, concat_axis=0, tiled=True)  49.6 us
    pallas_call x2, Pallas kernels, relax_level(): pl.pallas_call(functools.partial(relax_kernel, dims, counted, whole), out...  3.63 us
    pallas_call x2, Pallas kernels, depend_level(): pl.pallas_call(functools.partial(depend_kernel, dims, first, last), out_s...  2.92 us
    pallas_call x1, Pallas kernels, first_level(): pl.pallas_call(functools.partial(first_kernel, dims), out_shape=[piece(n_...  1.64 us
  transfers between devices with their start and end apart: 1, of which 0 were waited for; matrix products, arithmetic and copies ran while one was open for 0% of the time, Pallas kernels for 0%

profile of v11, /device:TPU:0, one launch (start us, length us, event | category | flops | bytes accessed | tf_op | source)
XLA Modules:
  0.0 59.5 jit_solution(9425606103153595034)
XLA Ops:
  0.6 1.6 %first_level.1 = (f32[16,8,128]{2,1,0:T(8,128)S(1)}, f32[16,128,128]{2,1,0:T(8,128)S(1)}, s32[8,128]{1,0:T(8,128)S(1)}) custom-call(s32[2,16]{1,0:T(2,128)} %bitcast.2, s32[8]{0:T(128)} %refs_1_.1, f32[16,128,128]{2,1,0:T(8,128)} %refs_2_.1), custom_call_target="tpu_custom_call" | custom-call | tf_op jit(solution)/shard_map/first_level/pallas_call | solution.py:148
  2.3 0.5 collective-permute-start
  2.8 13.4 %all_to_all.25.refs_3_ = f32[16,8,128]{2,1,0:T(8,128)S(1)} all-to-all(f32[16,8,128]{2,1,0:T(8,128)S(1)} %get-tuple-element.17), channel_id=1, replica_groups=mesh['groups'=2,'chip'=2,'core'=2,'col'=4] {'chip','core','col'}, dimensions={0} | all-to-all | bytes 131072 | tf_op jit(solution)/shard_map/all_to_all | solution.py:461
  16.2 0.0 collective-permute-done.refs_2_
  16.2 1.8 %relax_level.2 = f32[8,1,2,8,128]{4,3,2,1,0:T(8,128)S(1)} custom-call(s32[8,128]{1,0:T(8,128)S(1)} %get-tuple-element.15.refs_0_, f32[16,128,128]{2,1,0:T(8,128)S(1)} %get-tuple-element.16.refs_1_, f32[16,128,128]{2,1,0:T(8,128)S(1)} %collective-permute-done.refs_2_, f32[16,8,128]{2,1,0:T(8,128)S(1)} %all_to_all.25.refs_3_), custom_call_target="tpu_custom_call" | custom-call | tf_op jit(solution)/shard_map/relax_level/pallas_call | solution.py:298
  18.1 9.3 %all_to_all.26.refs_3_ = f32[8,1,2,8,128]{4,3,2,1,0:T(8,128)S(1)} all-to-all(f32[8,1,2,8,128]{4,3,2,1,0:T(8,128)S(1)} %relax_level.2), channel_id=1, replica_groups=mesh['groups'=2,'chip'=2,'core'=2,'col'=4] {'col','chip'}, dimensions={0} | all-to-all | bytes 131072 | tf_op jit(solution)/shard_map/all_to_all | solution.py:461
  27.3 1.8 %relax_level.3 = f32[8,2,2,8,128]{4,3,2,1,0:T(8,128)S(1)} custom-call(s32[8,128]{1,0:T(8,128)S(1)} %get-tuple-element.15.refs_0_, f32[16,128,128]{2,1,0:T(8,128)S(1)} %get-tuple-element.16.refs_1_, f32[16,128,128]{2,1,0:T(8,128)S(1)} %collective-permute-done.refs_2_, f32[8,1,2,8,128]{4,3,2,1,0:T(8,128)S(1)} %all_to_all.26.refs_3_), custom_call_target="tpu_custom_call" | custom-call | tf_op jit(solution)/shard_map/relax_level/pallas_call | solution.py:298
  29.2 9.7 %all_to_all.27.refs_3_ = f32[8,2,2,8,128]{4,3,2,1,0:T(8,128)S(1)} all-to-all(f32[8,2,2,8,128]{4,3,2,1,0:T(8,128)S(1)} %relax_level.3), channel_id=1, replica_groups=mesh['groups'=2,'chip'=2,'core'=2,'col'=4] {'col','chip'}, dimensions={0} | all-to-all | bytes 262144 | tf_op jit(solution)/shard_map/all_to_all | solution.py:461
  38.9 1.9 %depend_level.2 = (f32[16,8,128]{2,1,0:T(8,128)S(1)}, f32[4,2,8,128]{3,2,1,0:T(8,128)S(1)}, f32[2,2,8,128]{3,2,1,0:T(8,128)S(1)}, f32[128,128,128]{2,1,0:T(8,128)S(1)}) custom-call(s32[8,128]{1,0:T(8,128)S(1)} %get-tuple-element.15.refs_0_, f32[16,128,128]{2,1,0:T(8,128)S(1)} %get-tuple-element.16.refs_1_, f32[16,128,128]{2,1,0:T(8,128)S(1)} %collective-permute-done.refs_2_, ...), custom_call_target="tpu_custom_call" | custom-call | tf_op jit(solution)/shard_map/depend_level/pallas_call | solution.py:429
  40.8 9.2 %all_to_all.28.refs_4_ = f32[16,8,128]{2,1,0:T(8,128)S(1)} all-to-all(f32[16,8,128]{2,1,0:T(8,128)S(1)} %get-tuple-element.21), channel_id=1, replica_groups=mesh['groups'=2,'chip'=2,'core'=2,'col'=4] {'chip','core','col'}, dimensions={0} | all-to-all | bytes 131072 | tf_op jit(solution)/shard_map/all_to_all | solution.py:461
  50.0 1.0 %depend_level.3 = (f32[8,1,128]{2,1,0:T(1,128)S(1)}, f32[2,8,128]{2,1,0:T(8,128)S(1)}) custom-call(s32[8,128]{1,0:T(8,128)S(1)} %get-tuple-element.15.refs_0_, f32[4,2,8,128]{3,2,1,0:T(8,128)S(1)} %get-tuple-element.18.refs_1_, f32[2,2,8,128]{3,2,1,0:T(8,128)S(1)} %get-tuple-element.19.refs_2_, f32[128,128,128]{2,1,0:T(8,128)S(1)} %get-tuple-element.20.refs_3_, ...), custom_call_target="tpu_custom_call" | custom-call | tf_op jit(solution)/shard_map/depend_level/pallas_call | solution.py:429
  51.0 7.9 %all_to_all.29.came = f32[8,1,128]{2,1,0:T(1,128)S(1)} all-to-all(f32[8,1,128]{2,1,0:T(1,128)S(1)} %get-tuple-element.22), channel_id=1, replica_groups=mesh['groups'=2,'chip'=2,'core'=2,'col'=4] {'core','col'}, dimensions={0} | all-to-all | bytes 8192 | tf_op jit(solution)/shard_map/all_to_all | solution.py:461
  58.9 0.6 %results.1 = (f32[8,128]{1,0:T(8,128)}, f32[8,128]{1,0:T(8,128)}, f32[1,128]{1,0:T(1,128)}) custom-call(f32[8,1,128]{2,1,0:T(1,128)S(1)} %all_to_all.29.came, f32[2,8,128]{2,1,0:T(8,128)S(1)} %get-tuple-element.23.state), custom_call_target="tpu_custom_call" | custom-call | tf_op jit(solution)/shard_map/results/pallas_call | solution.py:450
Async XLA Ops:
  2.3 14.0 %collective-permute-start = (f32[16,128,128]{2,1,0:T(8,128)S(1)}, f32[16,128,128]{2,1,0:T(8,128)S(1)}, u32[]{:S(2)}, u32[]{:S(2)}) collective-permute-start(f32[16,128,128]{2,1,0:T(8,128)S(1)} %get-tuple-element.16.refs_1_), channel_id=1, source_target_pairs={{0,4},{4,0},{1,5},{5,1},{2,6},{6,2},{3,7},{7,3},{8,12},{12,8},{9,1... | collective-permute-start | bytes 3145736 | tf_op jit(solution)/shard_map/ppermute | solution.py:465

commit v12 on v11

--- a/solution.py
+++ b/solution.py
@@ -12,7 +12,7 @@
 LANES = 128
 SUB = 8
 PAIR = 2
-SPAN = 16
+SPAN = 32
 
 far_value = 1000000.0
 no_edge = 2000000.0
@@ -143,7 +143,7 @@
 
 def first_level(dims, places, sources, tiles):
     n_row, n_col, slots, half = dims
-    parts = 4 if slots % 4 == 0 else 1
+    parts = 8 if slots % 8 == 0 else 1
     inputs = [pltpu.with_memory_space_constraint(x, pltpu.HBM) for x in (places, sources, tiles)]
     return pl.pallas_call(
         functools.partial(first_kernel, dims),

time: 59.9 us -> 60.1 us (level)
  no operation moved by 1% of the time
where the time goes in v12:
time: 60.1 us; the launch traced here: 59.8 us
  blocking collectives  49.6 us (83%)
  Pallas kernels  9.07 us (15%)
  between operations  0.66 us (1%)
    all_to_all x5, blocking collectives, all_to_all(): return lax.all_to_all(value, axes, split_axis=0, concat_axis=0, tiled=True)  49.6 us
    pallas_call x2, Pallas kernels, relax_level(): pl.pallas_call(functools.partial(relax_kernel, dims, counted, whole), out...  3.6 us
    pallas_call x2, Pallas kernels, depend_level(): pl.pallas_call(functools.partial(depend_kernel, dims, first, last), out_s...  2.92 us
    pallas_call x1, Pallas kernels, first_level(): pl.pallas_call(functools.partial(first_kernel, dims), out_shape=[piece(n_...  1.95 us
  transfers between devices with their start and end apart: 1, of which 0 were waited for; matrix products, arithmetic and copies ran while one was open for 0% of the time, Pallas kernels for 0%

profile of v12, /device:TPU:0, one launch (start us, length us, event | category | flops | bytes accessed | tf_op | source)
XLA Modules:
  0.0 59.8 jit_solution(17721484619929682643)
XLA Ops:
  0.6 1.9 %first_level.1 = (f32[16,8,128]{2,1,0:T(8,128)S(1)}, f32[16,128,128]{2,1,0:T(8,128)S(1)}, s32[8,128]{1,0:T(8,128)S(1)}) custom-call(s32[2,16]{1,0:T(2,128)} %bitcast.2, s32[8]{0:T(128)} %refs_1_.1, f32[16,128,128]{2,1,0:T(8,128)} %refs_2_.1), custom_call_target="tpu_custom_call" | custom-call | tf_op jit(solution)/shard_map/first_level/pallas_call | solution.py:148
  2.6 0.5 collective-permute-start
  3.1 13.4 %all_to_all.25.refs_3_ = f32[16,8,128]{2,1,0:T(8,128)S(1)} all-to-all(f32[16,8,128]{2,1,0:T(8,128)S(1)} %get-tuple-element.17), channel_id=1, replica_groups=mesh['groups'=2,'chip'=2,'core'=2,'col'=4] {'chip','core','col'}, dimensions={0} | all-to-all | bytes 131072 | tf_op jit(solution)/shard_map/all_to_all | solution.py:461
  16.5 0.0 collective-permute-done.refs_2_
  16.5 1.8 %relax_level.2 = f32[8,1,2,8,128]{4,3,2,1,0:T(8,128)S(1)} custom-call(s32[8,128]{1,0:T(8,128)S(1)} %get-tuple-element.15.refs_0_, f32[16,128,128]{2,1,0:T(8,128)S(1)} %get-tuple-element.16.refs_1_, f32[16,128,128]{2,1,0:T(8,128)S(1)} %collective-permute-done.refs_2_, f32[16,8,128]{2,1,0:T(8,128)S(1)} %all_to_all.25.refs_3_), custom_call_target="tpu_custom_call" | custom-call | tf_op jit(solution)/shard_map/relax_level/pallas_call | solution.py:298
  18.3 9.3 %all_to_all.26.refs_3_ = f32[8,1,2,8,128]{4,3,2,1,0:T(8,128)S(1)} all-to-all(f32[8,1,2,8,128]{4,3,2,1,0:T(8,128)S(1)} %relax_level.2), channel_id=1, replica_groups=mesh['groups'=2,'chip'=2,'core'=2,'col'=4] {'col','chip'}, dimensions={0} | all-to-all | bytes 131072 | tf_op jit(solution)/shard_map/all_to_all | solution.py:461
  27.6 1.8 %relax_level.3 = f32[8,2,2,8,128]{4,3,2,1,0:T(8,128)S(1)} custom-call(s32[8,128]{1,0:T(8,128)S(1)} %get-tuple-element.15.refs_0_, f32[16,128,128]{2,1,0:T(8,128)S(1)} %get-tuple-element.16.refs_1_, f32[16,128,128]{2,1,0:T(8,128)S(1)} %collective-permute-done.refs_2_, f32[8,1,2,8,128]{4,3,2,1,0:T(8,128)S(1)} %all_to_all.26.refs_3_), custom_call_target="tpu_custom_call" | custom-call | tf_op jit(solution)/shard_map/relax_level/pallas_call | solution.py:298
  29.4 9.7 %all_to_all.27.refs_3_ = f32[8,2,2,8,128]{4,3,2,1,0:T(8,128)S(1)} all-to-all(f32[8,2,2,8,128]{4,3,2,1,0:T(8,128)S(1)} %relax_level.3), channel_id=1, replica_groups=mesh['groups'=2,'chip'=2,'core'=2,'col'=4] {'col','chip'}, dimensions={0} | all-to-all | bytes 262144 | tf_op jit(solution)/shard_map/all_to_all | solution.py:461
  39.2 1.9 %depend_level.2 = (f32[16,8,128]{2,1,0:T(8,128)S(1)}, f32[4,2,8,128]{3,2,1,0:T(8,128)S(1)}, f32[2,2,8,128]{3,2,1,0:T(8,128)S(1)}, f32[128,128,128]{2,1,0:T(8,128)S(1)}) custom-call(s32[8,128]{1,0:T(8,128)S(1)} %get-tuple-element.15.refs_0_, f32[16,128,128]{2,1,0:T(8,128)S(1)} %get-tuple-element.16.refs_1_, f32[16,128,128]{2,1,0:T(8,128)S(1)} %collective-permute-done.refs_2_, ...), custom_call_target="tpu_custom_call" | custom-call | tf_op jit(solution)/shard_map/depend_level/pallas_call | solution.py:429
  41.1 9.2 %all_to_all.28.refs_4_ = f32[16,8,128]{2,1,0:T(8,128)S(1)} all-to-all(f32[16,8,128]{2,1,0:T(8,128)S(1)} %get-tuple-element.21), channel_id=1, replica_groups=mesh['groups'=2,'chip'=2,'core'=2,'col'=4] {'chip','core','col'}, dimensions={0} | all-to-all | bytes 131072 | tf_op jit(solution)/shard_map/all_to_all | solution.py:461
  50.3 1.0 %depend_level.3 = (f32[8,1,128]{2,1,0:T(1,128)S(1)}, f32[2,8,128]{2,1,0:T(8,128)S(1)}) custom-call(s32[8,128]{1,0:T(8,128)S(1)} %get-tuple-element.15.refs_0_, f32[4,2,8,128]{3,2,1,0:T(8,128)S(1)} %get-tuple-element.18.refs_1_, f32[2,2,8,128]{3,2,1,0:T(8,128)S(1)} %get-tuple-element.19.refs_2_, f32[128,128,128]{2,1,0:T(8,128)S(1)} %get-tuple-element.20.refs_3_, ...), custom_call_target="tpu_custom_call" | custom-call | tf_op jit(solution)/shard_map/depend_level/pallas_call | solution.py:429
  51.3 7.9 %all_to_all.29.came = f32[8,1,128]{2,1,0:T(1,128)S(1)} all-to-all(f32[8,1,128]{2,1,0:T(1,128)S(1)} %get-tuple-element.22), channel_id=1, replica_groups=mesh['groups'=2,'chip'=2,'core'=2,'col'=4] {'core','col'}, dimensions={0} | all-to-all | bytes 8192 | tf_op jit(solution)/shard_map/all_to_all | solution.py:461
  59.2 0.6 %results.1 = (f32[8,128]{1,0:T(8,128)}, f32[8,128]{1,0:T(8,128)}, f32[1,128]{1,0:T(1,128)}) custom-call(f32[8,1,128]{2,1,0:T(1,128)S(1)} %all_to_all.29.came, f32[2,8,128]{2,1,0:T(8,128)S(1)} %get-tuple-element.23.state), custom_call_target="tpu_custom_call" | custom-call | tf_op jit(solution)/shard_map/results/pallas_call | solution.py:450
Async XLA Ops:
  2.6 14.0 %collective-permute-start = (f32[16,128,128]{2,1,0:T(8,128)S(1)}, f32[16,128,128]{2,1,0:T(8,128)S(1)}, u32[]{:S(2)}, u32[]{:S(2)}) collective-permute-start(f32[16,128,128]{2,1,0:T(8,128)S(1)} %get-tuple-element.16.refs_1_), channel_id=1, source_target_pairs={{0,4},{4,0},{1,5},{5,1},{2,6},{6,2},{3,7},{7,3},{8,12},{12,8},{9,1... | collective-permute-start | bytes 3145736 | tf_op jit(solution)/shard_map/ppermute | solution.py:465

commit v13 on v12

--- a/solution.py
+++ b/solution.py
@@ -143,7 +143,7 @@
 
 def first_level(dims, places, sources, tiles):
     n_row, n_col, slots, half = dims
-    parts = 8 if slots % 8 == 0 else 1
+    parts = 2 if slots % 2 == 0 else 1
     inputs = [pltpu.with_memory_space_constraint(x, pltpu.HBM) for x in (places, sources, tiles)]
     return pl.pallas_call(
         functools.partial(first_kernel, dims),

time: 60.1 us -> 59.7 us (level)
  no operation moved by 1% of the time
where the time goes in v13:
time: 59.7 us; the launch traced here: 59.4 us
  blocking collectives  49.6 us (83%)
  Pallas kernels  8.68 us (15%)
  between operations  0.66 us (1%)
    all_to_all x5, blocking collectives, all_to_all(): return lax.all_to_all(value, axes, split_axis=0, concat_axis=0, tiled=True)  49.6 us
    pallas_call x2, Pallas kernels, relax_level(): pl.pallas_call(functools.partial(relax_kernel, dims, counted, whole), out...  3.6 us
    pallas_call x2, Pallas kernels, depend_level(): pl.pallas_call(functools.partial(depend_kernel, dims, first, last), out_s...  2.92 us
    pallas_call x1, Pallas kernels, first_level(): pl.pallas_call(functools.partial(first_kernel, dims), out_shape=[piece(n_...  1.56 us
  transfers between devices with their start and end apart: 1, of which 0 were waited for; matrix products, arithmetic and copies ran while one was open for 0% of the time, Pallas kernels for 0%

profile of v13, /device:TPU:0, one launch (start us, length us, event | category | flops | bytes accessed | tf_op | source)
XLA Modules:
  0.0 59.4 jit_solution(17229636510190946343)
XLA Ops:
  0.6 1.6 %first_level.1 = (f32[16,8,128]{2,1,0:T(8,128)S(1)}, f32[16,128,128]{2,1,0:T(8,128)S(1)}, s32[8,128]{1,0:T(8,128)S(1)}) custom-call(s32[2,16]{1,0:T(2,128)} %bitcast.2, s32[8]{0:T(128)} %refs_1_.1, f32[16,128,128]{2,1,0:T(8,128)} %refs_2_.1), custom_call_target="tpu_custom_call" | custom-call | tf_op jit(solution)/shard_map/first_level/pallas_call | solution.py:148
  2.2 0.5 collective-permute-start
  2.7 13.4 %all_to_all.25.refs_3_ = f32[16,8,128]{2,1,0:T(8,128)S(1)} all-to-all(f32[16,8,128]{2,1,0:T(8,128)S(1)} %get-tuple-element.17), channel_id=1, replica_groups=mesh['groups'=2,'chip'=2,'core'=2,'col'=4] {'chip','core','col'}, dimensions={0} | all-to-all | bytes 131072 | tf_op jit(solution)/shard_map/all_to_all | solution.py:461
  16.2 0.0 collective-permute-done.refs_2_
  16.2 1.8 %relax_level.2 = f32[8,1,2,8,128]{4,3,2,1,0:T(8,128)S(1)} custom-call(s32[8,128]{1,0:T(8,128)S(1)} %get-tuple-element.15.refs_0_, f32[16,128,128]{2,1,0:T(8,128)S(1)} %get-tuple-element.16.refs_1_, f32[16,128,128]{2,1,0:T(8,128)S(1)} %collective-permute-done.refs_2_, f32[16,8,128]{2,1,0:T(8,128)S(1)} %all_to_all.25.refs_3_), custom_call_target="tpu_custom_call" | custom-call | tf_op jit(solution)/shard_map/relax_level/pallas_call | solution.py:298
  18.0 9.3 %all_to_all.26.refs_3_ = f32[8,1,2,8,128]{4,3,2,1,0:T(8,128)S(1)} all-to-all(f32[8,1,2,8,128]{4,3,2,1,0:T(8,128)S(1)} %relax_level.2), channel_id=1, replica_groups=mesh['groups'=2,'chip'=2,'core'=2,'col'=4] {'col','chip'}, dimensions={0} | all-to-all | bytes 131072 | tf_op jit(solution)/shard_map/all_to_all | solution.py:461
  27.2 1.8 %relax_level.3 = f32[8,2,2,8,128]{4,3,2,1,0:T(8,128)S(1)} custom-call(s32[8,128]{1,0:T(8,128)S(1)} %get-tuple-element.15.refs_0_, f32[16,128,128]{2,1,0:T(8,128)S(1)} %get-tuple-element.16.refs_1_, f32[16,128,128]{2,1,0:T(8,128)S(1)} %collective-permute-done.refs_2_, f32[8,1,2,8,128]{4,3,2,1,0:T(8,128)S(1)} %all_to_all.26.refs_3_), custom_call_target="tpu_custom_call" | custom-call | tf_op jit(solution)/shard_map/relax_level/pallas_call | solution.py:298
  29.0 9.7 %all_to_all.27.refs_3_ = f32[8,2,2,8,128]{4,3,2,1,0:T(8,128)S(1)} all-to-all(f32[8,2,2,8,128]{4,3,2,1,0:T(8,128)S(1)} %relax_level.3), channel_id=1, replica_groups=mesh['groups'=2,'chip'=2,'core'=2,'col'=4] {'col','chip'}, dimensions={0} | all-to-all | bytes 262144 | tf_op jit(solution)/shard_map/all_to_all | solution.py:461
  38.8 1.9 %depend_level.2 = (f32[16,8,128]{2,1,0:T(8,128)S(1)}, f32[4,2,8,128]{3,2,1,0:T(8,128)S(1)}, f32[2,2,8,128]{3,2,1,0:T(8,128)S(1)}, f32[128,128,128]{2,1,0:T(8,128)S(1)}) custom-call(s32[8,128]{1,0:T(8,128)S(1)} %get-tuple-element.15.refs_0_, f32[16,128,128]{2,1,0:T(8,128)S(1)} %get-tuple-element.16.refs_1_, f32[16,128,128]{2,1,0:T(8,128)S(1)} %collective-permute-done.refs_2_, ...), custom_call_target="tpu_custom_call" | custom-call | tf_op jit(solution)/shard_map/depend_level/pallas_call | solution.py:429
  40.7 9.2 %all_to_all.28.refs_4_ = f32[16,8,128]{2,1,0:T(8,128)S(1)} all-to-all(f32[16,8,128]{2,1,0:T(8,128)S(1)} %get-tuple-element.21), channel_id=1, replica_groups=mesh['groups'=2,'chip'=2,'core'=2,'col'=4] {'chip','core','col'}, dimensions={0} | all-to-all | bytes 131072 | tf_op jit(solution)/shard_map/all_to_all | solution.py:461
  49.9 1.0 %depend_level.3 = (f32[8,1,128]{2,1,0:T(1,128)S(1)}, f32[2,8,128]{2,1,0:T(8,128)S(1)}) custom-call(s32[8,128]{1,0:T(8,128)S(1)} %get-tuple-element.15.refs_0_, f32[4,2,8,128]{3,2,1,0:T(8,128)S(1)} %get-tuple-element.18.refs_1_, f32[2,2,8,128]{3,2,1,0:T(8,128)S(1)} %get-tuple-element.19.refs_2_, f32[128,128,128]{2,1,0:T(8,128)S(1)} %get-tuple-element.20.refs_3_, ...), custom_call_target="tpu_custom_call" | custom-call | tf_op jit(solution)/shard_map/depend_level/pallas_call | solution.py:429
  50.9 7.9 %all_to_all.29.came = f32[8,1,128]{2,1,0:T(1,128)S(1)} all-to-all(f32[8,1,128]{2,1,0:T(1,128)S(1)} %get-tuple-element.22), channel_id=1, replica_groups=mesh['groups'=2,'chip'=2,'core'=2,'col'=4] {'core','col'}, dimensions={0} | all-to-all | bytes 8192 | tf_op jit(solution)/shard_map/all_to_all | solution.py:461
  58.8 0.6 %results.1 = (f32[8,128]{1,0:T(8,128)}, f32[8,128]{1,0:T(8,128)}, f32[1,128]{1,0:T(1,128)}) custom-call(f32[8,1,128]{2,1,0:T(1,128)S(1)} %all_to_all.29.came, f32[2,8,128]{2,1,0:T(8,128)S(1)} %get-tuple-element.23.state), custom_call_target="tpu_custom_call" | custom-call | tf_op jit(solution)/shard_map/results/pallas_call | solution.py:450
Async XLA Ops:
  2.2 14.0 %collective-permute-start = (f32[16,128,128]{2,1,0:T(8,128)S(1)}, f32[16,128,128]{2,1,0:T(8,128)S(1)}, u32[]{:S(2)}, u32[]{:S(2)}) collective-permute-start(f32[16,128,128]{2,1,0:T(8,128)S(1)} %get-tuple-element.16.refs_1_), channel_id=1, source_target_pairs={{0,4},{4,0},{1,5},{5,1},{2,6},{6,2},{3,7},{7,3},{8,12},{12,8},{9,1... | collective-permute-start | bytes 3145736 | tf_op jit(solution)/shard_map/ppermute | solution.py:465

commit v14 on v13

--- a/solution.py
+++ b/solution.py
@@ -143,7 +143,7 @@
 
 def first_level(dims, places, sources, tiles):
     n_row, n_col, slots, half = dims
-    parts = 2 if slots % 2 == 0 else 1
+    parts = 1
     inputs = [pltpu.with_memory_space_constraint(x, pltpu.HBM) for x in (places, sources, tiles)]
     return pl.pallas_call(
         functools.partial(first_kernel, dims),

time: 59.7 us -> 59.9 us (level)
  no operation moved by 1% of the time
where the time goes in v14:
time: 59.9 us; the launch traced here: 59.5 us
  blocking collectives  49.6 us (83%)
  Pallas kernels  8.79 us (15%)
  between operations  0.66 us (1%)
    all_to_all x5, blocking collectives, all_to_all(): return lax.all_to_all(value, axes, split_axis=0, concat_axis=0, tiled=True)  49.6 us
    pallas_call x2, Pallas kernels, relax_level(): pl.pallas_call(functools.partial(relax_kernel, dims, counted, whole), out...  3.6 us
    pallas_call x2, Pallas kernels, depend_level(): pl.pallas_call(functools.partial(depend_kernel, dims, first, last), out_s...  2.92 us
    pallas_call x1, Pallas kernels, first_level(): pl.pallas_call(functools.partial(first_kernel, dims), out_shape=[piece(n_...  1.67 us
  transfers between devices with their start and end apart: 1, of which 0 were waited for; matrix products, arithmetic and copies ran while one was open for 0% of the time, Pallas kernels for 0%

profile of v14, /device:TPU:0, one launch (start us, length us, event | category | flops | bytes accessed | tf_op | source)
XLA Modules:
  0.0 59.5 jit_solution(16637279281605191426)
XLA Ops:
  0.6 1.7 %first_level.1 = (f32[16,8,128]{2,1,0:T(8,128)S(1)}, f32[16,128,128]{2,1,0:T(8,128)S(1)}, s32[8,128]{1,0:T(8,128)S(1)}) custom-call(s32[2,16]{1,0:T(2,128)} %bitcast.2, s32[8]{0:T(128)} %refs_1_.1, f32[16,128,128]{2,1,0:T(8,128)} %refs_2_.1), custom_call_target="tpu_custom_call" | custom-call | tf_op jit(solution)/shard_map/first_level/pallas_call | solution.py:148
  2.3 0.5 collective-permute-start
  2.8 13.4 %all_to_all.25.refs_3_ = f32[16,8,128]{2,1,0:T(8,128)S(1)} all-to-all(f32[16,8,128]{2,1,0:T(8,128)S(1)} %get-tuple-element.17), channel_id=1, replica_groups=mesh['groups'=2,'chip'=2,'core'=2,'col'=4] {'chip','core','col'}, dimensions={0} | all-to-all | bytes 131072 | tf_op jit(solution)/shard_map/all_to_all | solution.py:461
  16.3 0.0 collective-permute-done.refs_2_
  16.3 1.8 %relax_level.2 = f32[8,1,2,8,128]{4,3,2,1,0:T(8,128)S(1)} custom-call(s32[8,128]{1,0:T(8,128)S(1)} %get-tuple-element.15.refs_0_, f32[16,128,128]{2,1,0:T(8,128)S(1)} %get-tuple-element.16.refs_1_, f32[16,128,128]{2,1,0:T(8,128)S(1)} %collective-permute-done.refs_2_, f32[16,8,128]{2,1,0:T(8,128)S(1)} %all_to_all.25.refs_3_), custom_call_target="tpu_custom_call" | custom-call | tf_op jit(solution)/shard_map/relax_level/pallas_call | solution.py:298
  18.1 9.3 %all_to_all.26.refs_3_ = f32[8,1,2,8,128]{4,3,2,1,0:T(8,128)S(1)} all-to-all(f32[8,1,2,8,128]{4,3,2,1,0:T(8,128)S(1)} %relax_level.2), channel_id=1, replica_groups=mesh['groups'=2,'chip'=2,'core'=2,'col'=4] {'col','chip'}, dimensions={0} | all-to-all | bytes 131072 | tf_op jit(solution)/shard_map/all_to_all | solution.py:461
  27.3 1.8 %relax_level.3 = f32[8,2,2,8,128]{4,3,2,1,0:T(8,128)S(1)} custom-call(s32[8,128]{1,0:T(8,128)S(1)} %get-tuple-element.15.refs_0_, f32[16,128,128]{2,1,0:T(8,128)S(1)} %get-tuple-element.16.refs_1_, f32[16,128,128]{2,1,0:T(8,128)S(1)} %collective-permute-done.refs_2_, f32[8,1,2,8,128]{4,3,2,1,0:T(8,128)S(1)} %all_to_all.26.refs_3_), custom_call_target="tpu_custom_call" | custom-call | tf_op jit(solution)/shard_map/relax_level/pallas_call | solution.py:298
  29.2 9.7 %all_to_all.27.refs_3_ = f32[8,2,2,8,128]{4,3,2,1,0:T(8,128)S(1)} all-to-all(f32[8,2,2,8,128]{4,3,2,1,0:T(8,128)S(1)} %relax_level.3), channel_id=1, replica_groups=mesh['groups'=2,'chip'=2,'core'=2,'col'=4] {'col','chip'}, dimensions={0} | all-to-all | bytes 262144 | tf_op jit(solution)/shard_map/all_to_all | solution.py:461
  38.9 1.9 %depend_level.2 = (f32[16,8,128]{2,1,0:T(8,128)S(1)}, f32[4,2,8,128]{3,2,1,0:T(8,128)S(1)}, f32[2,2,8,128]{3,2,1,0:T(8,128)S(1)}, f32[128,128,128]{2,1,0:T(8,128)S(1)}) custom-call(s32[8,128]{1,0:T(8,128)S(1)} %get-tuple-element.15.refs_0_, f32[16,128,128]{2,1,0:T(8,128)S(1)} %get-tuple-element.16.refs_1_, f32[16,128,128]{2,1,0:T(8,128)S(1)} %collective-permute-done.refs_2_, ...), custom_call_target="tpu_custom_call" | custom-call | tf_op jit(solution)/shard_map/depend_level/pallas_call | solution.py:429
  40.8 9.2 %all_to_all.28.refs_4_ = f32[16,8,128]{2,1,0:T(8,128)S(1)} all-to-all(f32[16,8,128]{2,1,0:T(8,128)S(1)} %get-tuple-element.21), channel_id=1, replica_groups=mesh['groups'=2,'chip'=2,'core'=2,'col'=4] {'chip','core','col'}, dimensions={0} | all-to-all | bytes 131072 | tf_op jit(solution)/shard_map/all_to_all | solution.py:461
  50.0 1.0 %depend_level.3 = (f32[8,1,128]{2,1,0:T(1,128)S(1)}, f32[2,8,128]{2,1,0:T(8,128)S(1)}) custom-call(s32[8,128]{1,0:T(8,128)S(1)} %get-tuple-element.15.refs_0_, f32[4,2,8,128]{3,2,1,0:T(8,128)S(1)} %get-tuple-element.18.refs_1_, f32[2,2,8,128]{3,2,1,0:T(8,128)S(1)} %get-tuple-element.19.refs_2_, f32[128,128,128]{2,1,0:T(8,128)S(1)} %get-tuple-element.20.refs_3_, ...), custom_call_target="tpu_custom_call" | custom-call | tf_op jit(solution)/shard_map/depend_level/pallas_call | solution.py:429
  51.0 7.9 %all_to_all.29.came = f32[8,1,128]{2,1,0:T(1,128)S(1)} all-to-all(f32[8,1,128]{2,1,0:T(1,128)S(1)} %get-tuple-element.22), channel_id=1, replica_groups=mesh['groups'=2,'chip'=2,'core'=2,'col'=4] {'core','col'}, dimensions={0} | all-to-all | bytes 8192 | tf_op jit(solution)/shard_map/all_to_all | solution.py:461
  58.9 0.6 %results.1 = (f32[8,128]{1,0:T(8,128)}, f32[8,128]{1,0:T(8,128)}, f32[1,128]{1,0:T(1,128)}) custom-call(f32[8,1,128]{2,1,0:T(1,128)S(1)} %all_to_all.29.came, f32[2,8,128]{2,1,0:T(8,128)S(1)} %get-tuple-element.23.state), custom_call_target="tpu_custom_call" | custom-call | tf_op jit(solution)/shard_map/results/pallas_call | solution.py:450
Async XLA Ops:
  2.3 14.0 %collective-permute-start = (f32[16,128,128]{2,1,0:T(8,128)S(1)}, f32[16,128,128]{2,1,0:T(8,128)S(1)}, u32[]{:S(2)}, u32[]{:S(2)}) collective-permute-start(f32[16,128,128]{2,1,0:T(8,128)S(1)} %get-tuple-element.16.refs_1_), channel_id=1, source_target_pairs={{0,4},{4,0},{1,5},{5,1},{2,6},{6,2},{3,7},{7,3},{8,12},{12,8},{9,1... | collective-permute-start | bytes 3145736 | tf_op jit(solution)/shard_map/ppermute | solution.py:465

commit v15 on v13

--- a/solution.py
+++ b/solution.py
@@ -398,7 +398,7 @@
             if last:
                 sums = jnp.sum(acc[k * n_col + r], axis=1)
                 term = weight[k * half : k * half + half] * sums
-                out[(my_core ^ k) * n_col + r] = jnp.sum(term, axis=0, keepdims=True)
+                out[r * PAIR + (my_core ^ k)] = jnp.sum(term, axis=0, keepdims=True)
             else:
                 sums = jnp.sum(acc[(my_core ^ k) * n_col + r], axis=1)
                 for chip in range(chips):
@@ -487,7 +487,7 @@
         last = back_no == BACK - 1
         came = all_to_all(sums, everyone)
         sums, state = depend_level(dims, False, last, places, ids, both, bands, came)
-    shown, paths, centrality = results(dims, all_to_all(sums, ("core", "col")), state)
+    shown, paths, centrality = results(dims, all_to_all(sums, ("col", "core")), state)
     return shown, paths, centrality.reshape(LANES)
 
 

time: 59.7 us -> 59.8 us (level)
  no operation moved by 1% of the time
where the time goes in v15:
time: 59.8 us; the launch traced here: 59.4 us
  blocking collectives  49.6 us (83%)
  Pallas kernels  8.68 us (15%)
  between operations  0.66 us (1%)
    all_to_all x5, blocking collectives, all_to_all(): return lax.all_to_all(value, axes, split_axis=0, concat_axis=0, tiled=True)  49.6 us
    pallas_call x2, Pallas kernels, relax_level(): pl.pallas_call(functools.partial(relax_kernel, dims, counted, whole), out...  3.6 us
    pallas_call x2, Pallas kernels, depend_level(): pl.pallas_call(functools.partial(depend_kernel, dims, first, last), out_s...  2.92 us
    pallas_call x1, Pallas kernels, first_level(): pl.pallas_call(functools.partial(first_kernel, dims), out_shape=[piece(n_...  1.56 us
  transfers between devices with their start and end apart: 1, of which 0 were waited for; matrix products, arithmetic and copies ran while one was open for 0% of the time, Pallas kernels for 0%

profile of v15, /device:TPU:0, one launch (start us, length us, event | category | flops | bytes accessed | tf_op | source)
XLA Modules:
  0.0 59.4 jit_solution(13753243547698977913)
XLA Ops:
  0.6 1.6 %first_level.1 = (f32[16,8,128]{2,1,0:T(8,128)S(1)}, f32[16,128,128]{2,1,0:T(8,128)S(1)}, s32[8,128]{1,0:T(8,128)S(1)}) custom-call(s32[2,16]{1,0:T(2,128)} %bitcast.2, s32[8]{0:T(128)} %refs_1_.1, f32[16,128,128]{2,1,0:T(8,128)} %refs_2_.1), custom_call_target="tpu_custom_call" | custom-call | tf_op jit(solution)/shard_map/first_level/pallas_call | solution.py:148
  2.2 0.5 collective-permute-start
  2.7 13.4 %all_to_all.25.refs_3_ = f32[16,8,128]{2,1,0:T(8,128)S(1)} all-to-all(f32[16,8,128]{2,1,0:T(8,128)S(1)} %get-tuple-element.17), channel_id=1, replica_groups=mesh['groups'=2,'chip'=2,'core'=2,'col'=4] {'chip','core','col'}, dimensions={0} | all-to-all | bytes 131072 | tf_op jit(solution)/shard_map/all_to_all | solution.py:461
  16.2 0.0 collective-permute-done.refs_2_
  16.2 1.8 %relax_level.2 = f32[8,1,2,8,128]{4,3,2,1,0:T(8,128)S(1)} custom-call(s32[8,128]{1,0:T(8,128)S(1)} %get-tuple-element.15.refs_0_, f32[16,128,128]{2,1,0:T(8,128)S(1)} %get-tuple-element.16.refs_1_, f32[16,128,128]{2,1,0:T(8,128)S(1)} %collective-permute-done.refs_2_, f32[16,8,128]{2,1,0:T(8,128)S(1)} %all_to_all.25.refs_3_), custom_call_target="tpu_custom_call" | custom-call | tf_op jit(solution)/shard_map/relax_level/pallas_call | solution.py:298
  18.0 9.3 %all_to_all.26.refs_3_ = f32[8,1,2,8,128]{4,3,2,1,0:T(8,128)S(1)} all-to-all(f32[8,1,2,8,128]{4,3,2,1,0:T(8,128)S(1)} %relax_level.2), channel_id=1, replica_groups=mesh['groups'=2,'chip'=2,'core'=2,'col'=4] {'col','chip'}, dimensions={0} | all-to-all | bytes 131072 | tf_op jit(solution)/shard_map/all_to_all | solution.py:461
  27.2 1.8 %relax_level.3 = f32[8,2,2,8,128]{4,3,2,1,0:T(8,128)S(1)} custom-call(s32[8,128]{1,0:T(8,128)S(1)} %get-tuple-element.15.refs_0_, f32[16,128,128]{2,1,0:T(8,128)S(1)} %get-tuple-element.16.refs_1_, f32[16,128,128]{2,1,0:T(8,128)S(1)} %collective-permute-done.refs_2_, f32[8,1,2,8,128]{4,3,2,1,0:T(8,128)S(1)} %all_to_all.26.refs_3_), custom_call_target="tpu_custom_call" | custom-call | tf_op jit(solution)/shard_map/relax_level/pallas_call | solution.py:298
  29.0 9.7 %all_to_all.27.refs_3_ = f32[8,2,2,8,128]{4,3,2,1,0:T(8,128)S(1)} all-to-all(f32[8,2,2,8,128]{4,3,2,1,0:T(8,128)S(1)} %relax_level.3), channel_id=1, replica_groups=mesh['groups'=2,'chip'=2,'core'=2,'col'=4] {'col','chip'}, dimensions={0} | all-to-all | bytes 262144 | tf_op jit(solution)/shard_map/all_to_all | solution.py:461
  38.8 1.9 %depend_level.2 = (f32[16,8,128]{2,1,0:T(8,128)S(1)}, f32[4,2,8,128]{3,2,1,0:T(8,128)S(1)}, f32[2,2,8,128]{3,2,1,0:T(8,128)S(1)}, f32[128,128,128]{2,1,0:T(8,128)S(1)}) custom-call(s32[8,128]{1,0:T(8,128)S(1)} %get-tuple-element.15.refs_0_, f32[16,128,128]{2,1,0:T(8,128)S(1)} %get-tuple-element.16.refs_1_, f32[16,128,128]{2,1,0:T(8,128)S(1)} %collective-permute-done.refs_2_, ...), custom_call_target="tpu_custom_call" | custom-call | tf_op jit(solution)/shard_map/depend_level/pallas_call | solution.py:429
  40.7 9.2 %all_to_all.28.refs_4_ = f32[16,8,128]{2,1,0:T(8,128)S(1)} all-to-all(f32[16,8,128]{2,1,0:T(8,128)S(1)} %get-tuple-element.21), channel_id=1, replica_groups=mesh['groups'=2,'chip'=2,'core'=2,'col'=4] {'chip','core','col'}, dimensions={0} | all-to-all | bytes 131072 | tf_op jit(solution)/shard_map/all_to_all | solution.py:461
  49.9 1.0 %depend_level.3 = (f32[8,1,128]{2,1,0:T(1,128)S(1)}, f32[2,8,128]{2,1,0:T(8,128)S(1)}) custom-call(s32[8,128]{1,0:T(8,128)S(1)} %get-tuple-element.15.refs_0_, f32[4,2,8,128]{3,2,1,0:T(8,128)S(1)} %get-tuple-element.18.refs_1_, f32[2,2,8,128]{3,2,1,0:T(8,128)S(1)} %get-tuple-element.19.refs_2_, f32[128,128,128]{2,1,0:T(8,128)S(1)} %get-tuple-element.20.refs_3_, ...), custom_call_target="tpu_custom_call" | custom-call | tf_op jit(solution)/shard_map/depend_level/pallas_call | solution.py:429
  50.9 7.9 %all_to_all.29.came = f32[8,1,128]{2,1,0:T(1,128)S(1)} all-to-all(f32[8,1,128]{2,1,0:T(1,128)S(1)} %get-tuple-element.22), channel_id=1, replica_groups=mesh['groups'=2,'chip'=2,'core'=2,'col'=4] {'col','core'}, dimensions={0} | all-to-all | bytes 8192 | tf_op jit(solution)/shard_map/all_to_all | solution.py:461
  58.8 0.6 %results.1 = (f32[8,128]{1,0:T(8,128)}, f32[8,128]{1,0:T(8,128)}, f32[1,128]{1,0:T(1,128)}) custom-call(f32[8,1,128]{2,1,0:T(1,128)S(1)} %all_to_all.29.came, f32[2,8,128]{2,1,0:T(8,128)S(1)} %get-tuple-element.23.state), custom_call_target="tpu_custom_call" | custom-call | tf_op jit(solution)/shard_map/results/pallas_call | solution.py:450
Async XLA Ops:
  2.2 14.0 %collective-permute-start = (f32[16,128,128]{2,1,0:T(8,128)S(1)}, f32[16,128,128]{2,1,0:T(8,128)S(1)}, u32[]{:S(2)}, u32[]{:S(2)}) collective-permute-start(f32[16,128,128]{2,1,0:T(8,128)S(1)} %get-tuple-element.16.refs_1_), channel_id=1, source_target_pairs={{0,4},{4,0},{1,5},{5,1},{2,6},{6,2},{3,7},{7,3},{8,12},{12,8},{9,1... | collective-permute-start | bytes 3145736 | tf_op jit(solution)/shard_map/ppermute | solution.py:465
